TPU v7x, 512 devices: a whole 4x8x8 slice. The times are simulated.
512 devices in a mesh: dp: 4 (over x), ctx: 32 (over y_lo, z, core), tp: 4 (over y_hi).
Axes of the slice: x: 4, y: 8 (y_hi: 4, y_lo: 2; y = y_hi * 2 + y_lo), z: 8, core: 2. Of those that a mesh axis runs over, the one named last changes fastest.
Arguments:
- upstream: bfloat16 [16384, 3072], P(('dp', 'ctx'), 'tp'), may hold values from -6 to 6
- router_logits: float32 [16384, 2], P(('dp', 'ctx')), may hold values from -6 to 6
- expert_ids: int32 [16384, 2], P(('dp', 'ctx')), may hold values from 0 to 7, all different within a row; in each aligned block of 128 rows (0 to 127, 128 to 255, ...) at most 36 rows name the same one
- hidden_saved: bfloat16 [4608, 65536], P('dp', ('ctx', 'tp')), may hold values from -0.75 to 0.75
- down_weight: bfloat16 [65536, 3072], P(('ctx', 'tp'), 'dp'), may hold values from -0.0625 to 0.0625
Outputs:
- hidden_grad: bfloat16 [4608, 65536], P('dp', ('ctx', 'tp'))
- down_grad: bfloat16 [65536, 3072], P(('ctx', 'tp'), 'dp')
- logit_grad: float32 [16384, 2], P(('dp', 'ctx'))
Inputs may be any that keep to these rules, and one draw needn't show every extreme that they name: `expert_ids`: the ids of a row differ; in each aligned block of 128 rows (the rows of one device) no expert is named more than 36 times.
All inputs are finite; a program needn't handle non-finite values.
Results may differ from a plain program's by a relative error of at most 0.013.
Values may be sent and summed in bfloat16 or wider, within the bound.
No kernel may reach another device: no remote copies, remote signals or barrier semaphores. Data moves between devices by JAX's collectives and lax.ppermute only.
A program may use at most 128 MiB of HBM per device.

v0:
```python
import jax
import jax.numpy as jnp
from jax import lax
from jax.sharding import PartitionSpec as P

EXPERTS = 8
TOP = 2


def pack_rows(columns, token_place):
    packed = lax.dot_general(
        token_place, columns, (((0,), (0,)), ((), ())), preferred_element_type=jnp.float32
    )
    return packed.astype(jnp.bfloat16)


def local(upstream, router_logits, expert_ids, hidden_saved, down_weight):
    token_count = upstream.shape[0]
    tensor_count = lax.axis_size("tp")
    context_count = lax.axis_size("ctx")
    block_count = context_count * tensor_count
    capacity = hidden_saved.shape[0] // context_count
    gates = 1.0 / (1.0 + jnp.exp(router_logits[:, ::-1] - router_logits))
    gates_sent = gates.astype(jnp.bfloat16)
    routes = expert_ids.reshape(-1)
    onehot = (routes[:, None] == jnp.arange(EXPERTS, dtype=jnp.int32)[None, :]).astype(jnp.int32)
    earlier = jnp.cumsum(onehot, axis=0) - onehot
    slot = jnp.sum(earlier * onehot, axis=1)
    position = routes * capacity + slot
    place = (position[:, None] == jnp.arange(EXPERTS * capacity, dtype=jnp.int32)[None, :]).astype(
        jnp.float32
    )
    token_place = (
        place.reshape(token_count, TOP, EXPERTS * capacity).sum(axis=1).astype(jnp.bfloat16)
    )
    gate_packed = jnp.sum(
        place * gates_sent.reshape(-1).astype(jnp.float32)[:, None], axis=0
    ).astype(jnp.bfloat16)
    group_size = block_count // EXPERTS
    packed = pack_rows(upstream, token_place)
    feature_cols = packed.shape[1]
    outgoing = jnp.broadcast_to(
        packed.reshape(EXPERTS, 1, capacity, feature_cols),
        (EXPERTS, group_size, capacity, feature_cols),
    ).reshape(block_count, capacity, feature_cols)
    gate_out = jnp.broadcast_to(
        gate_packed.reshape(EXPERTS, 1, capacity), (EXPERTS, group_size, capacity)
    ).reshape(block_count, capacity)
    received, gate_in = (
        lax.all_to_all(outgoing, ("ctx", "tp"), split_axis=0, concat_axis=0, tiled=True),
        lax.all_to_all(gate_out, ("ctx", "tp"), split_axis=0, concat_axis=0, tiled=True),
    )
    rows = received.reshape(context_count, tensor_count, capacity, feature_cols)
    rows = rows.transpose(0, 2, 1, 3).reshape(context_count * capacity, tensor_count * feature_cols)
    gate_rows = gate_in.reshape(context_count, tensor_count, capacity)[:, 0, :].reshape(-1)
    proj = lax.dot_general(
        rows,
        lax.all_gather(down_weight, "dp", axis=1, tiled=True),
        (((1,), (1,)), ((), ())),
        preferred_element_type=jnp.float32,
    )
    gate_column = gate_rows.astype(jnp.float32)[:, None]
    hidden_grad = (gate_column * proj).astype(jnp.bfloat16)
    weighted = (gate_column * rows.astype(jnp.float32)).astype(jnp.bfloat16)
    product = lax.dot_general(
        hidden_saved, weighted, (((0,), (0,)), ((), ())), preferred_element_type=jnp.float32
    )
    down_grad = lax.psum_scatter(
        product.astype(jnp.bfloat16), "dp", scatter_dimension=1, tiled=True
    )
    partial_value = jnp.sum(hidden_saved.astype(jnp.float32) * proj, axis=1).reshape(
        context_count, capacity
    )
    group_size = block_count // EXPERTS
    outgoing_parts = jnp.broadcast_to(
        partial_value[:, None, :], (context_count, tensor_count, capacity)
    ).reshape(block_count, capacity)
    returned = lax.all_to_all(
        outgoing_parts, ("ctx", "tp"), split_axis=0, concat_axis=0, tiled=True
    )
    expert_sums = returned.reshape(EXPERTS, group_size, capacity).sum(axis=1)
    route_grad = jnp.take(expert_sums.reshape(-1), position).reshape(token_count, TOP)
    logit_grad = gates * (route_grad - jnp.sum(gates * route_grad, axis=1, keepdims=True))
    return (hidden_grad, down_grad, logit_grad)


def solution(mesh):
    in_specs = (
        P(("dp", "ctx"), "tp"),
        P(("dp", "ctx"), None),
        P(("dp", "ctx"), None),
        P("dp", ("ctx", "tp")),
        P(("ctx", "tp"), "dp"),
    )
    out_specs = (P("dp", ("ctx", "tp")), P(("ctx", "tp"), "dp"), P(("dp", "ctx"), None))
    return jax.shard_map(local, mesh=mesh, in_specs=in_specs, out_specs=out_specs, check_vma=False)
```

profile of v0, /device:TPU:1, one launch (start us, length us, event | category | flops | bytes accessed | tf_op | source)
XLA Modules:
  0.0 374.3 jit_solution(6665161345819443386)
XLA Ops:
  7.2 0.8 copy.55
  8.0 0.1 eq.46
  8.1 0.1 reshape.133
  8.3 0.6 reduce-window.6
  8.9 0.2 slice_reduce_fusion
  9.2 0.8 copy.57
  10.2 0.1 reshape.141
  10.3 0.2 select_reduce_fusion
  10.6 0.7 copy.59
  11.2 18.4 %all-to-all-start = ((bf16[128,1,36]{2,1,0:T(2,128)(2,1)}), bf16[128,1,36]{2,1,0:T(2,128)(2,1)S(1)}, u32[]{:S(2)}, u32[]{:S(2)}) async-start(bf16[128,1,36]{2,1,0:T(2,128)(2,1)} %copy.59), calls=%async_computation | async-start | bytes 131072 | tf_op jit(solution)/shard_map/all_to_all | solution.py:51
  30.0 0.5 copy-done.5
  30.5 0.3 convolution_convert_fusion
  30.8 10.3 %all-to-all-done = bf16[128,1,36]{2,1,0:T(2,128)(2,1)S(1)} async-done(((bf16[128,1,36]{2,1,0:T(2,128)(2,1)}), bf16[128,1,36]{2,1,0:T(2,128)(2,1)S(1)}, u32[]{:S(2)}, u32[]{:S(2)}) %all-to-all-start) | async-done | bytes 9248 | tf_op jit(solution)/shard_map/all_to_all | solution.py:51
  41.1 3.7 broadcast_in_dim.18
  44.7 6.7 %all-to-all-start.1 = ((bf16[128,36,768]{2,1,0:T(8,128)(2,1)}), bf16[128,36,768]{2,1,0:T(8,128)(2,1)}, u32[]{:S(2)}, u32[]{:S(2)}) async-start(bf16[128,36,768]{2,1,0:T(8,128)(2,1)} %bitcast.30), calls=%async_computation.1 | async-start | bytes 15728640 | tf_op jit(solution)/shard_map/all_to_all | solution.py:50
  51.5 0.7 all-gather.2.cloned.1.call-update
  52.2 0.2 reduce-scatter.2.cloned.1.call-start
  52.6 221.7 %all-to-all-done.1 = bf16[128,36,768]{2,1,0:T(8,128)(2,1)} async-done(((bf16[128,36,768]{2,1,0:T(8,128)(2,1)}), bf16[128,36,768]{2,1,0:T(8,128)(2,1)}, u32[]{:S(2)}, u32[]{:S(2)}) %all-to-all-start.1) | async-done | bytes 7077920 | tf_op jit(solution)/shard_map/all_to_all | solution.py:50
  274.3 8.9 %copy.69 = bf16[32,4,36,768]{3,1,2,0:T(4,128)(2,1)} copy(bf16[32,4,36,768]{3,2,1,0:T(8,128)(2,1)} %bitcast.4) | data formatting | bytes 14155776 | tf_op jit(solution)/shard_map/transpose | solution.py:54
  283.2 4.7 %copy.71 = bf16[144,8,4,768]{3,1,2,0:T(8,128)(2,1)S(1)} copy(bf16[144,8,4,768]{3,2,1,0:T(4,128)(2,1)} %bitcast.31) | data formatting | bytes 14155776
  288.0 2.9 copy-done.1
  290.9 6.0 %fusion.3 = bf16[512,3072]{0,1:T(8,128)(2,1)} fusion(bf16[1152,512]{1,0:T(8,128)(2,1)S(1)} %copy-done.2, bf16[1152,3072]{1,0:T(8,128)(2,1)S(1)} %bitcast.32, f32[1152]{0:T(1024)S(1)} %reshape.142), kind=kOutput, calls=%fused_computation.5 | convolution fusion | flops 3636068352 | bytes 11407872 | tf_op jit(solution)/shard_map/dot_general | solution.py:65
  296.9 0.7 copy.64
  297.8 8.2 %multiply_reduce_fusion = (f32[1152]{0:T(1024)S(1)}, bf16[1152,512]{0,1:T(8,128)(2,1)S(1)}) fusion(bf16[1152,512]{0,1:T(8,128)(2,1)S(1)} %copy.64, f32[1152]{0:T(1024)S(1)} %reshape.142, bf16[1152,3072]{1,0:T(8,128)(2,1)} %bitcast.33, bf16[512,3072]{1,0:T(8,128)(2,1)} %all-gather.2.cloned.1.call-done), kind=kOutput, calls=%fused_computation.6 | convolution fusion | flops 3626826752 | bytes 12592128 | tf_op jit(solution)/shard_map/dot_general | solution.py:56
  306.1 0.6 broadcast_in_dim.35
  306.8 37.4 %all-to-all-start.2 = ((f32[128,1,36]{2,1,0:T(1,128)}), f32[128,1,36]{2,1,0:T(1,128)S(1)}, u32[]{:S(2)}, u32[]{:S(2)}) async-start(f32[128,1,36]{2,1,0:T(1,128)} %bitcast.8), calls=%async_computation.3 | async-start | bytes 131072 | tf_op jit(solution)/shard_map/all_to_all | solution.py:78
  344.2 1.4 copy.65
  345.7 10.0 %all-to-all-done.2 = f32[128,1,36]{2,1,0:T(1,128)S(1)} async-done(((f32[128,1,36]{2,1,0:T(1,128)}), f32[128,1,36]{2,1,0:T(1,128)S(1)}, u32[]{:S(2)}, u32[]{:S(2)}) %all-to-all-start.2) | async-done | bytes 18464 | tf_op jit(solution)/shard_map/all_to_all | solution.py:78
  355.7 1.9 gather_fusion
  358.1 0.6 copy.67
  358.7 6.5 %reduce-scatter.2.cloned.1.call-done = bf16[512,768]{0,1:T(8,128)(2,1)} async-done(((bf16[512,3072]{0,1:T(8,128)(2,1)}), bf16[512,768]{0,1:T(8,128)(2,1)}) %reduce-scatter.2.cloned.1.call-update) | async-done | bytes 786448 | tf_op jit(solution)/shard_map/reduce_scatter | solution.py:68
  365.2 2.3 copy.66
  (41 shorter events, 1.6 us)
Async XLA Ops:
  7.2 23.3 %copy-start = (bf16[128,768]{1,0:T(8,128)(2,1)S(1)}, bf16[128,768]{1,0:T(8,128)(2,1)}, u32[]{:S(2)}) copy-start(bf16[128,768]{1,0:T(8,128)(2,1)} %param.5) | copy-start | bytes 589828
  10.1 19.9 %copy-start.3 = (f32[128,2]{1,0:T(8,128)}, f32[128,2]{1,0:T(8,128)S(1)}, u32[]{:S(2)}) copy-start(f32[128,2]{1,0:T(8,128)S(1)} %rev.3) | copy-start | bytes 3076
  11.2 29.8 %all-to-all-start = ((bf16[128,1,36]{2,1,0:T(2,128)(2,1)}), bf16[128,1,36]{2,1,0:T(2,128)(2,1)S(1)}, u32[]{:S(2)}, u32[]{:S(2)}) async-start(bf16[128,1,36]{2,1,0:T(2,128)(2,1)} %copy.59), calls=%async_computation | async-start | bytes 131072 | tf_op jit(solution)/shard_map/all_to_all | solution.py:51
  29.8 0.6 copy-start.5
  44.7 229.6 %all-to-all-start.1 = ((bf16[128,36,768]{2,1,0:T(8,128)(2,1)}), bf16[128,36,768]{2,1,0:T(8,128)(2,1)}, u32[]{:S(2)}, u32[]{:S(2)}) async-start(bf16[128,36,768]{2,1,0:T(8,128)(2,1)} %bitcast.30), calls=%async_computation.1 | async-start | bytes 15728640 | tf_op jit(solution)/shard_map/all_to_all | solution.py:50
  51.5 246.3 %all-gather.2.cloned.1.call-start = ((), (), s32[]{:S(2)}) async-start(), calls=%async_computation.4 | async-start | bytes 3932160 | tf_op jit(solution)/shard_map/all_gather | solution.py:58
  52.2 313.0 %reduce-scatter.2.cloned.1.call-start = ((), (), s32[]{:S(2)}) async-start(), calls=%async_computation.5 | async-start | bytes 3932160 | tf_op jit(solution)/shard_map/reduce_scatter | solution.py:68
  283.2 7.7 %copy-start.2 = (bf16[1152,512]{1,0:T(8,128)(2,1)S(1)}, bf16[1152,512]{1,0:T(8,128)(2,1)}, u32[]{:S(2)}) copy-start(bf16[1152,512]{1,0:T(8,128)(2,1)} %param.8) | copy-start | bytes 3538948
  288.0 2.9 copy-start.1
  306.0 51.8 %copy-start.4 = (f32[128,2]{1,0:T(8,128)S(1)}, f32[128,2]{1,0:T(8,128)}, u32[]{:S(2)}) copy-start(f32[128,2]{1,0:T(8,128)} %copy-done.3) | copy-start | bytes 3076
  306.0 51.8 %copy-start.6 = (s32[128,2]{1,0:T(8,128)S(1)}, s32[128,2]{1,0:T(8,128)}, u32[]{:S(2)}) copy-start(s32[128,2]{1,0:T(8,128)} %copy-done.5) | copy-start | bytes 3076
  306.8 48.9 %all-to-all-start.2 = ((f32[128,1,36]{2,1,0:T(1,128)}), f32[128,1,36]{2,1,0:T(1,128)S(1)}, u32[]{:S(2)}, u32[]{:S(2)}) async-start(f32[128,1,36]{2,1,0:T(1,128)} %bitcast.8), calls=%async_computation.3 | async-start | bytes 131072 | tf_op jit(solution)/shard_map/all_to_all | solution.py:78
Sparse Core Ops, SparseCore 0:
  54.4 45.4 all-gather.1
  297.0 68.1 reduce-scatter.1
where the time goes:
time: 375 us; the launch traced here: 374 us
  waiting for transfers between devices  249 us (66%)
  starting transfers between devices  62.9 us (17%)
  local copies, waits for them, and re-layouts  32.3 us (9%)
  matrix products  14.4 us (4%)
  between operations  14.3 us (4%)
    all_to_all x1, waiting for transfers between devices, local(): lax.all_to_all(outgoing, ('ctx', 'tp'), split_axis=0, concat_axis=0, tile...  222 us
    all_to_all x1, starting transfers between devices, local(): lax.all_to_all(outgoing_parts, ('ctx', 'tp'), split_axis=0, concat_axis=0...  37.4 us
    all_to_all x1, starting transfers between devices, local(): lax.all_to_all(gate_out, ('ctx', 'tp'), split_axis=0, concat_axis=0, tile...  18.4 us
    unnamed x22, local copies, waits for them, and re-layouts  14.8 us
    all_to_all x1, waiting for transfers between devices, local(): lax.all_to_all(gate_out, ('ctx', 'tp'), split_axis=0, concat_axis=0, tile...  10.3 us
    all_to_all x1, waiting for transfers between devices, local(): lax.all_to_all(outgoing_parts, ('ctx', 'tp'), split_axis=0, concat_axis=0...  9.97 us
    transpose x1, local copies, waits for them, and re-layouts, local(): rows.transpose(0, 2, 1, 3)  8.88 us
    dot_general x1, matrix products, local(): lax.dot_general(rows, lax.all_gather(down_weight, 'dp', axis=1, tiled=Tru...  8.19 us
  transfers between devices with their start and end apart: 5, of which 4 were waited for; matrix products, arithmetic and copies ran while one was open for 9% of the time, Pallas kernels for 0%

commit v1 on v0

v1 whole, which is shorter than its diff:
```python
import jax
import jax.numpy as jnp
from jax import lax
from jax.experimental import pallas as pl
from jax.experimental.pallas import tpu as pltpu
from jax.sharding import PartitionSpec as P

EXPERTS = 8
TOP = 2
QUADS = 4
VMEM_LIMIT = 56 * 1024 * 1024


def compare_dot(a, b):
    return lax.dot_general(a, b, (((1,), (1,)), ((), ())), preferred_element_type=jnp.float32)


def pack_kernel(ids_ref, logits_ref, upstream_ref, packed_ref, position_ref, gates_ref):
    tokens = upstream_ref.shape[0]
    rows = packed_ref.shape[0]
    per_quad = rows // (EXPERTS * QUADS)
    slots = per_quad - 1
    capacity = slots * QUADS
    ids = [ids_ref[k : k + 1, :] for k in range(TOP)]
    expert = lax.broadcasted_iota(jnp.int32, (EXPERTS, tokens), 0)
    chosen = [(expert == ids[k]).astype(jnp.float32) for k in range(TOP)]
    before = (
        lax.broadcasted_iota(jnp.int32, (tokens, tokens), 0)
        < lax.broadcasted_iota(jnp.int32, (tokens, tokens), 1)
    ).astype(jnp.bfloat16)
    earlier = jnp.dot(
        (chosen[0] + chosen[1]).astype(jnp.bfloat16), before, preferred_element_type=jnp.float32
    )
    row = lax.broadcasted_iota(jnp.int32, (rows, tokens), 0)
    column = lax.broadcasted_iota(jnp.int32, (128, tokens), 0)
    place = jnp.zeros((rows, tokens), jnp.float32)
    gate_block = jnp.zeros((rows, 128), jnp.float32)
    for k in range(TOP):
        slot = jnp.sum(earlier * chosen[k], axis=0, keepdims=True).astype(jnp.int32)
        gate = 1.0 / (1.0 + jnp.exp(logits_ref[1 - k : 2 - k, :] - logits_ref[k : k + 1, :]))
        quad = sum((slot >= slots * i).astype(jnp.int32) for i in range(1, QUADS))
        within = slot - quad * slots
        base = (ids[k] * QUADS + quad) * per_quad
        place = place + (row == base + within).astype(jnp.float32)
        sent = jnp.where(row == base + slots, gate, 0.0).astype(jnp.bfloat16)
        gate_block = gate_block + compare_dot(sent, (column == within).astype(jnp.bfloat16))
        position_ref[k : k + 1, :] = ids[k] * capacity + slot
        gates_ref[k : k + 1, :] = gate
    packed = jnp.dot(
        place.astype(jnp.bfloat16), upstream_ref[...], preferred_element_type=jnp.float32
    )
    packed_ref[:, :128] = (packed[:, :128] + gate_block).astype(jnp.bfloat16)
    packed_ref[:, 128:] = packed[:, 128:].astype(jnp.bfloat16)


def pack(ids, logits, upstream, slots):
    tokens, cols = upstream.shape
    rows = EXPERTS * QUADS * (slots + 1)
    return pl.pallas_call(
        pack_kernel,
        out_shape=(
            jax.ShapeDtypeStruct((rows, cols), jnp.bfloat16),
            jax.ShapeDtypeStruct((TOP, tokens), jnp.int32),
            jax.ShapeDtypeStruct((TOP, tokens), jnp.float32),
        ),
        compiler_params=pltpu.CompilerParams(vmem_limit_bytes=VMEM_LIMIT),
        cost_estimate=pl.CostEstimate(
            flops=2 * rows * tokens * cols, bytes_accessed=2 * (rows + tokens) * cols, transcendentals=0
        ),
    )(ids, logits, upstream)


def gather_rows(pieces, j, full_ref):
    part = pieces[0].shape[1]
    for i, piece in enumerate(pieces):
        full_ref[i * part : (i + 1) * part, :] = piece[j]


def first_kernel(p0, p1, p2, p3, weight_ref, hidden_t_ref, proj_ref, product_ref, full_ref):
    for j in range(weight_ref.shape[0]):
        gather_rows((p0, p1, p2, p3), j, full_ref)
        part = compare_dot(full_ref[...], weight_ref[j])
        if j == 0:
            proj_ref[...] = part
        else:
            proj_ref[...] += part
        product_ref[j] = jnp.dot(
            hidden_t_ref[...], full_ref[...], preferred_element_type=jnp.float32
        ).astype(jnp.bfloat16)


def last_kernel(
    quad_ref, p0, p1, p2, p3, weight_ref, hidden_t_ref, proj_ref, hidden_ref, gate_ref,
    grad_ref, partial_ref, product_ref, full_ref, total_ref,
):
    blocks = weight_ref.shape[0]
    for j in range(blocks):
        gather_rows((p0, p1, p2, p3), j, full_ref)
        part = compare_dot(full_ref[...], weight_ref[j])
        if j == 0:
            total_ref[...] = proj_ref[...] + part
        else:
            total_ref[...] += part
        product_ref[j] = jnp.dot(
            hidden_t_ref[...], full_ref[...], preferred_element_type=jnp.float32
        ).astype(jnp.bfloat16)
    rows = p0.shape[1]
    quad = quad_ref[0]
    for i in range(QUADS):
        owner = jnp.bitwise_xor(quad, i)
        proj = total_ref[i * rows : (i + 1) * rows, :]
        partial_ref[owner] = jnp.sum(hidden_ref[i].astype(jnp.float32) * proj, axis=1, keepdims=True)
        grad_ref[owner] = (gate_ref[i] * proj).astype(jnp.bfloat16)


def local(upstream, router_logits, expert_ids, hidden_saved, down_weight):
    tokens, cols = upstream.shape
    tensor_count = lax.axis_size("tp")
    context_count = lax.axis_size("ctx")
    data_count = lax.axis_size("dp")
    capacity = hidden_saved.shape[0] // context_count
    slots = capacity // QUADS
    units = hidden_saved.shape[1]
    rows = context_count * slots
    half = cols // 2
    quad = lax.rem(lax.axis_index("ctx"), QUADS)

    packed, position, gates = pack(expert_ids.T, router_logits.T, upstream, slots)
    outgoing = packed.reshape(context_count, (slots + 1) * cols // 128, 128)
    received = lax.all_to_all(outgoing, "ctx", split_axis=0, concat_axis=0, tiled=True)
    received = received.reshape(context_count, slots + 1, cols)
    own_rows = received[:, :slots].reshape(rows, cols)
    own_gate = received[:, slots, :slots].reshape(rows)

    def swap(x, bit):
        return lax.ppermute(x, "ctx", [(c, c ^ bit) for c in range(context_count)])

    def spread(x):
        core = swap(x, 1)
        other = swap(x, 2)
        return x, core, other, swap(other, 1)

    weight = lax.all_gather(down_weight, "dp", axis=0, tiled=False)
    gathered = [
        lax.all_gather(own_rows[:, s : s + half], "tp", axis=0, tiled=False) for s in (0, half)
    ]
    pair_gate = jnp.stack([own_gate, swap(own_gate, 1)])
    gate = jnp.concatenate([pair_gate, swap(pair_gate, 2)])
    gate = gate.astype(jnp.float32)[:, :, None]

    quads = hidden_saved.reshape(context_count, QUADS, slots, units).transpose(1, 0, 2, 3)
    quads = quads.reshape(QUADS, rows, units)
    hidden = jnp.stack(
        [
            lax.dynamic_index_in_dim(quads, jnp.bitwise_xor(quad, i), 0, keepdims=False)
            for i in range(QUADS)
        ]
    )
    hidden_t = (gate * hidden.astype(jnp.float32)).astype(jnp.bfloat16)
    hidden_t = hidden_t.reshape(QUADS * rows, units).T

    total = QUADS * rows
    scratch = pltpu.VMEM((total, half), jnp.bfloat16)
    flops = 4 * total * units * tensor_count * half
    cost = pl.CostEstimate(flops=flops, bytes_accessed=8 << 20, transcendentals=0)
    product_shape = jax.ShapeDtypeStruct((data_count, units, half), jnp.bfloat16)
    pieces = spread(gathered[0])
    proj, product = pl.pallas_call(
        first_kernel,
        out_shape=(jax.ShapeDtypeStruct((total, units), jnp.float32), product_shape),
        scratch_shapes=[scratch],
        compiler_params=pltpu.CompilerParams(vmem_limit_bytes=VMEM_LIMIT),
        cost_estimate=cost,
    )(*pieces, weight[:, :, :half], hidden_t)
    grad_first = lax.psum_scatter(product, "dp", scatter_dimension=0, tiled=False)
    pieces = spread(gathered[1])
    vmem = pl.BlockSpec(memory_space=pltpu.VMEM)
    hidden_grad, partial, product = pl.pallas_call(
        last_kernel,
        out_shape=(
            jax.ShapeDtypeStruct((QUADS, rows, units), jnp.bfloat16),
            jax.ShapeDtypeStruct((QUADS, rows, 1), jnp.float32),
            product_shape,
        ),
        in_specs=[pl.BlockSpec(memory_space=pltpu.SMEM)] + [vmem] * 9,
        scratch_shapes=[scratch, pltpu.VMEM((total, units), jnp.float32)],
        compiler_params=pltpu.CompilerParams(vmem_limit_bytes=VMEM_LIMIT),
        cost_estimate=cost,
    )(quad.astype(jnp.int32).reshape(1), *pieces, weight[:, :, half:], hidden_t, proj, hidden, gate)
    grad_second = lax.psum_scatter(product, "dp", scatter_dimension=0, tiled=False)
    down_grad = jnp.concatenate([grad_first, grad_second], axis=1)

    def canonical(x):
        x = x.reshape(QUADS, context_count, slots, -1).transpose(1, 0, 2, 3)
        return x.reshape(context_count * capacity, -1)

    hidden_grad = canonical(hidden_grad)
    sums = canonical(partial).reshape(context_count, 1, capacity)
    outgoing_sums = jnp.broadcast_to(sums, (context_count, tensor_count, capacity))
    returned = lax.all_to_all(
        outgoing_sums.reshape(context_count * tensor_count, capacity),
        ("ctx", "tp"), split_axis=0, concat_axis=0, tiled=True,
    )
    expert_sums = returned.reshape(EXPERTS, -1, capacity).sum(axis=1)
    route_grad = jnp.take(expert_sums.reshape(-1), position)
    logit_grad = gates * (route_grad - jnp.sum(gates * route_grad, axis=0, keepdims=True))
    return (hidden_grad, down_grad, logit_grad.T)


def solution(mesh):
    in_specs = (
        P(("dp", "ctx"), "tp"),
        P(("dp", "ctx"), None),
        P(("dp", "ctx"), None),
        P("dp", ("ctx", "tp")),
        P(("ctx", "tp"), "dp"),
    )
    out_specs = (P("dp", ("ctx", "tp")), P(("ctx", "tp"), "dp"), P(("dp", "ctx"), None))
    return jax.shard_map(local, mesh=mesh, in_specs=in_specs, out_specs=out_specs, check_vma=False)
```

time: 375 us -> 215 us (0.57)
  waiting for transfers between devices: 249 us -> 57.7 us
  blocking collectives: 0 us -> 35.7 us
  Pallas kernels: 0 us -> 22.2 us
  matrix products: 14.4 us -> 0 us
  local copies, waits for them, and re-layouts: 32.3 us -> 22.1 us
  starting transfers between devices: 62.9 us -> 54.3 us
  other arithmetic: 1.27 us -> 7.79 us
    all_to_all x3 -> x2, waiting for transfers between devices: 242 us -> 19.9 us  [the longest x1 11.3 us: local(): lax.all_to_all(outgoing, 'ctx', split_axis=0, concat_axis=0, tiled=True)]
    all_to_all x3 -> x2, starting transfers between devices: 62.6 us -> 24.7 us  [the longest x1 13 us: local(): lax.all_to_all(outgoing, 'ctx', split_axis=0, concat_axis=0, tiled=True)]
    all_gather x0 -> x2, blocking collectives: none -> 35.7 us  [local(): lax.all_gather(own_rows[:, s:s + half], 'tp', axis=0, tiled=False)]
    ppermute x0 -> x8, starting transfers between devices: none -> 29.4 us  [swap(): return lax.ppermute(x, 'ctx', [(c, c ^ bit) for c in range(context_count)])]
    reduce_scatter x1 -> x2, waiting for transfers between devices: 6.5 us -> 35.2 us  [local(): lax.psum_scatter(product, 'dp', scatter_dimension=0, tiled=False)]
    pallas_call x0 -> x3, Pallas kernels: none -> 22.2 us  [the longest x1 10.6 us: local(): pl.pallas_call(last_kernel, out_shape=(jax.ShapeDtypeStruct((QUADS, rows,...]
    dot_general x3 -> x0, matrix products: 14.4 us -> none  [the longest x1 8.19 us: local(): lax.dot_general(rows, lax.all_gather(down_weight, 'dp', axis=1, tiled=Tru...]
    unnamed x22 -> x17, local copies, waits for them, and re-layouts: 14.8 us -> 1.4 us
  transfers between devices with their start and end apart: 5 -> 13, of which waited for: 4 -> 5; matrix products, arithmetic and copies ran while one was open for 9% -> 12% of each run, Pallas kernels for 0% -> 5%
where the time goes in v1:
time: 215 us; the launch traced here: 214 us
  waiting for transfers between devices  57.7 us (27%)
  starting transfers between devices  54.3 us (25%)
  blocking collectives  35.7 us (17%)
  Pallas kernels  22.2 us (10%)
  local copies, waits for them, and re-layouts  22.1 us (10%)
  between operations  14.2 us (7%)
  other arithmetic  7.79 us (4%)
    all_gather x2, blocking collectives, local(): lax.all_gather(own_rows[:, s:s + half], 'tp', axis=0, tiled=False)  35.7 us
    reduce_scatter x2, waiting for transfers between devices, local(): lax.psum_scatter(product, 'dp', scatter_dimension=0, tiled=False)  35.2 us
    ppermute x8, starting transfers between devices, swap(): return lax.ppermute(x, 'ctx', [(c, c ^ bit) for c in range(context_count)])  29.4 us
    all_to_all x1, starting transfers between devices, local(): lax.all_to_all(outgoing, 'ctx', split_axis=0, concat_axis=0, tiled=True)  13 us
    all_to_all x1, starting transfers between devices, local(): lax.all_to_all(outgoing_sums.reshape(context_count * tensor_count, capaci...  11.7 us
    all_to_all x1, waiting for transfers between devices, local(): lax.all_to_all(outgoing, 'ctx', split_axis=0, concat_axis=0, tiled=True)  11.3 us
    pallas_call x1, Pallas kernels, local(): pl.pallas_call(last_kernel, out_shape=(jax.ShapeDtypeStruct((QUADS, rows,...  10.6 us
    pallas_call x1, Pallas kernels, local(): pl.pallas_call(first_kernel, out_shape=(jax.ShapeDtypeStruct((total, unit...  9.29 us
  transfers between devices with their start and end apart: 13, of which 5 were waited for; matrix products, arithmetic and copies ran while one was open for 12% of the time, Pallas kernels for 5%

profile of v1, /device:TPU:1, one launch (start us, length us, event | category | flops | bytes accessed | tf_op | source)
XLA Modules:
  0.0 213.9 jit_solution(2964347703688839834)
XLA Ops:
  7.9 2.3 %shard_map.76 = (bf16[320,768]{1,0:T(8,128)(2,1)}, s32[2,128]{1,0:T(2,128)}, f32[2,128]{1,0:T(2,128)}) custom-call(s32[2,128]{1,0:T(2,128)} %bitcast.47, f32[2,128]{1,0:T(2,128)} %bitcast.48, bf16[128,768]{1,0:T(8,128)(2,1)} %upstream_ref.1), custom_call_target="tpu_custom_call" | custom-call | flops 62914560 | bytes 688128 | tf_op jit(solution)/shard_map/pallas_call | solution.py:59
  10.2 2.3 %reshape.105 = bf16[32,60,128]{2,1,0:T(8,128)(2,1)} reshape(bf16[320,768]{1,0:T(8,128)(2,1)} %get-tuple-element.11) | data formatting | bytes 983040 | tf_op jit(solution)/shard_map/reshape | solution.py:129
  12.5 13.0 %all-to-all-start = ((bf16[32,60,128]{2,1,0:T(8,128)(2,1)}), bf16[32,60,128]{2,1,0:T(8,128)(2,1)}, u32[]{:S(2)}, u32[]{:S(2)}) async-start(bf16[32,60,128]{2,1,0:T(8,128)(2,1)} %reshape.105), calls=%async_computation | async-start | bytes 1048576 | tf_op jit(solution)/shard_map/all_to_all | solution.py:130
  26.2 1.2 copy.40
  27.4 2.4 %constant_dynamic-slice_fusion = (bf16[1,288,512]{2,0,1:T(2,128)(2,1)S(1)}, bf16[1,288,512]{2,0,1:T(2,128)(2,1)S(1)}, bf16[1,288,512]{2,0,1:T(2,128)(2,1)S(1)}, bf16[1,288,512]{2,0,1:T(2,128)(2,1)S(1)}) fusion(bf16[4,288,512]{2,0,1:T(4,128)(2,1)S(1)} %bitcast.37, s32[]{:T(128)S(6)} %select_n.25, s32[]{:T(128)S(6)} %select_n.24, s32[]{:T(128)S(6)} %select_n.23, ...), kind=kLoop, calls=%fused_computation.18 | loop fusion | bytes 2359312 | tf_op jit(solution)/shard_map/jit(dynamic_index_in_dim)/dynamic_slice | solution.py:155
  30.0 11.3 %all-to-all-done = bf16[32,60,128]{2,1,0:T(8,128)(2,1)} async-done(((bf16[32,60,128]{2,1,0:T(8,128)(2,1)}), bf16[32,60,128]{2,1,0:T(8,128)(2,1)}, u32[]{:S(2)}, u32[]{:S(2)}) %all-to-all-start) | async-done | bytes 491552 | tf_op jit(solution)/shard_map/all_to_all | solution.py:130
  41.3 1.5 reshape.106
  43.0 2.3 %collective-permute-start.3 = (bf16[288]{0:T(512)(128)(2,1)S(1)}, bf16[288]{0:T(512)(128)(2,1)S(1)}, u32[]{:S(2)}, u32[]{:S(2)}) collective-permute-start(bf16[288]{0:T(512)(128)(2,1)S(1)} %reshape_squeeze.3), channel_id=1, source_target_pairs={{0,4},{4,0},{8,12},{12,8},{16,20},{20,16},{24,28},{28,24},{32,36},... | collective-permute-start | bytes 1736 | tf_op jit(solution)/shard_map/ppermute | solution.py:136
  45.6 20.7 %all-gather.2 = bf16[1152,384]{1,0:T(8,128)(2,1)} all-gather(bf16[288,384]{1,0:T(8,128)(2,1)S(1)} %get-tuple-element.25), channel_id=4, replica_groups=mesh['dp'=4,'ctx'=32,'tp'=4] {'tp'}, dimensions={0}, use_global_device_ids=true | all-gather | bytes 1105920 | tf_op jit(solution)/shard_map/all_gather | solution.py:145
  66.3 4.5 %collective-permute-start.6 = (bf16[4,288,384]{2,1,0:T(8,128)(2,1)}, bf16[4,288,384]{2,1,0:T(8,128)(2,1)}, u32[]{:S(2)}, u32[]{:S(2)}) collective-permute-start(bf16[4,288,384]{2,1,0:T(8,128)(2,1)} %bitcast.10.p0), channel_id=1, source_target_pairs={{0,8},{4,12},{8,0},{12,4},{16,24},{20,28},{24,16},{28,20},{32,40},... | collective-permute-start | bytes 2654216 | tf_op jit(solution)/shard_map/ppermute | solution.py:136
  70.8 14.9 %all-gather = bf16[1152,384]{1,0:T(8,128)(2,1)} all-gather(bf16[288,384]{1,0:T(8,128)(2,1)S(1)} %get-tuple-element.26), channel_id=2, replica_groups=mesh['dp'=4,'ctx'=32,'tp'=4] {'tp'}, dimensions={0}, use_global_device_ids=true | all-gather | bytes 1105920 | tf_op jit(solution)/shard_map/all_gather | solution.py:145
  85.8 3.6 %collective-permute-start.1 = (bf16[4,288,384]{2,1,0:T(8,128)(2,1)}, bf16[4,288,384]{2,1,0:T(8,128)(2,1)}, u32[]{:S(2)}, u32[]{:S(2)}) collective-permute-start(bf16[4,288,384]{2,1,0:T(8,128)(2,1)} %bitcast.3.p0), channel_id=1, source_target_pairs={{0,8},{4,12},{8,0},{12,4},{16,24},{20,28},{24,16},{28,20},{32,40},... | collective-permute-start | bytes 2654216 | tf_op jit(solution)/shard_map/ppermute | solution.py:136
  90.3 1.9 collective-permute-start.4
  92.2 1.9 bitcast_convert_fusion
  94.1 2.0 copy.45
  96.2 7.1 %collective-permute-start.5 = (bf16[4,288,384]{2,1,0:T(8,128)(2,1)}, bf16[4,288,384]{2,1,0:T(8,128)(2,1)}, u32[]{:S(2)}, u32[]{:S(2)}) collective-permute-start(bf16[4,288,384]{2,1,0:T(8,128)(2,1)} %bitcast.10.p0), channel_id=1, source_target_pairs={{0,4},{4,0},{8,12},{12,8},{16,20},{20,16},{24,28},{28,24},{32,36},... | collective-permute-start | bytes 2654216 | tf_op jit(solution)/shard_map/ppermute | solution.py:136
  103.3 1.9 collective-permute-start
  105.3 1.2 collective-permute-done.4
  107.0 6.1 %collective-permute-start.7 = (bf16[4,288,384]{2,1,0:T(8,128)(2,1)}, bf16[4,288,384]{2,1,0:T(8,128)(2,1)}, u32[]{:S(2)}, u32[]{:S(2)}) collective-permute-start(bf16[4,288,384]{2,1,0:T(8,128)(2,1)} %collective-permute-done.6.p2), channel_id=1, source_target_pairs={{0,4},{4,0},{8,12},{12,8},{16,20},{20,16},{24,28},{28,24},{32,36},... | collective-permute-start | bytes 2654216 | tf_op jit(solution)/shard_map/ppermute | solution.py:136
  113.1 2.1 collective-permute-start.2
  115.2 1.2 fusion.hidden_t_ref
  117.3 3.9 %fusion.3 = (bf16[4,512,384]{2,1,0:T(8,128)(2,1)}, bf16[4,512,384]{2,1,0:T(8,128)(2,1)}) fusion(bf16[4,512,768]{2,1,0:T(8,128)(2,1)} %bitcast.41), kind=kLoop, calls=%fused_computation.24 | loop fusion | bytes 6291456 | tf_op jit(solution)/shard_map/slice | solution.py:174
  121.1 9.3 %shard_map.77 = (f32[1152,512]{1,0:T(8,128)}, bf16[4,512,384]{2,1,0:T(8,128)(2,1)}) custom-call(bf16[4,288,384]{2,1,0:T(8,128)(2,1)} %bitcast.10.p0, bf16[4,288,384]{2,1,0:T(8,128)(2,1)} %collective-permute-done.5.p1, bf16[4,288,384]{2,1,0:T(8,128)(2,1)} %collective-permute-done.6.p2, bf16[4,288,384]{2,1,0:T(8,128)(2,1)} %collective-permute-done.7.p3, ...), custom_call_target="tpu_custom_call" | custom-call | flops 3623878656 | bytes 8388608 | tf_op jit(solution)/shard_map/pallas_call | solution.py:168
  130.4 0.9 copy-done.6
  131.4 10.6 %shard_map.78 = (bf16[4,288,512]{2,1,0:T(8,128)(2,1)}, f32[4,288,1]{2,1,0:T(8,128)}, bf16[4,512,384]{2,1,0:T(8,128)(2,1)}) custom-call(s32[1]{0:T(128)} %bitcast.quad_ref, bf16[4,288,384]{2,1,0:T(8,128)(2,1)} %bitcast.3.p0, bf16[4,288,384]{2,1,0:T(8,128)(2,1)} %collective-permute-done.p1, bf16[4,288,384]{2,1,0:T(8,128)(2,1)} %collective-permute-done.1.p2, ...), custom_call_target="tpu_custom_call" | custom-call | flops 3623878656 | bytes 8388608 | tf_op jit(solution)/shard_map/pallas_call | solution.py:178
  144.3 11.7 %all-to-all-start.1 = ((f32[128,1,36]{2,1,0:T(1,128)}), f32[128,1,36]{2,1,0:T(1,128)S(1)}, u32[]{:S(2)}, u32[]{:S(2)}) async-start(f32[128,1,36]{2,1,0:T(1,128)} %bitcast.16), calls=%async_computation.3 | async-start | bytes 131072 | tf_op jit(solution)/shard_map/all_to_all | solution.py:200
  157.5 1.4 reshape.111
  158.8 8.6 %all-to-all-done.1 = f32[128,1,36]{2,1,0:T(1,128)S(1)} async-done(((f32[128,1,36]{2,1,0:T(1,128)}), f32[128,1,36]{2,1,0:T(1,128)S(1)}, u32[]{:S(2)}, u32[]{:S(2)}) %all-to-all-start.1) | async-done | bytes 18464 | tf_op jit(solution)/shard_map/all_to_all | solution.py:200
  167.5 1.9 gather_fusion
  170.1 1.4 reduce-scatter.5.cloned.1.call-done
  171.5 33.8 %reduce-scatter.3.cloned.1.call-done = bf16[1,512,384]{2,1,0:T(8,128)(2,1)} async-done(((bf16[4,512,384]{2,1,0:T(8,128)(2,1)}), bf16[1,512,384]{2,1,0:T(8,128)(2,1)}) %reduce-scatter.3.cloned.1.call-update) | async-done | bytes 393232 | tf_op jit(solution)/shard_map/reduce_scatter | solution.py:175
  205.3 2.1 pad_maximum_fusion
  (59 shorter events, 8.7 us)
Async XLA Ops:
  7.2 110.1 %all-gather.5.cloned.1.call-start = ((), (), s32[]{:S(2)}) async-start(), calls=%async_computation.6 | async-start | bytes 3932160 | tf_op jit(solution)/shard_map/all_gather | solution.py:143
  7.9 17.7 %copy-start.1 = (bf16[1152,512]{1,0:T(8,128)(2,1)S(1)}, bf16[1152,512]{1,0:T(8,128)(2,1)}, u32[]{:S(2)}) copy-start(bf16[1152,512]{1,0:T(8,128)(2,1)} %param.8) | copy-start | bytes 3538948
  12.5 28.8 %all-to-all-start = ((bf16[32,60,128]{2,1,0:T(8,128)(2,1)}), bf16[32,60,128]{2,1,0:T(8,128)(2,1)}, u32[]{:S(2)}, u32[]{:S(2)}) async-start(bf16[32,60,128]{2,1,0:T(8,128)(2,1)} %reshape.105), calls=%async_computation | async-start | bytes 1048576 | tf_op jit(solution)/shard_map/all_to_all | solution.py:130
  25.6 146.0 %reduce-scatter.5.cloned.1.call-start = ((), (), s32[]{:S(2)}) async-start(), calls=%async_computation.5 | async-start | bytes 1966080 | tf_op jit(solution)/shard_map/reduce_scatter | solution.py:190
  43.0 46.5 %collective-permute-start.3 = (bf16[288]{0:T(512)(128)(2,1)S(1)}, bf16[288]{0:T(512)(128)(2,1)S(1)}, u32[]{:S(2)}, u32[]{:S(2)}) collective-permute-start(bf16[288]{0:T(512)(128)(2,1)S(1)} %reshape_squeeze.3), channel_id=1, source_target_pairs={{0,4},{4,0},{8,12},{12,8},{16,20},{20,16},{24,28},{28,24},{32,36},... | collective-permute-start | bytes 1736 | tf_op jit(solution)/shard_map/ppermute | solution.py:136
  66.3 40.7 %collective-permute-start.6 = (bf16[4,288,384]{2,1,0:T(8,128)(2,1)}, bf16[4,288,384]{2,1,0:T(8,128)(2,1)}, u32[]{:S(2)}, u32[]{:S(2)}) collective-permute-start(bf16[4,288,384]{2,1,0:T(8,128)(2,1)} %bitcast.10.p0), channel_id=1, source_target_pairs={{0,8},{4,12},{8,0},{12,4},{16,24},{20,28},{24,16},{28,20},{32,40},... | collective-permute-start | bytes 2654216 | tf_op jit(solution)/shard_map/ppermute | solution.py:136
  85.8 27.3 %collective-permute-start.1 = (bf16[4,288,384]{2,1,0:T(8,128)(2,1)}, bf16[4,288,384]{2,1,0:T(8,128)(2,1)}, u32[]{:S(2)}, u32[]{:S(2)}) collective-permute-start(bf16[4,288,384]{2,1,0:T(8,128)(2,1)} %bitcast.3.p0), channel_id=1, source_target_pairs={{0,8},{4,12},{8,0},{12,4},{16,24},{20,28},{24,16},{28,20},{32,40},... | collective-permute-start | bytes 2654216 | tf_op jit(solution)/shard_map/ppermute | solution.py:136
  89.4 4.6 %copy-start = (bf16[4,288,512]{2,1,0:T(8,128)(2,1)}, bf16[4,288,512]{2,1,0:T(8,128)(2,1)S(1)}, u32[]{:S(2)}) copy-start(bf16[4,288,512]{2,1,0:T(8,128)(2,1)S(1)} %copy_dynamic-update-slice_fusion.hidden_ref) | copy-start | bytes 3538948
  90.3 16.3 %collective-permute-start.4 = (bf16[2,288]{1,0:T(2,128)(2,1)}, bf16[2,288]{1,0:T(2,128)(2,1)S(1)}, u32[]{:S(2)}, u32[]{:S(2)}) collective-permute-start(bf16[2,288]{1,0:T(2,128)(2,1)} %pad_maximum_fusion.1), channel_id=1, source_target_pairs={{0,8},{4,12},{8,0},{12,4},{16,24},{20,28},{24,16},{28,20},{32,40},... | collective-permute-start | bytes 3464 | tf_op jit(solution)/shard_map/ppermute | solution.py:136
  96.2 24.9 %collective-permute-start.5 = (bf16[4,288,384]{2,1,0:T(8,128)(2,1)}, bf16[4,288,384]{2,1,0:T(8,128)(2,1)}, u32[]{:S(2)}, u32[]{:S(2)}) collective-permute-start(bf16[4,288,384]{2,1,0:T(8,128)(2,1)} %bitcast.10.p0), channel_id=1, source_target_pairs={{0,4},{4,0},{8,12},{12,8},{16,20},{20,16},{24,28},{28,24},{32,36},... | collective-permute-start | bytes 2654216 | tf_op jit(solution)/shard_map/ppermute | solution.py:136
  103.3 27.1 %collective-permute-start = (bf16[4,288,384]{2,1,0:T(8,128)(2,1)}, bf16[4,288,384]{2,1,0:T(8,128)(2,1)}, u32[]{:S(2)}, u32[]{:S(2)}) collective-permute-start(bf16[4,288,384]{2,1,0:T(8,128)(2,1)} %bitcast.3.p0), channel_id=1, source_target_pairs={{0,4},{4,0},{8,12},{12,8},{16,20},{20,16},{24,28},{28,24},{32,36},... | collective-permute-start | bytes 2654216 | tf_op jit(solution)/shard_map/ppermute | solution.py:136
  107.0 14.1 %collective-permute-start.7 = (bf16[4,288,384]{2,1,0:T(8,128)(2,1)}, bf16[4,288,384]{2,1,0:T(8,128)(2,1)}, u32[]{:S(2)}, u32[]{:S(2)}) collective-permute-start(bf16[4,288,384]{2,1,0:T(8,128)(2,1)} %collective-permute-done.6.p2), channel_id=1, source_target_pairs={{0,4},{4,0},{8,12},{12,8},{16,20},{20,16},{24,28},{28,24},{32,36},... | collective-permute-start | bytes 2654216 | tf_op jit(solution)/shard_map/ppermute | solution.py:136
  113.1 17.3 %collective-permute-start.2 = (bf16[4,288,384]{2,1,0:T(8,128)(2,1)}, bf16[4,288,384]{2,1,0:T(8,128)(2,1)S(1)}, u32[]{:S(2)}, u32[]{:S(2)}) collective-permute-start(bf16[4,288,384]{2,1,0:T(8,128)(2,1)} %collective-permute-done.1.p2), channel_id=1, source_target_pairs={{0,4},{4,0},{8,12},{12,8},{16,20},{20,16},{24,28},{28,24},{32,36},... | collective-permute-start | bytes 2654216 | tf_op jit(solution)/shard_map/ppermute | solution.py:136
  130.4 1.0 copy-start.6
  142.0 0.8 copy-start.4
  142.0 1.1 copy-start.3
  142.0 63.3 %reduce-scatter.3.cloned.1.call-start = ((), (), s32[]{:S(2)}) async-start(), calls=%async_computation.4 | async-start | bytes 1966080 | tf_op jit(solution)/shard_map/reduce_scatter | solution.py:175
  142.1 14.0 %copy-start.2 = (bf16[4,288,512]{2,1,0:T(8,128)(2,1)S(1)}, bf16[4,288,512]{2,1,0:T(8,128)(2,1)}, u32[]{:S(2)}) copy-start(bf16[4,288,512]{2,1,0:T(8,128)(2,1)} %get-tuple-element.13) | copy-start | bytes 3538948
  144.3 23.1 %all-to-all-start.1 = ((f32[128,1,36]{2,1,0:T(1,128)}), f32[128,1,36]{2,1,0:T(1,128)S(1)}, u32[]{:S(2)}, u32[]{:S(2)}) async-start(f32[128,1,36]{2,1,0:T(1,128)} %bitcast.16), calls=%async_computation.3 | async-start | bytes 131072 | tf_op jit(solution)/shard_map/all_to_all | solution.py:200
  157.5 12.0 %copy-start.5 = (f32[2,128]{1,0:T(2,128)S(1)}, f32[2,128]{1,0:T(2,128)}, u32[]{:S(2)}) copy-start(f32[2,128]{1,0:T(2,128)} %get-tuple-element.16) | copy-start | bytes 3076
Sparse Core Ops, SparseCore 0:
  10.1 50.3 all-gather.4
  142.1 29.3 reduce-scatter.4
  174.4 30.8 reduce-scatter.2

commit v2 on v1

v2 whole, which is shorter than its diff:
```python
import functools

import jax
import jax.numpy as jnp
from jax import lax
from jax.experimental import pallas as pl
from jax.experimental.pallas import tpu as pltpu
from jax.sharding import PartitionSpec as P

EXPERTS = 8
TOP = 2
QUADS = 4
VMEM_LIMIT = 56 * 1024 * 1024
CHUNKS = ((0, 384), (384, 384))


def compare_dot(a, b):
    return lax.dot_general(a, b, (((1,), (1,)), ((), ())), preferred_element_type=jnp.float32)


def slab_rows(capacity):
    return (capacity // 8 + 1) * 8


def pack_kernel(capacity, ids_ref, logits_ref, upstream_ref, packed_ref, position_ref, gates_ref):
    tokens = upstream_ref.shape[0]
    rows = packed_ref.shape[0]
    per_expert = rows // EXPERTS
    ids = [ids_ref[k : k + 1, :] for k in range(TOP)]
    expert = lax.broadcasted_iota(jnp.int32, (EXPERTS, tokens), 0)
    chosen = [(expert == ids[k]).astype(jnp.float32) for k in range(TOP)]
    before = (
        lax.broadcasted_iota(jnp.int32, (tokens, tokens), 0)
        < lax.broadcasted_iota(jnp.int32, (tokens, tokens), 1)
    ).astype(jnp.bfloat16)
    earlier = jnp.dot(
        (chosen[0] + chosen[1]).astype(jnp.bfloat16), before, preferred_element_type=jnp.float32
    )
    row = lax.broadcasted_iota(jnp.int32, (rows, tokens), 0)
    column = lax.broadcasted_iota(jnp.int32, (128, tokens), 0)
    place = jnp.zeros((rows, tokens), jnp.float32)
    gate_block = jnp.zeros((rows, 128), jnp.float32)
    for k in range(TOP):
        slot = jnp.sum(earlier * chosen[k], axis=0, keepdims=True).astype(jnp.int32)
        gate = 1.0 / (1.0 + jnp.exp(logits_ref[1 - k : 2 - k, :] - logits_ref[k : k + 1, :]))
        base = ids[k] * per_expert
        place = place + (row == base + slot).astype(jnp.float32)
        sent = jnp.where(row == base + capacity, gate, 0.0).astype(jnp.bfloat16)
        gate_block = gate_block + compare_dot(sent, (column == slot).astype(jnp.bfloat16))
        position_ref[k : k + 1, :] = ids[k] * capacity + slot
        gates_ref[k : k + 1, :] = gate
    packed = jnp.dot(
        place.astype(jnp.bfloat16), upstream_ref[...], preferred_element_type=jnp.float32
    )
    packed_ref[:, :128] = (packed[:, :128] + gate_block).astype(jnp.bfloat16)
    packed_ref[:, 128:] = packed[:, 128:].astype(jnp.bfloat16)


def pack(ids, logits, upstream, capacity):
    tokens, cols = upstream.shape
    rows = EXPERTS * slab_rows(capacity)
    return pl.pallas_call(
        functools.partial(pack_kernel, capacity),
        out_shape=(
            jax.ShapeDtypeStruct((rows, cols), jnp.bfloat16),
            jax.ShapeDtypeStruct((TOP, tokens), jnp.int32),
            jax.ShapeDtypeStruct((TOP, tokens), jnp.float32),
        ),
        compiler_params=pltpu.CompilerParams(vmem_limit_bytes=VMEM_LIMIT),
        cost_estimate=pl.CostEstimate(
            flops=2 * rows * tokens * cols, bytes_accessed=2 * (rows + tokens) * cols, transcendentals=0
        ),
    )(ids, logits, upstream)


def chunk_kernel(start, first, last, quad_ref, *refs):
    refs = list(refs)
    pieces = [refs.pop(0) for _ in range(QUADS)]
    weight_ref, hidden_t_ref = refs.pop(0), refs.pop(0)
    before_ref = None if first else refs.pop(0)
    hidden_ref, gate_ref = (refs.pop(0), refs.pop(0)) if last else (None, None)
    grad_ref, partial_ref = (refs.pop(0), refs.pop(0)) if last else (None, None)
    proj_ref = None if last else refs.pop(0)
    product_ref = refs.pop(0)
    full, side, hidden_t, total, product, sems = refs[:6]
    hidden = refs[6] if last else None
    blocks, _, width = product.shape
    rows = total.shape[0] // QUADS
    copies = []

    def copy(source, target):
        made = pltpu.make_async_copy(source, target, sems.at[len(copies)])
        copies.append(made)
        made.start()
        return made

    def columns(j):
        return slice(j * width, (j + 1) * width)

    sides = [
        copy(weight_ref.at[j, :, start : start + width], side.at[:, columns(j)])
        for j in range(blocks)
    ]
    loads = []
    for i in range(QUADS):
        at = slice(i * rows, (i + 1) * rows)
        loads.append([copy(pieces[i].at[j], full.at[at, columns(j)]) for j in range(blocks)])
        if not first:
            loads[i].append(copy(before_ref.at[at, :], total.at[at, :]))
        if last:
            loads[i].append(copy(hidden_ref.at[i], hidden.at[i]))
    hidden_t_load = copy(hidden_t_ref, hidden_t)
    stores = []
    for made in sides:
        made.wait()
    for i in range(QUADS):
        for made in loads[i]:
            made.wait()
        at = slice(i * rows, (i + 1) * rows)
        proj = compare_dot(full[at, :], side[...])
        if not first:
            proj = total[at, :] + proj
        if last:
            owner = jnp.bitwise_xor(quad_ref[0], i)
            partial_ref[owner] = jnp.sum(
                hidden[i].astype(jnp.float32) * proj, axis=1, keepdims=True
            )
            grad_ref[owner] = (gate_ref[i] * proj).astype(jnp.bfloat16)
        else:
            total[at, :] = proj
            stores.append(copy(total.at[at, :], proj_ref.at[at, :]))
    hidden_t_load.wait()
    for j in range(blocks):
        result = jnp.dot(hidden_t[...], full[:, columns(j)], preferred_element_type=jnp.float32)
        product[j] = result.astype(jnp.bfloat16)
        stores.append(copy(product.at[j], product_ref.at[j]))
    for made in stores:
        made.wait()


def after(x, *others):
    return lax.optimization_barrier((x,) + others)[0]


def local(upstream, router_logits, expert_ids, hidden_saved, down_weight):
    tokens, cols = upstream.shape
    tensor_count = lax.axis_size("tp")
    context_count = lax.axis_size("ctx")
    data_count = lax.axis_size("dp")
    capacity = hidden_saved.shape[0] // context_count
    units = hidden_saved.shape[1]
    rows = EXPERTS * capacity
    total = QUADS * rows
    quad = lax.rem(lax.axis_index("ctx"), QUADS)

    packed, position, gates = pack(expert_ids.T, router_logits.T, upstream, capacity)
    outgoing = packed.reshape(EXPERTS, slab_rows(capacity), cols)
    groups = [[q + QUADS * e for e in range(EXPERTS)] for q in range(QUADS)]
    received = lax.all_to_all(
        outgoing, "ctx", split_axis=0, concat_axis=0, tiled=True, axis_index_groups=groups
    )
    own_rows = received[:, :capacity].reshape(rows, cols)
    own_gate = received[:, capacity, :capacity].reshape(rows)

    def swap(x, bit):
        return lax.ppermute(x, "ctx", [(c, c ^ bit) for c in range(context_count)])

    weight = lax.all_gather(down_weight, "dp", axis=0, tiled=False)
    gathered = [
        lax.all_gather(own_rows[:, s : s + w], "tp", axis=0, tiled=False) for s, w in CHUNKS
    ]
    pair_gate = jnp.stack([own_gate, swap(own_gate, 1)])
    gate = jnp.concatenate([pair_gate, swap(pair_gate, 2)])
    gate = gate.astype(jnp.float32)[:, :, None]
    quads = hidden_saved.reshape(EXPERTS, QUADS, capacity, units).transpose(1, 0, 2, 3)
    quads = quads.reshape(QUADS, rows, units)
    hidden = jnp.stack(
        [
            lax.dynamic_index_in_dim(quads, jnp.bitwise_xor(quad, i), 0, keepdims=False)
            for i in range(QUADS)
        ]
    )
    hidden_t = (gate * hidden.astype(jnp.float32)).astype(jnp.bfloat16)
    hidden_t = hidden_t.reshape(total, units).T

    def run(start, width, pieces, before=None, last=False):
        first = before is None
        product_shape = jax.ShapeDtypeStruct((data_count, units, width), jnp.bfloat16)
        held = pl.BlockSpec(memory_space=pl.ANY)
        vmem = pl.BlockSpec(memory_space=pltpu.VMEM)
        inputs = list(pieces) + [weight, hidden_t] + ([] if first else [before])
        specs = [pl.BlockSpec(memory_space=pltpu.SMEM)] + [held] * len(inputs)
        if last:
            inputs += [hidden, gate]
            specs += [held, vmem]
            outputs = (
                jax.ShapeDtypeStruct((QUADS, rows, units), jnp.bfloat16),
                jax.ShapeDtypeStruct((QUADS, rows, 1), jnp.float32),
                product_shape,
            )
            out_specs = (vmem, vmem, held)
        else:
            outputs = (jax.ShapeDtypeStruct((total, units), jnp.float32), product_shape)
            out_specs = (held, held)
        scratch = [
            pltpu.VMEM((total, data_count * width), jnp.bfloat16),
            pltpu.VMEM((units, data_count * width), jnp.bfloat16),
            pltpu.VMEM((units, total), jnp.bfloat16),
            pltpu.VMEM((total, units), jnp.float32),
            pltpu.VMEM((data_count, units, width), jnp.bfloat16),
            pltpu.SemaphoreType.DMA((1 + data_count * (QUADS + 2) + 3 * QUADS,)),
        ] + ([pltpu.VMEM((QUADS, rows, units), jnp.bfloat16)] if last else [])
        return pl.pallas_call(
            functools.partial(chunk_kernel, start, first, last),
            out_shape=outputs,
            in_specs=specs,
            out_specs=out_specs,
            scratch_shapes=scratch,
            compiler_params=pltpu.CompilerParams(vmem_limit_bytes=VMEM_LIMIT),
            cost_estimate=pl.CostEstimate(
                flops=18 * 10**9 if last else 1 << 20, bytes_accessed=1 << 20, transcendentals=0
            ),
        )(quad.astype(jnp.int32).reshape(1), *inputs)

    proj, grads = None, []
    for n, (start, width) in enumerate(CHUNKS):
        held, other = gathered[n], swap(gathered[n], 2)
        ahead = (hidden_t,) + tuple(gathered[1:]) if n == 0 else (proj,)
        pieces = (held, swap(held, 1), other, swap(after(other, *ahead), 1))
        if n < len(CHUNKS) - 1:
            proj, product = run(start, width, pieces, proj)
        else:
            hidden_grad, partial, product = run(start, width, pieces, proj, True)
        grads.append(lax.psum_scatter(product, "dp", scatter_dimension=0, tiled=False))
    down_grad = jnp.concatenate(grads, axis=1)

    def canonical(x):
        x = x.reshape(QUADS, EXPERTS, capacity, -1).transpose(1, 0, 2, 3)
        return x.reshape(context_count * capacity, -1)

    hidden_grad = canonical(hidden_grad)
    sums = canonical(partial).reshape(context_count, 1, capacity)
    outgoing_sums = jnp.broadcast_to(sums, (context_count, tensor_count, capacity))
    returned = lax.all_to_all(
        outgoing_sums.reshape(context_count * tensor_count, capacity),
        ("ctx", "tp"), split_axis=0, concat_axis=0, tiled=True,
    )
    expert_sums = returned.reshape(EXPERTS, -1, capacity).sum(axis=1)
    route_grad = jnp.take(expert_sums.reshape(-1), position)
    logit_grad = gates * (route_grad - jnp.sum(gates * route_grad, axis=0, keepdims=True))
    return (hidden_grad, down_grad, logit_grad.T)


def solution(mesh):
    in_specs = (
        P(("dp", "ctx"), "tp"),
        P(("dp", "ctx"), None),
        P(("dp", "ctx"), None),
        P("dp", ("ctx", "tp")),
        P(("ctx", "tp"), "dp"),
    )
    out_specs = (P("dp", ("ctx", "tp")), P(("ctx", "tp"), "dp"), P(("dp", "ctx"), None))
    return jax.shard_map(local, mesh=mesh, in_specs=in_specs, out_specs=out_specs, check_vma=False)
```

time: 215 us -> 178 us (0.83)
  waiting for transfers between devices: 57.7 us -> 30 us
  local copies, waits for them, and re-layouts: 22.1 us -> 16.2 us
    reduce_scatter x2, waiting for transfers between devices: 35.2 us -> 7.62 us  [local(): lax.psum_scatter(product, 'dp', scatter_dimension=0, tiled=False)]
    ppermute x8, waiting for transfers between devices: 1.21 us -> 11.1 us  [swap(): return lax.ppermute(x, 'ctx', [(c, c ^ bit) for c in range(context_count)])]
    all_to_all x1, waiting for transfers between devices: 11.3 us -> 1.51 us  [local(): lax.all_to_all(outgoing, 'ctx', split_axis=0, concat_axis=0, tiled=True,...]
    all_to_all x1, starting transfers between devices: 11.7 us -> 5.99 us  [local(): lax.all_to_all(outgoing_sums.reshape(context_count * tensor_count, capaci...]
    ppermute x8, starting transfers between devices: 29.4 us -> 34.3 us  [swap(): return lax.ppermute(x, 'ctx', [(c, c ^ bit) for c in range(context_count)])]
    reshape x5 -> x3, local copies, waits for them, and re-layouts: 4.62 us -> 0.44 us  [the longest x1 0.27 us: local(): hidden_saved.reshape(EXPERTS, QUADS, capacity, units).transpose(1, 0, 2, 3)]
    slice x3 -> x2, local copies, waits for them, and re-layouts: 3.97 us -> 0.76 us  [the longest x1 0.73 us: local(): own_rows[:, s:s + w]]
    unnamed x17 -> x27, local copies, waits for them, and re-layouts: 1.4 us -> 4.1 us
  transfers between devices with their start and end apart: 13 -> 13, of which waited for: 5 -> 6; matrix products, arithmetic and copies ran while one was open for 12% -> 10% of each run, Pallas kernels for 5% -> 12%
where the time goes in v2:
time: 178 us
  starting transfers between devices  52.2 us (29%)
  blocking collectives  36.7 us (21%)
  waiting for transfers between devices  30 us (17%)
  Pallas kernels  21.3 us (12%)
  local copies, waits for them, and re-layouts  16.2 us (9%)
  between operations  14.1 us (8%)
  other arithmetic  7.09 us (4%)
    all_gather x2, blocking collectives, local(): lax.all_gather(own_rows[:, s:s + w], 'tp', axis=0, tiled=False)  36.7 us
    ppermute x8, starting transfers between devices, swap(): return lax.ppermute(x, 'ctx', [(c, c ^ bit) for c in range(context_count)])  34.3 us
    pallas_call x2, Pallas kernels, run(): pl.pallas_call(functools.partial(chunk_kernel, start, first, last), out_s...  19.1 us
    all_to_all x1, starting transfers between devices, local(): lax.all_to_all(outgoing, 'ctx', split_axis=0, concat_axis=0, tiled=True,...  11.9 us
    ppermute x8, waiting for transfers between devices, swap(): return lax.ppermute(x, 'ctx', [(c, c ^ bit) for c in range(context_count)])  11.1 us
    all_to_all x1, waiting for transfers between devices, local(): lax.all_to_all(outgoing_sums.reshape(context_count * tensor_count, capaci...  9.05 us
    reduce_scatter x2, waiting for transfers between devices, local(): lax.psum_scatter(product, 'dp', scatter_dimension=0, tiled=False)  7.62 us
    all_to_all x1, starting transfers between devices, local(): lax.all_to_all(outgoing_sums.reshape(context_count * tensor_count, capaci...  5.99 us
  transfers between devices with their start and end apart: 13, of which 6 were waited for; matrix products, arithmetic and copies ran while one was open for 10% of the time, Pallas kernels for 12%

profile of v2, /device:TPU:1, one launch (start us, length us, event | category | flops | bytes accessed | tf_op | source)
XLA Modules:
  0.0 177.7 jit_solution(9057884354738365727)
XLA Ops:
  7.9 2.2 %shard_map.76 = (bf16[320,768]{1,0:T(8,128)(2,1)}, s32[2,128]{1,0:T(2,128)}, f32[2,128]{1,0:T(2,128)}) custom-call(s32[2,128]{1,0:T(2,128)} %bitcast.53, f32[2,128]{1,0:T(2,128)} %bitcast.54, bf16[128,768]{1,0:T(8,128)(2,1)} %upstream_ref.1), custom_call_target="tpu_custom_call" | custom-call | flops 62914560 | bytes 688128 | tf_op jit(solution)/shard_map/pallas_call | solution.py:62
  10.1 11.9 %all-to-all-start = ((bf16[8,40,768]{2,1,0:T(8,128)(2,1)}), bf16[8,40,768]{2,1,0:T(8,128)(2,1)S(1)}, u32[]{:S(2)}, u32[]{:S(2)}) async-start(bf16[8,40,768]{2,1,0:T(8,128)(2,1)} %bitcast.46), calls=%async_computation | async-start | bytes 983040 | tf_op jit(solution)/shard_map/all_to_all | solution.py:159
  23.0 2.4 %constant_dynamic-slice_fusion = (bf16[1,288,512]{2,0,1:T(2,128)(2,1)S(1)}, bf16[1,288,512]{2,0,1:T(2,128)(2,1)S(1)}, bf16[1,288,512]{2,0,1:T(2,128)(2,1)S(1)}, bf16[1,288,512]{2,0,1:T(2,128)(2,1)S(1)}) fusion(bf16[4,288,512]{2,0,1:T(4,128)(2,1)S(1)} %bitcast.37, s32[]{:T(128)S(6)} %select_n.25, s32[]{:T(128)S(6)} %select_n.24, s32[]{:T(128)S(6)} %select_n.23, ...), kind=kLoop, calls=%fused_computation.18 | loop fusion | bytes 2359312 | tf_op jit(solution)/shard_map/jit(dynamic_index_in_dim)/dynamic_slice | solution.py:179
  25.6 1.0 copy-done.1
  26.7 1.9 %bitcast_convert_fusion = f32[1152,512]{1,0:T(8,128)} fusion(bf16[4,288,512]{2,1,0:T(8,128)(2,1)S(1)} %copy_dynamic-update-slice_fusion.refs_7_), kind=kLoop, calls=%fused_computation.3 | loop fusion | flops 589824 | bytes 3538944 | tf_op jit(solution)/shard_map/convert_element_type | solution.py:183
  28.5 2.1 %copy.58 = f32[1152,512]{0,1:T(8,128)S(1)} copy(f32[1152,512]{1,0:T(8,128)} %bitcast_convert_fusion) | data formatting | bytes 4718592 | tf_op jit(solution)/shard_map/convert_element_type | solution.py:183
  30.7 1.5 all-to-all-done
  32.3 8.8 %collective-permute-start.4 = (bf16[288]{0:T(512)(128)(2,1)S(1)}, bf16[288]{0:T(512)(128)(2,1)S(1)}, u32[]{:S(2)}, u32[]{:S(2)}) collective-permute-start(bf16[288]{0:T(512)(128)(2,1)S(1)} %reshape_squeeze.3), channel_id=1, source_target_pairs={{0,4},{4,0},{8,12},{12,8},{16,20},{20,16},{24,28},{28,24},{32,36},... | collective-permute-start | bytes 1736 | tf_op jit(solution)/shard_map/ppermute | solution.py:166
  41.9 19.4 %all-gather.1 = bf16[1152,384]{1,0:T(8,128)(2,1)S(1)} all-gather(bf16[288,384]{1,0:T(8,128)(2,1)S(1)} %get-tuple-element.27), channel_id=3, replica_groups=mesh['dp'=4,'ctx'=32,'tp'=4] {'tp'}, dimensions={0}, use_global_device_ids=true | all-gather | bytes 1105920 | tf_op jit(solution)/shard_map/all_gather | solution.py:170
  61.4 3.0 %collective-permute-start.3 = (bf16[4,288,384]{2,1,0:T(8,128)(2,1)S(1)}, bf16[4,288,384]{2,1,0:T(8,128)(2,1)}, u32[]{:S(2)}, u32[]{:S(2)}) collective-permute-start(bf16[4,288,384]{2,1,0:T(8,128)(2,1)S(1)} %bitcast.40), channel_id=1, source_target_pairs={{0,8},{4,12},{8,0},{12,4},{16,24},{20,28},{24,16},{28,20},{32,40},... | collective-permute-start | bytes 2654216 | tf_op jit(solution)/shard_map/ppermute | solution.py:166
  64.4 4.1 %collective-permute-start.2 = (bf16[4,288,384]{2,1,0:T(8,128)(2,1)S(1)}, bf16[4,288,384]{2,1,0:T(8,128)(2,1)}, u32[]{:S(2)}, u32[]{:S(2)}) collective-permute-start(bf16[4,288,384]{2,1,0:T(8,128)(2,1)S(1)} %bitcast.41), channel_id=1, source_target_pairs={{0,4},{4,0},{8,12},{12,8},{16,20},{20,16},{24,28},{28,24},{32,36},... | collective-permute-start | bytes 2654216 | tf_op jit(solution)/shard_map/ppermute | solution.py:166
  68.6 3.4 %collective-permute-start.5 = (bf16[2,288]{1,0:T(2,128)(2,1)S(1)}, bf16[2,288]{1,0:T(2,128)(2,1)S(1)}, u32[]{:S(2)}, u32[]{:S(2)}) collective-permute-start(bf16[2,288]{1,0:T(2,128)(2,1)S(1)} %pad_maximum_fusion.1), channel_id=1, source_target_pairs={{0,8},{4,12},{8,0},{12,4},{16,24},{20,28},{24,16},{28,20},{32,40},... | collective-permute-start | bytes 3464 | tf_op jit(solution)/shard_map/ppermute | solution.py:166
  71.9 17.3 %all-gather = bf16[1152,384]{1,0:T(8,128)(2,1)} all-gather(bf16[288,384]{1,0:T(8,128)(2,1)S(1)} %copy-done.4), channel_id=2, replica_groups=mesh['dp'=4,'ctx'=32,'tp'=4] {'tp'}, dimensions={0}, use_global_device_ids=true | all-gather | bytes 1105920 | tf_op jit(solution)/shard_map/all_gather | solution.py:170
  89.9 1.2 fusion.refs_5_
  91.1 8.1 %collective-permute-start.6 = (bf16[4,288,384]{2,1,0:T(8,128)(2,1)}, bf16[4,288,384]{2,1,0:T(8,128)(2,1)S(1)}, u32[]{:S(2)}, u32[]{:S(2)}) collective-permute-start(bf16[4,288,384]{2,1,0:T(8,128)(2,1)} %collective-permute-done.3.refs_2_), channel_id=1, source_target_pairs={{0,4},{4,0},{8,12},{12,8},{16,20},{20,16},{24,28},{28,24},{32,36},... | collective-permute-start | bytes 2654216 | tf_op jit(solution)/shard_map/ppermute | solution.py:166
  99.2 1.9 %collective-permute-start.1 = (bf16[4,288,384]{2,1,0:T(8,128)(2,1)}, bf16[4,288,384]{2,1,0:T(8,128)(2,1)S(1)}, u32[]{:S(2)}, u32[]{:S(2)}) collective-permute-start(bf16[4,288,384]{2,1,0:T(8,128)(2,1)} %bitcast.4.refs_0_), channel_id=1, source_target_pairs={{0,8},{4,12},{8,0},{12,4},{16,24},{20,28},{24,16},{28,20},{32,40},... | collective-permute-start | bytes 2654216 | tf_op jit(solution)/shard_map/ppermute | solution.py:166
  101.4 1.0 copy-done.5
  102.4 8.1 %shard_map.77 = (f32[1152,512]{1,0:T(8,128)}, bf16[4,512,384]{2,1,0:T(8,128)(2,1)}) custom-call(s32[1]{0:T(128)} %bitcast.quad_ref, bf16[4,288,384]{2,1,0:T(8,128)(2,1)} %bitcast.42, bf16[4,288,384]{2,1,0:T(8,128)(2,1)} %collective-permute-done.2.refs_1_, bf16[4,288,384]{2,1,0:T(8,128)(2,1)} %collective-permute-done.3.refs_2_, ...), custom_call_target="tpu_custom_call" | custom-call | flops 1048576 | bytes 1048576 | tf_op jit(solution)/shard_map/pallas_call | solution.py:213
  110.5 2.3 %collective-permute-start = (bf16[4,288,384]{2,1,0:T(8,128)(2,1)}, bf16[4,288,384]{2,1,0:T(8,128)(2,1)S(1)}, u32[]{:S(2)}, u32[]{:S(2)}) collective-permute-start(bf16[4,288,384]{2,1,0:T(8,128)(2,1)} %bitcast.4.refs_0_), channel_id=1, source_target_pairs={{0,4},{4,0},{8,12},{12,8},{16,20},{20,16},{24,28},{28,24},{32,36},... | collective-permute-start | bytes 2654216 | tf_op jit(solution)/shard_map/ppermute | solution.py:166
  112.8 9.8 %collective-permute-done.1.refs_2_ = bf16[4,288,384]{2,1,0:T(8,128)(2,1)S(1)} collective-permute-done((bf16[4,288,384]{2,1,0:T(8,128)(2,1)}, bf16[4,288,384]{2,1,0:T(8,128)(2,1)S(1)}, u32[]{:S(2)}, u32[]{:S(2)}) %collective-permute-start.1) | collective-permute-done | bytes 884768 | tf_op jit(solution)/shard_map/ppermute | solution.py:166
  122.6 2.8 %collective-permute-start.7 = (bf16[4,288,384]{2,1,0:T(8,128)(2,1)S(1)}, bf16[4,288,384]{2,1,0:T(8,128)(2,1)S(1)}, u32[]{:S(2)}, u32[]{:S(2)}) collective-permute-start(bf16[4,288,384]{2,1,0:T(8,128)(2,1)S(1)} %collective-permute-done.1.refs_2_), channel_id=1, source_target_pairs={{0,4},{4,0},{8,12},{12,8},{16,20},{20,16},{24,28},{28,24},{32,36},... | collective-permute-start | bytes 2654216 | tf_op jit(solution)/shard_map/ppermute | solution.py:166
  125.4 0.9 maximum_convert_fusion.refs_8_
  126.3 0.9 collective-permute-done.7.refs_3_
  127.3 0.9 copy-done.11
  128.2 11.1 %shard_map.78 = (bf16[4,288,512]{2,1,0:T(8,128)(2,1)}, f32[4,288,1]{2,1,0:T(8,128)}, bf16[4,512,384]{2,1,0:T(8,128)(2,1)}) custom-call(s32[1]{0:T(128)} %bitcast.quad_ref, bf16[4,288,384]{2,1,0:T(8,128)(2,1)} %bitcast.4.refs_0_, bf16[4,288,384]{2,1,0:T(8,128)(2,1)} %copy-done.10, bf16[4,288,384]{2,1,0:T(8,128)(2,1)} %copy-done.9, ...), custom_call_target="tpu_custom_call" | custom-call | flops 17999998976 | bytes 1048576 | tf_op jit(solution)/shard_map/pallas_call | solution.py:213
  141.4 6.0 %all-to-all-start.1 = ((f32[128,1,36]{2,1,0:T(1,128)}), f32[128,1,36]{2,1,0:T(1,128)S(1)}, u32[]{:S(2)}, u32[]{:S(2)}) async-start(f32[128,1,36]{2,1,0:T(1,128)} %bitcast.18), calls=%async_computation.3 | async-start | bytes 131072 | tf_op jit(solution)/shard_map/all_to_all | solution.py:244
  147.4 0.9 copy.59
  148.6 1.1 reshape.108
  149.7 9.0 %all-to-all-done.1 = f32[128,1,36]{2,1,0:T(1,128)S(1)} async-done(((f32[128,1,36]{2,1,0:T(1,128)}), f32[128,1,36]{2,1,0:T(1,128)S(1)}, u32[]{:S(2)}, u32[]{:S(2)}) %all-to-all-start.1) | async-done | bytes 18464 | tf_op jit(solution)/shard_map/all_to_all | solution.py:244
  158.9 1.9 %gather_fusion = f32[256]{0:T(256)S(1)} fusion(f32[288]{0:T(512)S(1)} %reshape.111, s32[1024]{0:T(1024)S(1)} %pad_clamp_fusion), kind=kCustom, calls=%fused_computation | custom fusion | bytes 3072 | tf_op jit(solution)/shard_map/jit(_take)/gather | solution.py:249
  161.4 7.6 %reduce-scatter.5.cloned.1.call-done = bf16[1,512,384]{2,1,0:T(8,128)(2,1)} async-done(((bf16[4,512,384]{2,1,0:T(8,128)(2,1)}), bf16[1,512,384]{2,1,0:T(8,128)(2,1)}) %reduce-scatter.5.cloned.1.call-update) | async-done | bytes 393232 | tf_op jit(solution)/shard_map/reduce_scatter | solution.py:234
  169.1 2.1 %pad_maximum_fusion = bf16[512,768]{1,0:T(8,128)(2,1)} fusion(bf16[512,384]{1,0:T(8,128)(2,1)} %bitcast.48, bf16[512,384]{1,0:T(8,128)(2,1)} %bitcast.47), kind=kLoop, calls=%fused_computation.4 | loop fusion | flops 1572864 | bytes 1572864 | tf_op jit(solution)/shard_map/concatenate | solution.py:235
  (64 shorter events, 6.9 us)
Async XLA Ops:
  7.2 14.9 %copy-start.2 = (bf16[1152,512]{1,0:T(8,128)(2,1)S(1)}, bf16[1152,512]{1,0:T(8,128)(2,1)}, u32[]{:S(2)}) copy-start(bf16[1152,512]{1,0:T(8,128)(2,1)} %param.8) | copy-start | bytes 3538948
  7.2 94.2 %all-gather.5.cloned.1.call-start = ((), (), s32[]{:S(2)}) async-start(), calls=%async_computation.6 | async-start | bytes 3932160 | tf_op jit(solution)/shard_map/all_gather | solution.py:168
  10.1 22.1 %all-to-all-start = ((bf16[8,40,768]{2,1,0:T(8,128)(2,1)}), bf16[8,40,768]{2,1,0:T(8,128)(2,1)S(1)}, u32[]{:S(2)}, u32[]{:S(2)}) async-start(bf16[8,40,768]{2,1,0:T(8,128)(2,1)} %bitcast.46), calls=%async_computation | async-start | bytes 983040 | tf_op jit(solution)/shard_map/all_to_all | solution.py:159
  22.0 139.5 %reduce-scatter.3.cloned.1.call-start = ((), (), s32[]{:S(2)}) async-start(), calls=%async_computation.4 | async-start | bytes 1966080 | tf_op jit(solution)/shard_map/reduce_scatter | solution.py:234
  25.6 1.0 copy-start.1
  32.3 36.2 %collective-permute-start.4 = (bf16[288]{0:T(512)(128)(2,1)S(1)}, bf16[288]{0:T(512)(128)(2,1)S(1)}, u32[]{:S(2)}, u32[]{:S(2)}) collective-permute-start(bf16[288]{0:T(512)(128)(2,1)S(1)} %reshape_squeeze.3), channel_id=1, source_target_pairs={{0,4},{4,0},{8,12},{12,8},{16,20},{20,16},{24,28},{28,24},{32,36},... | collective-permute-start | bytes 1736 | tf_op jit(solution)/shard_map/ppermute | solution.py:166
  41.9 30.0 %copy-start.4 = (bf16[288,384]{1,0:T(8,128)(2,1)S(1)}, bf16[288,384]{1,0:T(8,128)(2,1)}, u32[]{:S(2)}) copy-start(bf16[288,384]{1,0:T(8,128)(2,1)} %get-tuple-element.28) | copy-start | bytes 663556
  61.3 29.8 %copy-start = (bf16[1152,384]{1,0:T(8,128)(2,1)}, bf16[1152,384]{1,0:T(8,128)(2,1)S(1)}, u32[]{:S(2)}) copy-start(bf16[1152,384]{1,0:T(8,128)(2,1)S(1)} %all-gather.1) | copy-start | bytes 2654212
  61.4 29.7 %collective-permute-start.3 = (bf16[4,288,384]{2,1,0:T(8,128)(2,1)S(1)}, bf16[4,288,384]{2,1,0:T(8,128)(2,1)}, u32[]{:S(2)}, u32[]{:S(2)}) collective-permute-start(bf16[4,288,384]{2,1,0:T(8,128)(2,1)S(1)} %bitcast.40), channel_id=1, source_target_pairs={{0,8},{4,12},{8,0},{12,4},{16,24},{20,28},{24,16},{28,20},{32,40},... | collective-permute-start | bytes 2654216 | tf_op jit(solution)/shard_map/ppermute | solution.py:166
  64.4 36.6 %collective-permute-start.2 = (bf16[4,288,384]{2,1,0:T(8,128)(2,1)S(1)}, bf16[4,288,384]{2,1,0:T(8,128)(2,1)}, u32[]{:S(2)}, u32[]{:S(2)}) collective-permute-start(bf16[4,288,384]{2,1,0:T(8,128)(2,1)S(1)} %bitcast.41), channel_id=1, source_target_pairs={{0,4},{4,0},{8,12},{12,8},{16,20},{20,16},{24,28},{28,24},{32,36},... | collective-permute-start | bytes 2654216 | tf_op jit(solution)/shard_map/ppermute | solution.py:166
  68.6 20.9 %collective-permute-start.5 = (bf16[2,288]{1,0:T(2,128)(2,1)S(1)}, bf16[2,288]{1,0:T(2,128)(2,1)S(1)}, u32[]{:S(2)}, u32[]{:S(2)}) collective-permute-start(bf16[2,288]{1,0:T(2,128)(2,1)S(1)} %pad_maximum_fusion.1), channel_id=1, source_target_pairs={{0,8},{4,12},{8,0},{12,4},{16,24},{20,28},{24,16},{28,20},{32,40},... | collective-permute-start | bytes 3464 | tf_op jit(solution)/shard_map/ppermute | solution.py:166
  91.1 10.3 %collective-permute-start.6 = (bf16[4,288,384]{2,1,0:T(8,128)(2,1)}, bf16[4,288,384]{2,1,0:T(8,128)(2,1)S(1)}, u32[]{:S(2)}, u32[]{:S(2)}) collective-permute-start(bf16[4,288,384]{2,1,0:T(8,128)(2,1)} %collective-permute-done.3.refs_2_), channel_id=1, source_target_pairs={{0,4},{4,0},{8,12},{12,8},{16,20},{20,16},{24,28},{28,24},{32,36},... | collective-permute-start | bytes 2654216 | tf_op jit(solution)/shard_map/ppermute | solution.py:166
  99.2 23.5 %collective-permute-start.1 = (bf16[4,288,384]{2,1,0:T(8,128)(2,1)}, bf16[4,288,384]{2,1,0:T(8,128)(2,1)S(1)}, u32[]{:S(2)}, u32[]{:S(2)}) collective-permute-start(bf16[4,288,384]{2,1,0:T(8,128)(2,1)} %bitcast.4.refs_0_), channel_id=1, source_target_pairs={{0,8},{4,12},{8,0},{12,4},{16,24},{20,28},{24,16},{28,20},{32,40},... | collective-permute-start | bytes 2654216 | tf_op jit(solution)/shard_map/ppermute | solution.py:166
  101.4 1.0 copy-start.5
  110.5 58.6 %reduce-scatter.5.cloned.1.call-start = ((), (), s32[]{:S(2)}) async-start(), calls=%async_computation.5 | async-start | bytes 1966080 | tf_op jit(solution)/shard_map/reduce_scatter | solution.py:234
  110.5 15.8 %collective-permute-start = (bf16[4,288,384]{2,1,0:T(8,128)(2,1)}, bf16[4,288,384]{2,1,0:T(8,128)(2,1)S(1)}, u32[]{:S(2)}, u32[]{:S(2)}) collective-permute-start(bf16[4,288,384]{2,1,0:T(8,128)(2,1)} %bitcast.4.refs_0_), channel_id=1, source_target_pairs={{0,4},{4,0},{8,12},{12,8},{16,20},{20,16},{24,28},{28,24},{32,36},... | collective-permute-start | bytes 2654216 | tf_op jit(solution)/shard_map/ppermute | solution.py:166
  122.6 4.6 %copy-start.9 = (bf16[4,288,384]{2,1,0:T(8,128)(2,1)}, bf16[4,288,384]{2,1,0:T(8,128)(2,1)S(1)}, u32[]{:S(2)}) copy-start(bf16[4,288,384]{2,1,0:T(8,128)(2,1)S(1)} %collective-permute-done.1.refs_2_) | copy-start | bytes 2654212
  122.6 4.6 %collective-permute-start.7 = (bf16[4,288,384]{2,1,0:T(8,128)(2,1)S(1)}, bf16[4,288,384]{2,1,0:T(8,128)(2,1)S(1)}, u32[]{:S(2)}, u32[]{:S(2)}) collective-permute-start(bf16[4,288,384]{2,1,0:T(8,128)(2,1)S(1)} %collective-permute-done.1.refs_2_), channel_id=1, source_target_pairs={{0,4},{4,0},{8,12},{12,8},{16,20},{20,16},{24,28},{28,24},{32,36},... | collective-permute-start | bytes 2654216 | tf_op jit(solution)/shard_map/ppermute | solution.py:166
  126.3 1.0 copy-start.10
  127.3 0.9 copy-start.11
  139.3 0.7 copy-start.7
  139.3 1.1 copy-start.6
  139.3 8.1 %copy-start.3 = (bf16[4,288,512]{2,1,0:T(8,128)(2,1)S(1)}, bf16[4,288,512]{2,1,0:T(8,128)(2,1)}, u32[]{:S(2)}) copy-start(bf16[4,288,512]{2,1,0:T(8,128)(2,1)} %get-tuple-element.17) | copy-start | bytes 3538948
  141.4 17.4 %all-to-all-start.1 = ((f32[128,1,36]{2,1,0:T(1,128)}), f32[128,1,36]{2,1,0:T(1,128)S(1)}, u32[]{:S(2)}, u32[]{:S(2)}) async-start(f32[128,1,36]{2,1,0:T(1,128)} %bitcast.18), calls=%async_computation.3 | async-start | bytes 131072 | tf_op jit(solution)/shard_map/all_to_all | solution.py:244
  148.6 12.3 %copy-start.8 = (f32[2,128]{1,0:T(2,128)S(1)}, f32[2,128]{1,0:T(2,128)}, u32[]{:S(2)}) copy-start(f32[2,128]{1,0:T(2,128)} %get-tuple-element.20) | copy-start | bytes 3076
Sparse Core Ops, SparseCore 0:
  10.1 50.3 all-gather.4
  110.6 24.7 reduce-scatter.2
  139.5 29.5 reduce-scatter.4

commit v3 on v2

v3 whole, which is shorter than its diff:
```python
import functools

import jax
import jax.numpy as jnp
from jax import lax
from jax.experimental import pallas as pl
from jax.experimental.pallas import tpu as pltpu
from jax.sharding import PartitionSpec as P

EXPERTS = 8
TOP = 2
QUADS = 4
VMEM_LIMIT = 56 * 1024 * 1024
CHUNKS = 3
RELATIVE = (1,)
WEIGH = (5 * 10**9, 1 << 20, 10 * 10**9)


def compare_dot(a, b):
    return lax.dot_general(a, b, (((1,), (1,)), ((), ())), preferred_element_type=jnp.float32)


def slab_rows(capacity):
    return (capacity // 8 + 1) * 8


def pack_kernel(capacity, ids_ref, logits_ref, upstream_ref, packed_ref, position_ref, gates_ref):
    tokens = upstream_ref.shape[0]
    rows = packed_ref.shape[0]
    per_expert = rows // EXPERTS
    ids = [ids_ref[k : k + 1, :] for k in range(TOP)]
    expert = lax.broadcasted_iota(jnp.int32, (EXPERTS, tokens), 0)
    chosen = [(expert == ids[k]).astype(jnp.float32) for k in range(TOP)]
    before = (
        lax.broadcasted_iota(jnp.int32, (tokens, tokens), 0)
        < lax.broadcasted_iota(jnp.int32, (tokens, tokens), 1)
    ).astype(jnp.bfloat16)
    earlier = jnp.dot(
        (chosen[0] + chosen[1]).astype(jnp.bfloat16), before, preferred_element_type=jnp.float32
    )
    row = lax.broadcasted_iota(jnp.int32, (rows, tokens), 0)
    column = lax.broadcasted_iota(jnp.int32, (128, tokens), 0)
    place = jnp.zeros((rows, tokens), jnp.float32)
    gate_block = jnp.zeros((rows, 128), jnp.float32)
    for k in range(TOP):
        slot = jnp.sum(earlier * chosen[k], axis=0, keepdims=True).astype(jnp.int32)
        gate = 1.0 / (1.0 + jnp.exp(logits_ref[1 - k : 2 - k, :] - logits_ref[k : k + 1, :]))
        base = ids[k] * per_expert
        place = place + (row == base + slot).astype(jnp.float32)
        sent = jnp.where(row == base + capacity, gate, 0.0).astype(jnp.bfloat16)
        gate_block = gate_block + compare_dot(sent, (column == slot).astype(jnp.bfloat16))
        position_ref[k : k + 1, :] = ids[k] * capacity + slot
        gates_ref[k : k + 1, :] = gate
    packed = jnp.dot(
        place.astype(jnp.bfloat16), upstream_ref[...], preferred_element_type=jnp.float32
    )
    packed_ref[:, :128] = (packed[:, :128] + gate_block).astype(jnp.bfloat16)
    packed_ref[:, 128:] = packed[:, 128:].astype(jnp.bfloat16)


def pack(ids, logits, upstream, capacity):
    tokens, cols = upstream.shape
    rows = EXPERTS * slab_rows(capacity)
    return pl.pallas_call(
        functools.partial(pack_kernel, capacity),
        out_shape=(
            jax.ShapeDtypeStruct((rows, cols), jnp.bfloat16),
            jax.ShapeDtypeStruct((TOP, tokens), jnp.int32),
            jax.ShapeDtypeStruct((TOP, tokens), jnp.float32),
        ),
        compiler_params=pltpu.CompilerParams(vmem_limit_bytes=VMEM_LIMIT),
        cost_estimate=pl.CostEstimate(
            flops=2 * rows * tokens * cols, bytes_accessed=2 * (rows + tokens) * cols, transcendentals=0
        ),
    )(ids, logits, upstream)


class Copies:
    def __init__(self, sems):
        self.sems, self.count = sems, 0

    def __call__(self, source, target):
        made = pltpu.make_async_copy(source, target, self.sems.at[self.count])
        self.count += 1
        made.start()
        return made


def spans(size, count):
    return [slice(i * size, (i + 1) * size) for i in range(count)]


def load_pieces(copy, pieces, full):
    rows, blocks = full.shape[0] // QUADS, pieces[0].shape[0]
    width = full.shape[1] // blocks
    return [
        [
            copy(pieces[i].at[j], full.at[at, column])
            for j, column in enumerate(spans(width, blocks))
        ]
        for i, at in enumerate(spans(rows, QUADS))
    ]


def wait(copies):
    for made in copies:
        made.wait()


def write_product(copy, relative, place_ref, hidden_t, full, product, product_ref):
    blocks, _, width = product.shape
    stores = []
    for j, column in enumerate(spans(width, blocks)):
        result = jnp.dot(hidden_t[...], full[:, column], preferred_element_type=jnp.float32)
        product[j] = result.astype(jnp.bfloat16)
        place = lax.rem(place_ref[1] + blocks - j, blocks) if relative else j
        stores.append(copy(product.at[j], product_ref.at[place]))
    return stores


def both_kernel(
    start, first, relative, place_ref, p0, p1, p2, p3, weight_ref, hidden_t_ref, before_ref,
    proj_ref, product_ref, full, side, hidden_t, total, product, sems,
):
    copy = Copies(sems)
    blocks, _, width = product.shape
    rows = total.shape[0] // QUADS
    sides = [
        copy(weight_ref.at[j, :, start : start + width], side.at[:, column])
        for j, column in enumerate(spans(width, blocks))
    ]
    loads = load_pieces(copy, (p0, p1, p2, p3), full)
    if not first:
        for i, at in enumerate(spans(rows, QUADS)):
            loads[i].append(copy(before_ref.at[at, :], total.at[at, :]))
    hidden_t_load = copy(hidden_t_ref, hidden_t)
    stores = []
    wait(sides)
    for i, at in enumerate(spans(rows, QUADS)):
        wait(loads[i])
        proj = compare_dot(full[at, :], side[...])
        total[at, :] = proj if first else total[at, :] + proj
        stores.append(copy(total.at[at, :], proj_ref.at[at, :]))
    hidden_t_load.wait()
    stores += write_product(copy, relative, place_ref, hidden_t, full, product, product_ref)
    wait(stores)


def product_kernel(
    relative, place_ref, p0, p1, p2, p3, hidden_t_ref, product_ref, full, hidden_t, product, sems
):
    copy = Copies(sems)
    hidden_t_load = copy(hidden_t_ref, hidden_t)
    for loads in load_pieces(copy, (p0, p1, p2, p3), full):
        wait(loads)
    hidden_t_load.wait()
    wait(write_product(copy, relative, place_ref, hidden_t, full, product, product_ref))


def last_kernel(
    start, place_ref, p0, p1, p2, p3, weight_ref, before_ref, hidden_ref, gate_ref,
    grad_ref, partial_ref, full, side, total, hidden, grad, sems,
):
    copy = Copies(sems)
    blocks = p0.shape[0]
    width = full.shape[1] // blocks
    rows = total.shape[0] // QUADS
    sides = [
        copy(weight_ref.at[j, :, start : start + width], side.at[:, column])
        for j, column in enumerate(spans(width, blocks))
    ]
    loads = load_pieces(copy, (p0, p1, p2, p3), full)
    for i, at in enumerate(spans(rows, QUADS)):
        loads[i].append(copy(before_ref.at[at, :], total.at[at, :]))
        loads[i].append(copy(hidden_ref.at[i], hidden.at[i]))
    wait(sides)
    stores = []
    for i, at in enumerate(spans(rows, QUADS)):
        wait(loads[i])
        proj = total[at, :] + compare_dot(full[at, :], side[...])
        owner = jnp.bitwise_xor(place_ref[0], i)
        partial_ref[owner] = jnp.sum(hidden[i].astype(jnp.float32) * proj, axis=1, keepdims=True)
        grad[i] = (gate_ref[i] * proj).astype(jnp.bfloat16)
        stores.append(copy(grad.at[i], grad_ref.at[owner]))
    wait(stores)


def after(x, *others):
    return lax.optimization_barrier((x,) + others)[0]


def local(upstream, router_logits, expert_ids, hidden_saved, down_weight):
    tokens, cols = upstream.shape
    tensor_count = lax.axis_size("tp")
    context_count = lax.axis_size("ctx")
    data_count = lax.axis_size("dp")
    capacity = hidden_saved.shape[0] // context_count
    units = hidden_saved.shape[1]
    rows = EXPERTS * capacity
    total = QUADS * rows
    quad = lax.rem(lax.axis_index("ctx"), QUADS)

    packed, position, gates = pack(expert_ids.T, router_logits.T, upstream, capacity)
    outgoing = packed.reshape(EXPERTS, slab_rows(capacity), cols)
    groups = [[q + QUADS * e for e in range(EXPERTS)] for q in range(QUADS)]
    received = lax.all_to_all(
        outgoing, "ctx", split_axis=0, concat_axis=0, tiled=True, axis_index_groups=groups
    )
    own_rows = received[:, :capacity].reshape(rows, cols)
    own_gate = received[:, capacity, :capacity].reshape(rows)

    def swap(x, bit):
        return lax.ppermute(x, "ctx", [(c, c ^ bit) for c in range(context_count)])

    quads = hidden_saved.reshape(EXPERTS, QUADS, capacity, units).transpose(1, 0, 2, 3)
    quads = quads.reshape(QUADS, rows, units)
    hidden = jnp.stack(
        [
            lax.dynamic_index_in_dim(quads, jnp.bitwise_xor(quad, i), 0, keepdims=False)
            for i in range(QUADS)
        ]
    )

    weight = lax.all_gather(down_weight, "dp", axis=0, tiled=False)
    width = cols // CHUNKS
    gathered = [
        lax.all_gather(own_rows[:, column], "tp", axis=0, tiled=False)
        for column in spans(width, CHUNKS)
    ]

    pair_gate = jnp.stack([own_gate, swap(own_gate, 1)])
    gate = jnp.concatenate([pair_gate, swap(pair_gate, 2)])
    gate = gate.astype(jnp.float32)[:, :, None]
    hidden_t = (gate * hidden.astype(jnp.float32)).astype(jnp.bfloat16)
    hidden_t = hidden_t.reshape(total, units).T

    place = jnp.stack([quad, lax.axis_index("dp")]).astype(jnp.int32)
    held = pl.BlockSpec(memory_space=pl.ANY)
    vmem = pl.BlockSpec(memory_space=pltpu.VMEM)
    smem = pl.BlockSpec(memory_space=pltpu.SMEM)
    product_shape = jax.ShapeDtypeStruct((data_count, units, width), jnp.bfloat16)
    full = pltpu.VMEM((total, data_count * width), jnp.bfloat16)
    side = pltpu.VMEM((units, data_count * width), jnp.bfloat16)
    hidden_t_space = pltpu.VMEM((units, total), jnp.bfloat16)
    total_space = pltpu.VMEM((total, units), jnp.float32)
    product_space = pltpu.VMEM((data_count, units, width), jnp.bfloat16)
    quad_space = pltpu.VMEM((QUADS, rows, units), jnp.bfloat16)
    sems = pltpu.SemaphoreType.DMA((data_count * (QUADS + 2) + 3 * QUADS + 1,))

    def call(kernel, inputs, specs, outputs, out_specs, scratch, weigh):
        return pl.pallas_call(
            kernel,
            out_shape=outputs,
            in_specs=specs,
            out_specs=out_specs,
            scratch_shapes=scratch,
            compiler_params=pltpu.CompilerParams(vmem_limit_bytes=VMEM_LIMIT),
            cost_estimate=pl.CostEstimate(
                flops=weigh, bytes_accessed=1 << 20, transcendentals=0
            ),
        )(place, *inputs)

    def turn(x, k):
        return lax.ppermute(x, "dp", [(d, (d + k) % data_count) for d in range(data_count)])

    def settle(relative, product):
        if not relative:
            return lax.psum_scatter(product, "dp", scatter_dimension=0, tiled=False)
        grad = product[0].astype(jnp.float32)
        for k in (2, 1, 3):
            grad = grad + turn(product[k], data_count - k).astype(jnp.float32)
        return grad.astype(jnp.bfloat16)

    core = [swap(x, 1) for x in gathered]
    others = [swap(x, 2) for x in gathered]
    proj, grads = None, []
    for n in range(CHUNKS):
        first, last = n == 0, n == CHUNKS - 1
        relative = n in RELATIVE
        other = others[n]
        ahead = (proj,) if last else (hidden_t, others[1], *gathered)
        pieces = (gathered[n], core[n], other, swap(after(other, *ahead), 1))
        if last:
            product = call(
                functools.partial(product_kernel, relative),
                pieces + (hidden_t,), [smem] + [held] * 5, product_shape, held,
                [full, hidden_t_space, product_space, sems], WEIGH[n],
            )
            hidden_grad, partial = call(
                functools.partial(last_kernel, n * width),
                pieces + (weight, proj, after(hidden, product), gate),
                [smem] + [held] * 7 + [vmem],
                (
                    jax.ShapeDtypeStruct((QUADS, rows, units), jnp.bfloat16),
                    jax.ShapeDtypeStruct((QUADS, rows, 1), jnp.float32),
                ),
                (held, vmem), [full, side, total_space, quad_space, quad_space, sems], 1 << 20,
            )
        else:
            proj, product = call(
                functools.partial(both_kernel, n * width, first, relative),
                pieces + (weight, hidden_t, hidden_t if first else proj),
                [smem] + [held] * 7,
                (jax.ShapeDtypeStruct((total, units), jnp.float32), product_shape), (held, held),
                [full, side, hidden_t_space, total_space, product_space, sems], WEIGH[n],
            )
        grads.append(settle(relative, product))
    down_grad = jnp.concatenate(grads, axis=1)

    def canonical(x):
        x = x.reshape(QUADS, EXPERTS, capacity, -1).transpose(1, 0, 2, 3)
        return x.reshape(context_count * capacity, -1)

    hidden_grad = canonical(hidden_grad)
    sums = canonical(partial).reshape(context_count, 1, capacity)
    outgoing_sums = jnp.broadcast_to(sums, (context_count, tensor_count, capacity))
    returned = lax.all_to_all(
        outgoing_sums.reshape(context_count * tensor_count, capacity),
        ("ctx", "tp"), split_axis=0, concat_axis=0, tiled=True,
    )
    expert_sums = returned.reshape(EXPERTS, -1, capacity).sum(axis=1)
    route_grad = jnp.take(expert_sums.reshape(-1), position)
    logit_grad = gates * (route_grad - jnp.sum(gates * route_grad, axis=0, keepdims=True))
    return (hidden_grad, down_grad, logit_grad.T)


def solution(mesh):
    in_specs = (
        P(("dp", "ctx"), "tp"),
        P(("dp", "ctx"), None),
        P(("dp", "ctx"), None),
        P("dp", ("ctx", "tp")),
        P(("ctx", "tp"), "dp"),
    )
    out_specs = (P("dp", ("ctx", "tp")), P(("ctx", "tp"), "dp"), P(("dp", "ctx"), None))
    return jax.shard_map(local, mesh=mesh, in_specs=in_specs, out_specs=out_specs, check_vma=False)
```

time: 178 us -> 207 us (1.16)
  starting transfers between devices: 52.2 us -> 73.5 us
  waiting for transfers between devices: 30 us -> 13.8 us
  blocking collectives: 36.7 us -> 45.1 us
  Pallas kernels: 21.3 us -> 29.2 us
  local copies, waits for them, and re-layouts: 16.2 us -> 19.7 us
  other arithmetic: 7.09 us -> 9.95 us
    ppermute x8 -> x11, starting transfers between devices: 34.3 us -> 44.1 us  [swap(): return lax.ppermute(x, 'ctx', [(c, c ^ bit) for c in range(context_count)])]
    ppermute x0 -> x3, starting transfers between devices: none -> 9.79 us  [turn(): lax.ppermute(x, 'dp', [(d, (d + k) % data_count) for d in range(data_coun...]
    ppermute x8 -> x11, waiting for transfers between devices: 11.1 us -> 1.43 us  [swap(): return lax.ppermute(x, 'ctx', [(c, c ^ bit) for c in range(context_count)])]
    all_gather x2 -> x3, blocking collectives: 36.7 us -> 45.1 us  [local(): lax.all_gather(own_rows[:, column], 'tp', axis=0, tiled=False)]
    pallas_call x2 -> x4, Pallas kernels: 19.1 us -> 27 us  [call(): pl.pallas_call(kernel, out_shape=outputs, in_specs=specs, out_specs=out_s...]
    reduce_scatter x2, waiting for transfers between devices: 7.62 us -> 0.01 us  [settle(): return lax.psum_scatter(product, 'dp', scatter_dimension=0, tiled=False)]
  transfers between devices with their start and end apart: 13 -> 19, of which waited for: 6 -> 3; matrix products, arithmetic and copies ran while one was open for 10% -> 12% of each run, Pallas kernels for 12% -> 14%
where the time goes in v3:
time: 207 us; the launch traced here: 206 us
  starting transfers between devices  73.5 us (36%)
  blocking collectives  45.1 us (22%)
  Pallas kernels  29.2 us (14%)
  local copies, waits for them, and re-layouts  19.7 us (10%)
  between operations  14.4 us (7%)
  waiting for transfers between devices  13.8 us (7%)
  other arithmetic  9.95 us (5%)
    all_gather x3, blocking collectives, local(): lax.all_gather(own_rows[:, column], 'tp', axis=0, tiled=False)  45.1 us
    ppermute x11, starting transfers between devices, swap(): return lax.ppermute(x, 'ctx', [(c, c ^ bit) for c in range(context_count)])  44.1 us
    pallas_call x4, Pallas kernels, call(): pl.pallas_call(kernel, out_shape=outputs, in_specs=specs, out_specs=out_s...  27 us
    all_to_all x1, starting transfers between devices, local(): lax.all_to_all(outgoing, 'ctx', split_axis=0, concat_axis=0, tiled=True,...  11.9 us
    ppermute x3, starting transfers between devices, turn(): lax.ppermute(x, 'dp', [(d, (d + k) % data_count) for d in range(data_coun...  9.79 us
    all_to_all x1, waiting for transfers between devices, local(): lax.all_to_all(outgoing_sums.reshape(context_count * tensor_count, capaci...  8.89 us
    all_to_all x1, starting transfers between devices, local(): lax.all_to_all(outgoing_sums.reshape(context_count * tensor_count, capaci...  7.64 us
  transfers between devices with their start and end apart: 19, of which 3 were waited for; matrix products, arithmetic and copies ran while one was open for 12% of the time, Pallas kernels for 14%

profile of v3, /device:TPU:1, one launch (start us, length us, event | category | flops | bytes accessed | tf_op | source)
XLA Modules:
  0.0 205.7 jit_solution(6750198063748647000)
XLA Ops:
  7.9 2.2 %shard_map.76 = (bf16[320,768]{1,0:T(8,128)(2,1)}, s32[2,128]{1,0:T(2,128)}, f32[2,128]{1,0:T(2,128)}) custom-call(s32[2,128]{1,0:T(2,128)} %bitcast.68, f32[2,128]{1,0:T(2,128)} %bitcast.69, bf16[128,768]{1,0:T(8,128)(2,1)} %upstream_ref.1), custom_call_target="tpu_custom_call" | custom-call | flops 62914560 | bytes 688128 | tf_op jit(solution)/shard_map/pallas_call | solution.py:64
  10.1 11.9 %all-to-all-start = ((bf16[8,40,768]{2,1,0:T(8,128)(2,1)}), bf16[8,40,768]{2,1,0:T(8,128)(2,1)}, u32[]{:S(2)}, u32[]{:S(2)}) async-start(bf16[8,40,768]{2,1,0:T(8,128)(2,1)} %bitcast.61), calls=%async_computation | async-start | bytes 983040 | tf_op jit(solution)/shard_map/all_to_all | solution.py:206
  23.0 2.4 %constant_dynamic-slice_fusion = (bf16[1,288,512]{2,0,1:T(2,128)(2,1)S(1)}, bf16[1,288,512]{2,0,1:T(2,128)(2,1)S(1)}, bf16[1,288,512]{2,0,1:T(2,128)(2,1)S(1)}, bf16[1,288,512]{2,0,1:T(2,128)(2,1)S(1)}) fusion(bf16[4,288,512]{2,0,1:T(4,128)(2,1)S(1)} %bitcast.51, s32[]{:T(128)S(6)} %select_n.25, s32[]{:T(128)S(6)} %select_n.24, s32[]{:T(128)S(6)} %select_n.23, ...), kind=kLoop, calls=%fused_computation.25 | loop fusion | bytes 2359312 | tf_op jit(solution)/shard_map/jit(dynamic_index_in_dim)/dynamic_slice | solution.py:219
  25.6 1.9 bitcast_convert_fusion
  27.5 2.0 copy.58
  29.6 2.7 %all-to-all-done = bf16[8,40,768]{2,1,0:T(8,128)(2,1)} async-done(((bf16[8,40,768]{2,1,0:T(8,128)(2,1)}), bf16[8,40,768]{2,1,0:T(8,128)(2,1)}, u32[]{:S(2)}, u32[]{:S(2)}) %all-to-all-start) | async-done | bytes 491552 | tf_op jit(solution)/shard_map/all_to_all | solution.py:206
  34.4 15.2 %all-gather.2 = bf16[1152,256]{1,0:T(8,128)(2,1)} all-gather(bf16[288,256]{1,0:T(8,128)(2,1)S(1)} %get-tuple-element.36), channel_id=4, replica_groups=mesh['dp'=4,'ctx'=32,'tp'=4] {'tp'}, dimensions={0}, use_global_device_ids=true | all-gather | bytes 737280 | tf_op jit(solution)/shard_map/all_gather | solution.py:227
  49.5 9.5 %collective-permute-start.8 = (bf16[4,288,256]{2,1,0:T(8,128)(2,1)}, bf16[4,288,256]{2,1,0:T(8,128)(2,1)}, u32[]{:S(2)}, u32[]{:S(2)}) collective-permute-start(bf16[4,288,256]{2,1,0:T(8,128)(2,1)} %bitcast.12.p0), channel_id=1, source_target_pairs={{0,8},{4,12},{8,0},{12,4},{16,24},{20,28},{24,16},{28,20},{32,40},... | collective-permute-start | bytes 1769480 | tf_op jit(solution)/shard_map/ppermute | solution.py:213
  59.1 6.3 %collective-permute-start.7 = (bf16[4,288,256]{2,1,0:T(8,128)(2,1)}, bf16[4,288,256]{2,1,0:T(8,128)(2,1)}, u32[]{:S(2)}, u32[]{:S(2)}) collective-permute-start(bf16[4,288,256]{2,1,0:T(8,128)(2,1)} %bitcast.12.p0), channel_id=1, source_target_pairs={{0,4},{4,0},{8,12},{12,8},{16,20},{20,16},{24,28},{28,24},{32,36},... | collective-permute-start | bytes 1769480 | tf_op jit(solution)/shard_map/ppermute | solution.py:213
  65.4 1.9 collective-permute-start.4
  67.3 14.1 %all-gather.1 = bf16[1152,256]{1,0:T(8,128)(2,1)S(1)} all-gather(bf16[288,256]{1,0:T(8,128)(2,1)S(1)} %get-tuple-element.37), channel_id=3, replica_groups=mesh['dp'=4,'ctx'=32,'tp'=4] {'tp'}, dimensions={0}, use_global_device_ids=true | all-gather | bytes 737280 | tf_op jit(solution)/shard_map/all_gather | solution.py:227
  81.4 1.9 collective-permute-start.3
  83.4 3.4 %collective-permute-start.5 = (bf16[2,288]{1,0:T(2,128)(2,1)S(1)}, bf16[2,288]{1,0:T(2,128)(2,1)S(1)}, u32[]{:S(2)}, u32[]{:S(2)}) collective-permute-start(bf16[2,288]{1,0:T(2,128)(2,1)S(1)} %pad_maximum_fusion.1), channel_id=1, source_target_pairs={{0,8},{4,12},{8,0},{12,4},{16,24},{20,28},{24,16},{28,20},{32,40},... | collective-permute-start | bytes 3464 | tf_op jit(solution)/shard_map/ppermute | solution.py:213
  86.7 15.9 %all-gather = bf16[1152,256]{1,0:T(8,128)(2,1)S(1)} all-gather(bf16[288,256]{1,0:T(8,128)(2,1)S(1)} %get-tuple-element.38), channel_id=2, replica_groups=mesh['dp'=4,'ctx'=32,'tp'=4] {'tp'}, dimensions={0}, use_global_device_ids=true | all-gather | bytes 737280 | tf_op jit(solution)/shard_map/all_gather | solution.py:227
  107.4 10.3 %collective-permute-start.9 = (bf16[4,288,256]{2,1,0:T(8,128)(2,1)}, bf16[4,288,256]{2,1,0:T(8,128)(2,1)S(1)}, u32[]{:S(2)}, u32[]{:S(2)}) collective-permute-start(bf16[4,288,256]{2,1,0:T(8,128)(2,1)} %collective-permute-done.8.p2), channel_id=1, source_target_pairs={{0,4},{4,0},{8,12},{12,8},{16,20},{20,16},{24,28},{28,24},{32,36},... | collective-permute-start | bytes 1769480 | tf_op jit(solution)/shard_map/ppermute | solution.py:213
  118.4 1.9 collective-permute-start.2
  120.3 1.9 collective-permute-start.1
  122.2 2.4 %collective-permute-start.6 = (bf16[4,288,256]{2,1,0:T(8,128)(2,1)}, bf16[4,288,256]{2,1,0:T(8,128)(2,1)}, u32[]{:S(2)}, u32[]{:S(2)}) collective-permute-start(bf16[4,288,256]{2,1,0:T(8,128)(2,1)} %collective-permute-done.3.p2), channel_id=1, source_target_pairs={{0,4},{4,0},{8,12},{12,8},{16,20},{20,16},{24,28},{28,24},{32,36},... | collective-permute-start | bytes 1769480 | tf_op jit(solution)/shard_map/ppermute | solution.py:213
  125.5 6.7 %shard_map.77 = (f32[1152,512]{1,0:T(8,128)}, bf16[4,512,256]{2,1,0:T(8,128)(2,1)}) custom-call(s32[2]{0:T(128)} %pad_add_fusion.place_ref, bf16[4,288,256]{2,1,0:T(8,128)(2,1)} %bitcast.12.p0, bf16[4,288,256]{2,1,0:T(8,128)(2,1)} %collective-permute-done.7.p1, bf16[4,288,256]{2,1,0:T(8,128)(2,1)} %collective-permute-done.8.p2, ...), custom_call_target="tpu_custom_call" | custom-call | flops 5000000000 | bytes 1048576 | tf_op jit(solution)/shard_map/pallas_call | solution.py:251
  132.3 1.9 collective-permute-start
  135.1 7.5 %shard_map.78 = (f32[1152,512]{1,0:T(8,128)}, bf16[4,512,256]{2,1,0:T(8,128)(2,1)}) custom-call(s32[2]{0:T(128)} %pad_add_fusion.place_ref, bf16[4,288,256]{2,1,0:T(8,128)(2,1)} %bitcast.60, bf16[4,288,256]{2,1,0:T(8,128)(2,1)} %copy-done.12, bf16[4,288,256]{2,1,0:T(8,128)(2,1)} %collective-permute-done.3.p2, ...), custom_call_target="tpu_custom_call" | custom-call | flops 1048576 | bytes 1048576 | tf_op jit(solution)/shard_map/pallas_call | solution.py:251
  142.6 2.6 %collective-permute-start.10 = (bf16[4,288,256]{2,1,0:T(8,128)(2,1)S(1)}, bf16[4,288,256]{2,1,0:T(8,128)(2,1)S(1)}, u32[]{:S(2)}, u32[]{:S(2)}) collective-permute-start(bf16[4,288,256]{2,1,0:T(8,128)(2,1)S(1)} %collective-permute-done.1.p2), channel_id=1, source_target_pairs={{0,4},{4,0},{8,12},{12,8},{16,20},{20,16},{24,28},{28,24},{32,36},... | collective-permute-start | bytes 1769480 | tf_op jit(solution)/shard_map/ppermute | solution.py:213
  147.5 5.3 %shard_map.79 = bf16[4,512,256]{2,1,0:T(8,128)(2,1)} custom-call(s32[2]{0:T(128)} %pad_add_fusion.place_ref, bf16[4,288,256]{2,1,0:T(8,128)(2,1)} %bitcast.56, bf16[4,288,256]{2,1,0:T(8,128)(2,1)} %copy-done.10, bf16[4,288,256]{2,1,0:T(8,128)(2,1)} %copy-done.9, bf16[4,288,256]{2,1,0:T(8,128)(2,1)} %copy-done.11, bf16[512,1152]{1,0:T(8,128)(2,1)} %fusion.hidden_t_ref.before_ref), custom_call_target="tpu_custom_call" | custom-call | flops 10000000000 | bytes 1048576 | tf_op jit(solution)/shard_map/pallas_call | solution.py:251
  154.9 4.5 %collective-permute-start.11 = (bf16[512,256]{1,0:T(8,128)(2,1)}, bf16[512,256]{1,0:T(8,128)(2,1)S(1)}, u32[]{:S(2)}, u32[]{:S(2)}) collective-permute-start(bf16[512,256]{1,0:T(8,128)(2,1)} %get-tuple-element.33), channel_id=1, source_target_pairs={{0,256},{128,384},{256,0},{384,128},{1,257},{129,385},{257,1},{385... | collective-permute-start | bytes 786440 | tf_op jit(solution)/shard_map/ppermute | solution.py:264
  159.5 1.9 collective-permute-start.12
  161.4 3.4 %collective-permute-start.13 = (bf16[512,256]{1,0:T(8,128)(2,1)}, bf16[512,256]{1,0:T(8,128)(2,1)S(1)}, u32[]{:S(2)}, u32[]{:S(2)}) collective-permute-start(bf16[512,256]{1,0:T(8,128)(2,1)} %get-tuple-element.34), channel_id=1, source_target_pairs={{0,128},{128,256},{256,384},{384,0},{1,129},{129,257},{257,385},{3... | collective-permute-start | bytes 786440 | tf_op jit(solution)/shard_map/ppermute | solution.py:264
  165.7 7.5 %shard_map.80 = (bf16[4,288,512]{2,1,0:T(8,128)(2,1)}, f32[4,288,1]{2,1,0:T(8,128)}) custom-call(s32[2]{0:T(128)} %pad_add_fusion.place_ref, bf16[4,288,256]{2,1,0:T(8,128)(2,1)} %bitcast.57, bf16[4,288,256]{2,1,0:T(8,128)(2,1)} %copy-done.10, bf16[4,288,256]{2,1,0:T(8,128)(2,1)} %copy-done.9, bf16[4,288,256]{2,1,0:T(8,128)(2,1)} %copy-done.11, ...), custom_call_target="tpu_custom_call" | custom-call | flops 1048576 | bytes 1048576 | tf_op jit(solution)/shard_map/pallas_call | solution.py:251
  173.3 1.4 reduce.4
  175.5 7.6 %all-to-all-start.1 = ((f32[128,1,36]{2,1,0:T(1,128)}), f32[128,1,36]{2,1,0:T(1,128)S(1)}, u32[]{:S(2)}, u32[]{:S(2)}) async-start(f32[128,1,36]{2,1,0:T(1,128)} %bitcast.24), calls=%async_computation.3 | async-start | bytes 131072 | tf_op jit(solution)/shard_map/all_to_all | solution.py:317
  185.6 8.9 %all-to-all-done.1 = f32[128,1,36]{2,1,0:T(1,128)S(1)} async-done(((f32[128,1,36]{2,1,0:T(1,128)}), f32[128,1,36]{2,1,0:T(1,128)S(1)}, u32[]{:S(2)}, u32[]{:S(2)}) %all-to-all-start.1) | async-done | bytes 18464 | tf_op jit(solution)/shard_map/all_to_all | solution.py:317
  194.6 1.9 gather_fusion
  197.2 2.0 pad_maximum_fusion
  (90 shorter events, 20.2 us)
Async XLA Ops:
  7.2 14.9 %copy-start.4 = (bf16[1152,512]{1,0:T(8,128)(2,1)S(1)}, bf16[1152,512]{1,0:T(8,128)(2,1)}, u32[]{:S(2)}) copy-start(bf16[1152,512]{1,0:T(8,128)(2,1)} %param.8) | copy-start | bytes 3538948
  7.2 117.5 %all-gather.6.cloned.1.call-start = ((), (), s32[]{:S(2)}) async-start(), calls=%async_computation.6 | async-start | bytes 3932160 | tf_op jit(solution)/shard_map/all_gather | solution.py:224
  10.1 22.2 %all-to-all-start = ((bf16[8,40,768]{2,1,0:T(8,128)(2,1)}), bf16[8,40,768]{2,1,0:T(8,128)(2,1)}, u32[]{:S(2)}, u32[]{:S(2)}) async-start(bf16[8,40,768]{2,1,0:T(8,128)(2,1)} %bitcast.61), calls=%async_computation | async-start | bytes 983040 | tf_op jit(solution)/shard_map/all_to_all | solution.py:206
  22.0 175.2 %reduce-scatter.3.cloned.1.call-start = ((), (), s32[]{:S(2)}) async-start(), calls=%async_computation.4 | async-start | bytes 1310720 | tf_op jit(solution)/shard_map/reduce_scatter | solution.py:268
  25.6 1.9 copy-start
  49.5 57.9 %collective-permute-start.8 = (bf16[4,288,256]{2,1,0:T(8,128)(2,1)}, bf16[4,288,256]{2,1,0:T(8,128)(2,1)}, u32[]{:S(2)}, u32[]{:S(2)}) collective-permute-start(bf16[4,288,256]{2,1,0:T(8,128)(2,1)} %bitcast.12.p0), channel_id=1, source_target_pairs={{0,8},{4,12},{8,0},{12,4},{16,24},{20,28},{24,16},{28,20},{32,40},... | collective-permute-start | bytes 1769480 | tf_op jit(solution)/shard_map/ppermute | solution.py:213
  59.1 65.6 %collective-permute-start.7 = (bf16[4,288,256]{2,1,0:T(8,128)(2,1)}, bf16[4,288,256]{2,1,0:T(8,128)(2,1)}, u32[]{:S(2)}, u32[]{:S(2)}) collective-permute-start(bf16[4,288,256]{2,1,0:T(8,128)(2,1)} %bitcast.12.p0), channel_id=1, source_target_pairs={{0,4},{4,0},{8,12},{12,8},{16,20},{20,16},{24,28},{28,24},{32,36},... | collective-permute-start | bytes 1769480 | tf_op jit(solution)/shard_map/ppermute | solution.py:213
  65.4 17.9 %collective-permute-start.4 = (bf16[288]{0:T(512)(128)(2,1)S(1)}, bf16[288]{0:T(512)(128)(2,1)S(1)}, u32[]{:S(2)}, u32[]{:S(2)}) collective-permute-start(bf16[288]{0:T(512)(128)(2,1)S(1)} %reshape_squeeze.3), channel_id=1, source_target_pairs={{0,4},{4,0},{8,12},{12,8},{16,20},{20,16},{24,28},{28,24},{32,36},... | collective-permute-start | bytes 1736 | tf_op jit(solution)/shard_map/ppermute | solution.py:213
  81.4 37.0 %copy-start.2 = (bf16[1152,256]{1,0:T(8,128)(2,1)}, bf16[1152,256]{1,0:T(8,128)(2,1)S(1)}, u32[]{:S(2)}) copy-start(bf16[1152,256]{1,0:T(8,128)(2,1)S(1)} %all-gather.1) | copy-start | bytes 1769476
  81.4 26.0 %collective-permute-start.3 = (bf16[4,288,256]{2,1,0:T(8,128)(2,1)S(1)}, bf16[4,288,256]{2,1,0:T(8,128)(2,1)}, u32[]{:S(2)}, u32[]{:S(2)}) collective-permute-start(bf16[4,288,256]{2,1,0:T(8,128)(2,1)S(1)} %bitcast.58), channel_id=1, source_target_pairs={{0,8},{4,12},{8,0},{12,4},{16,24},{20,28},{24,16},{28,20},{32,40},... | collective-permute-start | bytes 1769480 | tf_op jit(solution)/shard_map/ppermute | solution.py:213
  83.4 20.8 %collective-permute-start.5 = (bf16[2,288]{1,0:T(2,128)(2,1)S(1)}, bf16[2,288]{1,0:T(2,128)(2,1)S(1)}, u32[]{:S(2)}, u32[]{:S(2)}) collective-permute-start(bf16[2,288]{1,0:T(2,128)(2,1)S(1)} %pad_maximum_fusion.1), channel_id=1, source_target_pairs={{0,8},{4,12},{8,0},{12,4},{16,24},{20,28},{24,16},{28,20},{32,40},... | collective-permute-start | bytes 3464 | tf_op jit(solution)/shard_map/ppermute | solution.py:213
  102.6 29.7 %copy-start.1 = (bf16[1152,256]{1,0:T(8,128)(2,1)}, bf16[1152,256]{1,0:T(8,128)(2,1)S(1)}, u32[]{:S(2)}) copy-start(bf16[1152,256]{1,0:T(8,128)(2,1)S(1)} %all-gather) | copy-start | bytes 1769476
  107.4 17.2 %collective-permute-start.9 = (bf16[4,288,256]{2,1,0:T(8,128)(2,1)}, bf16[4,288,256]{2,1,0:T(8,128)(2,1)S(1)}, u32[]{:S(2)}, u32[]{:S(2)}) collective-permute-start(bf16[4,288,256]{2,1,0:T(8,128)(2,1)} %collective-permute-done.8.p2), channel_id=1, source_target_pairs={{0,4},{4,0},{8,12},{12,8},{16,20},{20,16},{24,28},{28,24},{32,36},... | collective-permute-start | bytes 1769480 | tf_op jit(solution)/shard_map/ppermute | solution.py:213
  118.4 15.9 %collective-permute-start.2 = (bf16[4,288,256]{2,1,0:T(8,128)(2,1)S(1)}, bf16[4,288,256]{2,1,0:T(8,128)(2,1)S(1)}, u32[]{:S(2)}, u32[]{:S(2)}) collective-permute-start(bf16[4,288,256]{2,1,0:T(8,128)(2,1)S(1)} %bitcast.59), channel_id=1, source_target_pairs={{0,4},{4,0},{8,12},{12,8},{16,20},{20,16},{24,28},{28,24},{32,36},... | collective-permute-start | bytes 1769480 | tf_op jit(solution)/shard_map/ppermute | solution.py:213
  120.3 22.3 %collective-permute-start.1 = (bf16[4,288,256]{2,1,0:T(8,128)(2,1)S(1)}, bf16[4,288,256]{2,1,0:T(8,128)(2,1)S(1)}, u32[]{:S(2)}, u32[]{:S(2)}) collective-permute-start(bf16[4,288,256]{2,1,0:T(8,128)(2,1)S(1)} %bitcast.54), channel_id=1, source_target_pairs={{0,8},{4,12},{8,0},{12,4},{16,24},{20,28},{24,16},{28,20},{32,40},... | collective-permute-start | bytes 1769480 | tf_op jit(solution)/shard_map/ppermute | solution.py:213
  122.2 12.0 %collective-permute-start.6 = (bf16[4,288,256]{2,1,0:T(8,128)(2,1)}, bf16[4,288,256]{2,1,0:T(8,128)(2,1)}, u32[]{:S(2)}, u32[]{:S(2)}) collective-permute-start(bf16[4,288,256]{2,1,0:T(8,128)(2,1)} %collective-permute-done.3.p2), channel_id=1, source_target_pairs={{0,4},{4,0},{8,12},{12,8},{16,20},{20,16},{24,28},{28,24},{32,36},... | collective-permute-start | bytes 1769480 | tf_op jit(solution)/shard_map/ppermute | solution.py:213
  132.3 64.9 %reduce-scatter.5.cloned.1.call-start = ((), (), s32[]{:S(2)}) async-start(), calls=%async_computation.5 | async-start | bytes 1310720 | tf_op jit(solution)/shard_map/reduce_scatter | solution.py:268
  132.3 12.9 %collective-permute-start = (bf16[4,288,256]{2,1,0:T(8,128)(2,1)S(1)}, bf16[4,288,256]{2,1,0:T(8,128)(2,1)S(1)}, u32[]{:S(2)}, u32[]{:S(2)}) collective-permute-start(bf16[4,288,256]{2,1,0:T(8,128)(2,1)S(1)} %bitcast.55), channel_id=1, source_target_pairs={{0,4},{4,0},{8,12},{12,8},{16,20},{20,16},{24,28},{28,24},{32,36},... | collective-permute-start | bytes 1769480 | tf_op jit(solution)/shard_map/ppermute | solution.py:213
  142.6 4.0 %copy-start.9 = (bf16[4,288,256]{2,1,0:T(8,128)(2,1)}, bf16[4,288,256]{2,1,0:T(8,128)(2,1)S(1)}, u32[]{:S(2)}) copy-start(bf16[4,288,256]{2,1,0:T(8,128)(2,1)S(1)} %collective-permute-done.1.p2) | copy-start | bytes 1769476
  142.6 4.0 %collective-permute-start.10 = (bf16[4,288,256]{2,1,0:T(8,128)(2,1)S(1)}, bf16[4,288,256]{2,1,0:T(8,128)(2,1)S(1)}, u32[]{:S(2)}, u32[]{:S(2)}) collective-permute-start(bf16[4,288,256]{2,1,0:T(8,128)(2,1)S(1)} %collective-permute-done.1.p2), channel_id=1, source_target_pairs={{0,4},{4,0},{8,12},{12,8},{16,20},{20,16},{24,28},{28,24},{32,36},... | collective-permute-start | bytes 1769480 | tf_op jit(solution)/shard_map/ppermute | solution.py:213
  145.2 1.4 copy-start.10
  152.8 1.2 copy-start.6
  152.8 12.0 %copy-start.13 = (s32[2,128]{1,0:T(2,128)S(1)}, s32[2,128]{1,0:T(2,128)}, u32[]{:S(2)}) copy-start(s32[2,128]{1,0:T(2,128)} %get-tuple-element.27) | copy-start | bytes 3076
  152.8 12.0 %copy-start.3 = (bf16[2,288,1]{2,1,0:T(8,128)(2,1)S(1)}, bf16[2,288,1]{2,1,0:T(8,128)(2,1)}, u32[]{:S(2)}) copy-start(bf16[2,288,1]{2,1,0:T(8,128)(2,1)} %copy.52) | copy-start | bytes 3460
  152.8 12.0 %copy-start.7 = (bf16[1,288,1]{2,1,0:T(8,128)(2,1)S(1)}, bf16[1,288,1]{2,1,0:T(8,128)(2,1)}, u32[]{:S(2)}) copy-start(bf16[1,288,1]{2,1,0:T(8,128)(2,1)} %concatenate.25) | copy-start | bytes 1732
  152.8 12.0 %copy-start.8 = (bf16[1,288,1]{2,1,0:T(8,128)(2,1)S(1)}, bf16[1,288,1]{2,1,0:T(8,128)(2,1)}, u32[]{:S(2)}) copy-start(bf16[1,288,1]{2,1,0:T(8,128)(2,1)} %concatenate.26) | copy-start | bytes 1732
  154.9 28.2 %collective-permute-start.11 = (bf16[512,256]{1,0:T(8,128)(2,1)}, bf16[512,256]{1,0:T(8,128)(2,1)S(1)}, u32[]{:S(2)}, u32[]{:S(2)}) collective-permute-start(bf16[512,256]{1,0:T(8,128)(2,1)} %get-tuple-element.33), channel_id=1, source_target_pairs={{0,256},{128,384},{256,0},{384,128},{1,257},{129,385},{257,1},{385... | collective-permute-start | bytes 786440 | tf_op jit(solution)/shard_map/ppermute | solution.py:264
  159.5 23.7 %collective-permute-start.12 = (bf16[512,256]{1,0:T(8,128)(2,1)}, bf16[512,256]{1,0:T(8,128)(2,1)S(1)}, u32[]{:S(2)}, u32[]{:S(2)}) collective-permute-start(bf16[512,256]{1,0:T(8,128)(2,1)} %get-tuple-element.35), channel_id=1, source_target_pairs={{0,384},{128,0},{256,128},{384,256},{1,385},{129,1},{257,129},{385... | collective-permute-start | bytes 786440 | tf_op jit(solution)/shard_map/ppermute | solution.py:264
  161.4 21.8 %collective-permute-start.13 = (bf16[512,256]{1,0:T(8,128)(2,1)}, bf16[512,256]{1,0:T(8,128)(2,1)S(1)}, u32[]{:S(2)}, u32[]{:S(2)}) collective-permute-start(bf16[512,256]{1,0:T(8,128)(2,1)} %get-tuple-element.34), channel_id=1, source_target_pairs={{0,128},{128,256},{256,384},{384,0},{1,129},{129,257},{257,385},{3... | collective-permute-start | bytes 786440 | tf_op jit(solution)/shard_map/ppermute | solution.py:264
  173.3 10.0 %copy-start.5 = (bf16[4,288,512]{2,1,0:T(8,128)(2,1)S(1)}, bf16[4,288,512]{2,1,0:T(8,128)(2,1)}, u32[]{:S(2)}) copy-start(bf16[4,288,512]{2,1,0:T(8,128)(2,1)} %get-tuple-element.23) | copy-start | bytes 3538948
  175.5 19.1 %all-to-all-start.1 = ((f32[128,1,36]{2,1,0:T(1,128)}), f32[128,1,36]{2,1,0:T(1,128)S(1)}, u32[]{:S(2)}, u32[]{:S(2)}) async-start(f32[128,1,36]{2,1,0:T(1,128)} %bitcast.24), calls=%async_computation.3 | async-start | bytes 131072 | tf_op jit(solution)/shard_map/all_to_all | solution.py:317
  184.5 12.1 %copy-start.14 = (f32[2,128]{1,0:T(2,128)S(1)}, f32[2,128]{1,0:T(2,128)}, u32[]{:S(2)}) copy-start(f32[2,128]{1,0:T(2,128)} %get-tuple-element.26) | copy-start | bytes 3076
  (3 other events, 2.5 us)
Sparse Core Ops, SparseCore 0:
  10.1 50.3 all-gather.5
  132.4 21.0 reduce-scatter.2
  156.5 34.0 reduce-scatter.4

commit v4 on v3

--- a/solution.py
+++ b/solution.py
@@ -11,9 +11,9 @@
 TOP = 2
 QUADS = 4
 VMEM_LIMIT = 56 * 1024 * 1024
-CHUNKS = 3
-RELATIVE = (1,)
-WEIGH = (5 * 10**9, 1 << 20, 10 * 10**9)
+CHUNKS = 2
+RELATIVE = ()
+WEIGH = (1 << 20, 18 * 10**9)
 
 
 def compare_dot(a, b):
@@ -95,7 +95,7 @@
     width = full.shape[1] // blocks
     return [
         [
-            copy(pieces[i].at[j], full.at[at, column])
+            copy(pieces[i].at[j, 0:rows, :], full.at[at, column])
             for j, column in enumerate(spans(width, blocks))
         ]
         for i, at in enumerate(spans(rows, QUADS))
@@ -173,13 +173,17 @@
     for i, at in enumerate(spans(rows, QUADS)):
         loads[i].append(copy(before_ref.at[at, :], total.at[at, :]))
         loads[i].append(copy(hidden_ref.at[i], hidden.at[i]))
+    ones = jnp.ones((8, hidden.shape[2]), jnp.float32)
     wait(sides)
     stores = []
     for i, at in enumerate(spans(rows, QUADS)):
         wait(loads[i])
         proj = total[at, :] + compare_dot(full[at, :], side[...])
         owner = jnp.bitwise_xor(place_ref[0], i)
-        partial_ref[owner] = jnp.sum(hidden[i].astype(jnp.float32) * proj, axis=1, keepdims=True)
+        partial_ref[owner] = lax.dot_general(
+            ones, hidden[i].astype(jnp.float32) * proj, (((1,), (1,)), ((), ())),
+            precision=lax.Precision.HIGHEST, preferred_element_type=jnp.float32,
+        )
         grad[i] = (gate_ref[i] * proj).astype(jnp.bfloat16)
         stores.append(copy(grad.at[i], grad_ref.at[owner]))
     wait(stores)
@@ -207,7 +211,7 @@
         outgoing, "ctx", split_axis=0, concat_axis=0, tiled=True, axis_index_groups=groups
     )
     own_rows = received[:, :capacity].reshape(rows, cols)
-    own_gate = received[:, capacity, :capacity].reshape(rows)
+    gate_line = received[:, capacity, :capacity].reshape(1, rows)
 
     def swap(x, bit):
         return lax.ppermute(x, "ctx", [(c, c ^ bit) for c in range(context_count)])
@@ -221,18 +225,21 @@
         ]
     )
 
+    hidden_turned = hidden.reshape(total, units).T
     weight = lax.all_gather(down_weight, "dp", axis=0, tiled=False)
     width = cols // CHUNKS
-    gathered = [
-        lax.all_gather(own_rows[:, column], "tp", axis=0, tiled=False)
-        for column in spans(width, CHUNKS)
-    ]
-
-    pair_gate = jnp.stack([own_gate, swap(own_gate, 1)])
-    gate = jnp.concatenate([pair_gate, swap(pair_gate, 2)])
-    gate = gate.astype(jnp.float32)[:, :, None]
-    hidden_t = (gate * hidden.astype(jnp.float32)).astype(jnp.bfloat16)
-    hidden_t = hidden_t.reshape(total, units).T
+    sent = [own_rows[:, column] for column in spans(width, CHUNKS)]
+    sent[0] = jnp.concatenate([sent[0], jnp.pad(gate_line, ((0, 7), (0, width - rows)))])
+    sent[0] = after(sent[0], hidden, hidden_turned)
+    gathered = [lax.all_gather(x, "tp", axis=0, tiled=False) for x in sent]
+    others = [swap(x, 2) for x in gathered]
+    core = [swap(after(x, others[0], *gathered), 1) for x in gathered]
+    last_others = swap(after(others[0], *gathered), 1)
+    firsts = (gathered[0], core[0], others[0], last_others)
+
+    gate = jnp.stack([piece[0, rows, :rows] for piece in firsts]).astype(jnp.float32)
+    hidden_t = (hidden_turned.astype(jnp.float32) * gate.reshape(1, total)).astype(jnp.bfloat16)
+    gate_column = gate[:, :, None]
 
     place = jnp.stack([quad, lax.axis_index("dp")]).astype(jnp.int32)
     held = pl.BlockSpec(memory_space=pl.ANY)
@@ -247,7 +254,7 @@
     quad_space = pltpu.VMEM((QUADS, rows, units), jnp.bfloat16)
     sems = pltpu.SemaphoreType.DMA((data_count * (QUADS + 2) + 3 * QUADS + 1,))
 
-    def call(kernel, inputs, specs, outputs, out_specs, scratch, weigh):
+    def call(kernel, inputs, specs, outputs, out_specs, scratch, weigh, place=place):
         return pl.pallas_call(
             kernel,
             out_shape=outputs,
@@ -271,15 +278,14 @@
             grad = grad + turn(product[k], data_count - k).astype(jnp.float32)
         return grad.astype(jnp.bfloat16)
 
-    core = [swap(x, 1) for x in gathered]
-    others = [swap(x, 2) for x in gathered]
     proj, grads = None, []
     for n in range(CHUNKS):
         first, last = n == 0, n == CHUNKS - 1
         relative = n in RELATIVE
-        other = others[n]
-        ahead = (proj,) if last else (hidden_t, others[1], *gathered)
-        pieces = (gathered[n], core[n], other, swap(after(other, *ahead), 1))
+        if first:
+            pieces = firsts
+        else:
+            pieces = (gathered[n], core[n], others[n], swap(after(others[n], proj, gate_column), 1))
         if last:
             product = call(
                 functools.partial(product_kernel, relative),
@@ -288,13 +294,14 @@
             )
             hidden_grad, partial = call(
                 functools.partial(last_kernel, n * width),
-                pieces + (weight, proj, after(hidden, product), gate),
+                pieces + (weight, proj, hidden, gate_column),
                 [smem] + [held] * 7 + [vmem],
                 (
                     jax.ShapeDtypeStruct((QUADS, rows, units), jnp.bfloat16),
-                    jax.ShapeDtypeStruct((QUADS, rows, 1), jnp.float32),
+                    jax.ShapeDtypeStruct((QUADS, 8, rows), jnp.float32),
                 ),
                 (held, vmem), [full, side, total_space, quad_space, quad_space, sems], 1 << 20,
+                after(place, product),
             )
         else:
             proj, product = call(
@@ -312,7 +319,8 @@
         return x.reshape(context_count * capacity, -1)
 
     hidden_grad = canonical(hidden_grad)
-    sums = canonical(partial).reshape(context_count, 1, capacity)
+    sums = partial[:, 0].reshape(QUADS, EXPERTS, capacity).transpose(1, 0, 2)
+    sums = sums.reshape(context_count, 1, capacity)
     outgoing_sums = jnp.broadcast_to(sums, (context_count, tensor_count, capacity))
     returned = lax.all_to_all(
         outgoing_sums.reshape(context_count * tensor_count, capacity),

time: 207 us -> 172 us (0.83)
  starting transfers between devices: 73.5 us -> 50 us
  blocking collectives: 45.1 us -> 33.7 us
  waiting for transfers between devices: 13.8 us -> 22.1 us
  other arithmetic: 9.95 us -> 5.49 us
  local copies, waits for them, and re-layouts: 19.7 us -> 17 us
    ppermute x11 -> x6, starting transfers between devices: 44.1 us -> 28.8 us  [swap(): return lax.ppermute(x, 'ctx', [(c, c ^ bit) for c in range(context_count)])]
    all_gather x3 -> x2, blocking collectives: 45.1 us -> 33.7 us  [local(): gathered = [lax.all_gather(x, 'tp', axis=0, tiled=False) for x in sent]]
    ppermute x3 -> x0, starting transfers between devices: 9.79 us -> none  [turn(): lax.ppermute(x, 'dp', [(d, (d + k) % data_count) for d in range(data_coun...]
    ppermute x11 -> x6, waiting for transfers between devices: 1.43 us -> 5.49 us  [swap(): return lax.ppermute(x, 'ctx', [(c, c ^ bit) for c in range(context_count)])]
    all_to_all x1, waiting for transfers between devices: 2.7 us -> 5.82 us  [local(): lax.all_to_all(outgoing, 'ctx', split_axis=0, concat_axis=0, tiled=True,...]
    another operation x3 -> x11, local copies, waits for them, and re-layouts: 0.17 us -> 2.86 us  [the longest x8 2.69 us: local(): jnp.stack([piece[0, rows, :rows] for piece in firsts]).astype(jnp.float32)]
    reduce_scatter x2, waiting for transfers between devices: 0.01 us -> 2.52 us  [settle(): return lax.psum_scatter(product, 'dp', scatter_dimension=0, tiled=False)]
    concatenate x3 -> x0, local copies, waits for them, and re-layouts: 2.36 us -> none  [local(): gate = jnp.concatenate([pair_gate, swap(pair_gate, 2)])]
  transfers between devices with their start and end apart: 19 -> 11, of which waited for: 3 -> 6; matrix products, arithmetic and copies ran while one was open for 12% -> 11% of each run, Pallas kernels for 14% -> 15%
where the time goes in v4:
time: 172 us; the launch traced here: 171 us
  starting transfers between devices  50 us (29%)
  blocking collectives  33.7 us (20%)
  Pallas kernels  28.6 us (17%)
  waiting for transfers between devices  22.1 us (13%)
  local copies, waits for them, and re-layouts  17 us (10%)
  between operations  14.1 us (8%)
  other arithmetic  5.49 us (3%)
    all_gather x2, blocking collectives, local(): gathered = [lax.all_gather(x, 'tp', axis=0, tiled=False) for x in sent]  33.7 us
    ppermute x6, starting transfers between devices, swap(): return lax.ppermute(x, 'ctx', [(c, c ^ bit) for c in range(context_count)])  28.8 us
    pallas_call x3, Pallas kernels, call(): pl.pallas_call(kernel, out_shape=outputs, in_specs=specs, out_specs=out_s...  26.3 us
    all_to_all x1, starting transfers between devices, local(): lax.all_to_all(outgoing, 'ctx', split_axis=0, concat_axis=0, tiled=True,...  11.9 us
    all_to_all x1, starting transfers between devices, local(): lax.all_to_all(outgoing_sums.reshape(context_count * tensor_count, capaci...  9.21 us
    all_to_all x1, waiting for transfers between devices, local(): lax.all_to_all(outgoing_sums.reshape(context_count * tensor_count, capaci...  7.58 us
    all_to_all x1, waiting for transfers between devices, local(): lax.all_to_all(outgoing, 'ctx', split_axis=0, concat_axis=0, tiled=True,...  5.82 us
    ppermute x6, waiting for transfers between devices, swap(): return lax.ppermute(x, 'ctx', [(c, c ^ bit) for c in range(context_count)])  5.49 us
  transfers between devices with their start and end apart: 11, of which 6 were waited for; matrix products, arithmetic and copies ran while one was open for 11% of the time, Pallas kernels for 15%

profile of v4, /device:TPU:1, one launch (start us, length us, event | category | flops | bytes accessed | tf_op | source)
XLA Modules:
  0.0 171.1 jit_solution(18265760252906325619)
XLA Ops:
  7.2 2.3 %shard_map.76 = (bf16[320,768]{1,0:T(8,128)(2,1)}, s32[2,128]{1,0:T(2,128)}, f32[2,128]{1,0:T(2,128)}) custom-call(s32[2,128]{1,0:T(2,128)} %bitcast.72, f32[2,128]{1,0:T(2,128)} %bitcast.73, bf16[128,768]{1,0:T(8,128)(2,1)} %upstream_ref.1), custom_call_target="tpu_custom_call" | custom-call | flops 62914560 | bytes 688128 | tf_op jit(solution)/shard_map/pallas_call | solution.py:64
  9.5 11.9 %all-to-all-start = ((bf16[8,40,768]{2,1,0:T(8,128)(2,1)}), bf16[8,40,768]{2,1,0:T(8,128)(2,1)S(1)}, u32[]{:S(2)}, u32[]{:S(2)}) async-start(bf16[8,40,768]{2,1,0:T(8,128)(2,1)} %bitcast.67), calls=%async_computation | async-start | bytes 983040 | tf_op jit(solution)/shard_map/all_to_all | solution.py:210
  23.1 2.4 %constant_dynamic-slice_fusion = (bf16[1,288,512]{2,0,1:T(2,128)(2,1)S(1)}, bf16[1,288,512]{2,0,1:T(2,128)(2,1)S(1)}, bf16[1,288,512]{2,0,1:T(2,128)(2,1)S(1)}, bf16[1,288,512]{2,0,1:T(2,128)(2,1)S(1)}) fusion(bf16[4,288,512]{2,0,1:T(4,128)(2,1)S(1)} %bitcast.54, s32[]{:T(128)S(6)} %select_n.25, s32[]{:T(128)S(6)} %select_n.24, s32[]{:T(128)S(6)} %select_n.23, ...), kind=kLoop, calls=%fused_computation.20 | loop fusion | bytes 2359312 | tf_op jit(solution)/shard_map/jit(dynamic_index_in_dim)/dynamic_slice | solution.py:223
  25.7 5.8 %all-to-all-done = bf16[8,40,768]{2,1,0:T(8,128)(2,1)S(1)} async-done(((bf16[8,40,768]{2,1,0:T(8,128)(2,1)}), bf16[8,40,768]{2,1,0:T(8,128)(2,1)S(1)}, u32[]{:S(2)}, u32[]{:S(2)}) %all-to-all-start) | async-done | bytes 491552 | tf_op jit(solution)/shard_map/all_to_all | solution.py:210
  31.8 16.6 %all-gather.1 = bf16[1184,384]{1,0:T(8,128)(2,1)S(1)} all-gather(bf16[296,384]{1,0:T(8,128)(2,1)S(1)} %fusion.1), channel_id=3, replica_groups=mesh['dp'=4,'ctx'=32,'tp'=4] {'tp'}, dimensions={0}, use_global_device_ids=true | all-gather | bytes 1136640 | tf_op jit(solution)/shard_map/all_gather | solution.py:234
  48.4 11.8 %collective-permute-start = (bf16[4,296,384]{2,1,0:T(8,128)(2,1)S(1)}, bf16[4,296,384]{2,1,0:T(8,128)(2,1)}, u32[]{:S(2)}, u32[]{:S(2)}) collective-permute-start(bf16[4,296,384]{2,1,0:T(8,128)(2,1)S(1)} %bitcast.58), channel_id=1, source_target_pairs={{0,8},{4,12},{8,0},{12,4},{16,24},{20,28},{24,16},{28,20},{32,40},... | collective-permute-start | bytes 2727944 | tf_op jit(solution)/shard_map/ppermute | solution.py:217
  60.3 17.1 %all-gather = bf16[1152,384]{1,0:T(8,128)(2,1)} all-gather(bf16[288,384]{1,0:T(8,128)(2,1)S(1)} %get-tuple-element.42), channel_id=2, replica_groups=mesh['dp'=4,'ctx'=32,'tp'=4] {'tp'}, dimensions={0}, use_global_device_ids=true | all-gather | bytes 1105920 | tf_op jit(solution)/shard_map/all_gather | solution.py:234
  77.8 6.4 %collective-permute-start.4 = (bf16[4,296,384]{2,1,0:T(8,128)(2,1)}, bf16[4,296,384]{2,1,0:T(8,128)(2,1)}, u32[]{:S(2)}, u32[]{:S(2)}) collective-permute-start(bf16[4,296,384]{2,1,0:T(8,128)(2,1)} %collective-permute-done.p2), channel_id=1, source_target_pairs={{0,4},{4,0},{8,12},{12,8},{16,20},{20,16},{24,28},{28,24},{32,36},... | collective-permute-start | bytes 2727944 | tf_op jit(solution)/shard_map/ppermute | solution.py:217
  84.2 1.9 %collective-permute-start.3 = (bf16[4,296,384]{2,1,0:T(8,128)(2,1)S(1)}, bf16[4,296,384]{2,1,0:T(8,128)(2,1)}, u32[]{:S(2)}, u32[]{:S(2)}) collective-permute-start(bf16[4,296,384]{2,1,0:T(8,128)(2,1)S(1)} %bitcast.59), channel_id=1, source_target_pairs={{0,4},{4,0},{8,12},{12,8},{16,20},{20,16},{24,28},{28,24},{32,36},... | collective-permute-start | bytes 2727944 | tf_op jit(solution)/shard_map/ppermute | solution.py:217
  86.1 0.7 copy.45
  87.5 2.6 %collective-permute-start.2 = (bf16[4,288,384]{2,1,0:T(8,128)(2,1)}, bf16[4,288,384]{2,1,0:T(8,128)(2,1)}, u32[]{:S(2)}, u32[]{:S(2)}) collective-permute-start(bf16[4,288,384]{2,1,0:T(8,128)(2,1)} %bitcast.62), channel_id=1, source_target_pairs={{0,8},{4,12},{8,0},{12,4},{16,24},{20,28},{24,16},{28,20},{32,40},... | collective-permute-start | bytes 2654216 | tf_op jit(solution)/shard_map/ppermute | solution.py:217
  90.1 0.7 slice_bitcast_fusion.2
  90.8 0.7 slice_bitcast_fusion
  92.3 1.2 multiply_convert_fusion.hidden_t_ref.before_ref
  93.5 8.7 %shard_map.77 = (f32[1152,512]{1,0:T(8,128)}, bf16[4,512,384]{2,1,0:T(8,128)(2,1)}) custom-call(s32[2]{0:T(128)} %pad_add_fusion.place_ref, bf16[4,296,384]{2,1,0:T(8,128)(2,1)} %bitcast.61, bf16[4,296,384]{2,1,0:T(8,128)(2,1)} %collective-permute-done.3.p1, bf16[4,296,384]{2,1,0:T(8,128)(2,1)} %collective-permute-done.p2, ...), custom_call_target="tpu_custom_call" | custom-call | flops 1048576 | bytes 1048576 | tf_op jit(solution)/shard_map/pallas_call | solution.py:258
  102.6 0.8 copy-done.2
  103.4 2.7 %collective-permute-start.1 = (bf16[4,288,384]{2,1,0:T(8,128)(2,1)S(1)}, bf16[4,288,384]{2,1,0:T(8,128)(2,1)S(1)}, u32[]{:S(2)}, u32[]{:S(2)}) collective-permute-start(bf16[4,288,384]{2,1,0:T(8,128)(2,1)S(1)} %bitcast.65), channel_id=1, source_target_pairs={{0,4},{4,0},{8,12},{12,8},{16,20},{20,16},{24,28},{28,24},{32,36},... | collective-permute-start | bytes 2654216 | tf_op jit(solution)/shard_map/ppermute | solution.py:217
  106.4 0.9 maximum_convert_fusion.gate_ref
  107.3 3.1 %collective-permute-done.2.p2 = bf16[4,288,384]{2,1,0:T(8,128)(2,1)} collective-permute-done((bf16[4,288,384]{2,1,0:T(8,128)(2,1)}, bf16[4,288,384]{2,1,0:T(8,128)(2,1)}, u32[]{:S(2)}, u32[]{:S(2)}) %collective-permute-start.2) | collective-permute-done | bytes 884768 | tf_op jit(solution)/shard_map/ppermute | solution.py:217
  110.4 3.4 %collective-permute-start.5 = (bf16[4,288,384]{2,1,0:T(8,128)(2,1)}, bf16[4,288,384]{2,1,0:T(8,128)(2,1)S(1)}, u32[]{:S(2)}, u32[]{:S(2)}) collective-permute-start(bf16[4,288,384]{2,1,0:T(8,128)(2,1)} %collective-permute-done.2.p2), channel_id=1, source_target_pairs={{0,4},{4,0},{8,12},{12,8},{16,20},{20,16},{24,28},{28,24},{32,36},... | collective-permute-start | bytes 2654216 | tf_op jit(solution)/shard_map/ppermute | solution.py:217
  113.8 2.0 %collective-permute-done.5.p3 = bf16[4,288,384]{2,1,0:T(8,128)(2,1)S(1)} collective-permute-done((bf16[4,288,384]{2,1,0:T(8,128)(2,1)}, bf16[4,288,384]{2,1,0:T(8,128)(2,1)S(1)}, u32[]{:S(2)}, u32[]{:S(2)}) %collective-permute-start.5) | collective-permute-done | bytes 884768 | tf_op jit(solution)/shard_map/ppermute | solution.py:217
  115.9 0.9 copy-done.5
  116.8 6.8 %shard_map.78 = bf16[4,512,384]{2,1,0:T(8,128)(2,1)} custom-call(s32[2]{0:T(128)} %pad_add_fusion.place_ref, bf16[4,288,384]{2,1,0:T(8,128)(2,1)} %bitcast.63, bf16[4,288,384]{2,1,0:T(8,128)(2,1)} %copy-done.4, bf16[4,288,384]{2,1,0:T(8,128)(2,1)} %collective-permute-done.2.p2, bf16[4,288,384]{2,1,0:T(8,128)(2,1)} %copy-done.5, ...), custom_call_target="tpu_custom_call" | custom-call | flops 17999998976 | bytes 1048576 | tf_op jit(solution)/shard_map/pallas_call | solution.py:258
  124.3 10.8 %shard_map.79 = (bf16[4,288,512]{2,1,0:T(8,128)(2,1)}, f32[4,8,288]{2,1,0:T(8,128)}) custom-call(s32[2]{0:T(128)} %pad_add_fusion.place_ref, bf16[4,288,384]{2,1,0:T(8,128)(2,1)} %bitcast.64, bf16[4,288,384]{2,1,0:T(8,128)(2,1)} %copy-done.4, bf16[4,288,384]{2,1,0:T(8,128)(2,1)} %collective-permute-done.2.p2, bf16[4,288,384]{2,1,0:T(8,128)(2,1)} %copy-done.5, ...), custom_call_target="tpu_custom_call" | custom-call | flops 1048576 | bytes 1048576 | tf_op jit(solution)/shard_map/pallas_call | solution.py:258
  135.1 0.8 slice_reduce_fusion
  136.7 9.2 %all-to-all-start.1 = ((f32[128,1,36]{2,1,0:T(1,128)}), f32[128,1,36]{2,1,0:T(1,128)S(1)}, u32[]{:S(2)}, u32[]{:S(2)}) async-start(f32[128,1,36]{2,1,0:T(1,128)} %bitcast.26), calls=%async_computation.3 | async-start | bytes 131072 | tf_op jit(solution)/shard_map/all_to_all | solution.py:325
  145.9 2.4 %copy.50 = bf16[4,288,512]{2,0,1:T(4,128)(2,1)S(1)} copy(bf16[4,288,512]{2,1,0:T(8,128)(2,1)} %get-tuple-element.24) | data formatting | bytes 2359296 | tf_op jit(solution)/shard_map/pallas_call | solution.py:258
  148.6 1.1 reshape.119
  149.7 7.6 %all-to-all-done.1 = f32[128,1,36]{2,1,0:T(1,128)S(1)} async-done(((f32[128,1,36]{2,1,0:T(1,128)}), f32[128,1,36]{2,1,0:T(1,128)S(1)}, u32[]{:S(2)}, u32[]{:S(2)}) %all-to-all-start.1) | async-done | bytes 18464 | tf_op jit(solution)/shard_map/all_to_all | solution.py:325
  157.4 1.9 %gather_fusion = f32[256]{0:T(256)S(1)} fusion(f32[288]{0:T(512)S(1)} %reshape.121, s32[1024]{0:T(1024)S(1)} %pad_clamp_fusion), kind=kCustom, calls=%fused_computation | custom fusion | bytes 3072 | tf_op jit(solution)/shard_map/jit(_take)/gather | solution.py:330
  160.0 2.5 %reduce-scatter.5.cloned.1.call-done = bf16[1,512,384]{2,1,0:T(8,128)(2,1)} async-done(((bf16[4,512,384]{2,1,0:T(8,128)(2,1)}), bf16[1,512,384]{2,1,0:T(8,128)(2,1)}) %reduce-scatter.5.cloned.1.call-update) | async-done | bytes 393232 | tf_op jit(solution)/shard_map/reduce_scatter | solution.py:275
  162.5 2.1 %pad_maximum_fusion = bf16[512,768]{1,0:T(8,128)(2,1)} fusion(bf16[512,384]{1,0:T(8,128)(2,1)} %bitcast.69, bf16[512,384]{1,0:T(8,128)(2,1)} %bitcast.68), kind=kLoop, calls=%fused_computation.2 | loop fusion | flops 1572864 | bytes 1572864 | tf_op jit(solution)/shard_map/concatenate | solution.py:315
  (56 shorter events, 6.9 us)
Async XLA Ops:
  7.2 15.0 %copy-start.3 = (bf16[1152,512]{1,0:T(8,128)(2,1)S(1)}, bf16[1152,512]{1,0:T(8,128)(2,1)}, u32[]{:S(2)}) copy-start(bf16[1152,512]{1,0:T(8,128)(2,1)} %param.8) | copy-start | bytes 3538948
  9.5 22.1 %all-to-all-start = ((bf16[8,40,768]{2,1,0:T(8,128)(2,1)}), bf16[8,40,768]{2,1,0:T(8,128)(2,1)S(1)}, u32[]{:S(2)}, u32[]{:S(2)}) async-start(bf16[8,40,768]{2,1,0:T(8,128)(2,1)} %bitcast.67), calls=%async_computation | async-start | bytes 983040 | tf_op jit(solution)/shard_map/all_to_all | solution.py:210
  21.3 72.2 %all-gather.5.cloned.1.call-start = ((), (), s32[]{:S(2)}) async-start(), calls=%async_computation.6 | async-start | bytes 3932160 | tf_op jit(solution)/shard_map/all_gather | solution.py:229
  22.1 137.9 %reduce-scatter.3.cloned.1.call-start = ((), (), s32[]{:S(2)}) async-start(), calls=%async_computation.4 | async-start | bytes 1966080 | tf_op jit(solution)/shard_map/reduce_scatter | solution.py:275
  25.7 60.4 %copy-start = (bf16[4,288,512]{2,1,0:T(8,128)(2,1)}, bf16[4,288,512]{2,1,0:T(8,128)(2,1)S(1)}, u32[]{:S(2)}) copy-start(bf16[4,288,512]{2,1,0:T(8,128)(2,1)S(1)} %copy_dynamic-update-slice_fusion.hidden_ref) | copy-start | bytes 3538948
  48.4 41.6 %copy-start.1 = (bf16[1184,384]{1,0:T(8,128)(2,1)}, bf16[1184,384]{1,0:T(8,128)(2,1)S(1)}, u32[]{:S(2)}) copy-start(bf16[1184,384]{1,0:T(8,128)(2,1)S(1)} %all-gather.1) | copy-start | bytes 2727940
  48.4 29.3 %collective-permute-start = (bf16[4,296,384]{2,1,0:T(8,128)(2,1)S(1)}, bf16[4,296,384]{2,1,0:T(8,128)(2,1)}, u32[]{:S(2)}, u32[]{:S(2)}) collective-permute-start(bf16[4,296,384]{2,1,0:T(8,128)(2,1)S(1)} %bitcast.58), channel_id=1, source_target_pairs={{0,8},{4,12},{8,0},{12,4},{16,24},{20,28},{24,16},{28,20},{32,40},... | collective-permute-start | bytes 2727944 | tf_op jit(solution)/shard_map/ppermute | solution.py:217
  77.8 13.0 %collective-permute-start.4 = (bf16[4,296,384]{2,1,0:T(8,128)(2,1)}, bf16[4,296,384]{2,1,0:T(8,128)(2,1)}, u32[]{:S(2)}, u32[]{:S(2)}) collective-permute-start(bf16[4,296,384]{2,1,0:T(8,128)(2,1)} %collective-permute-done.p2), channel_id=1, source_target_pairs={{0,4},{4,0},{8,12},{12,8},{16,20},{20,16},{24,28},{28,24},{32,36},... | collective-permute-start | bytes 2727944 | tf_op jit(solution)/shard_map/ppermute | solution.py:217
  84.2 7.3 %collective-permute-start.3 = (bf16[4,296,384]{2,1,0:T(8,128)(2,1)S(1)}, bf16[4,296,384]{2,1,0:T(8,128)(2,1)}, u32[]{:S(2)}, u32[]{:S(2)}) collective-permute-start(bf16[4,296,384]{2,1,0:T(8,128)(2,1)S(1)} %bitcast.59), channel_id=1, source_target_pairs={{0,4},{4,0},{8,12},{12,8},{16,20},{20,16},{24,28},{28,24},{32,36},... | collective-permute-start | bytes 2727944 | tf_op jit(solution)/shard_map/ppermute | solution.py:217
  87.5 22.9 %collective-permute-start.2 = (bf16[4,288,384]{2,1,0:T(8,128)(2,1)}, bf16[4,288,384]{2,1,0:T(8,128)(2,1)}, u32[]{:S(2)}, u32[]{:S(2)}) collective-permute-start(bf16[4,288,384]{2,1,0:T(8,128)(2,1)} %bitcast.62), channel_id=1, source_target_pairs={{0,8},{4,12},{8,0},{12,4},{16,24},{20,28},{24,16},{28,20},{32,40},... | collective-permute-start | bytes 2654216 | tf_op jit(solution)/shard_map/ppermute | solution.py:217
  102.2 1.2 copy-start.2
  102.3 60.2 %reduce-scatter.5.cloned.1.call-start = ((), (), s32[]{:S(2)}) async-start(), calls=%async_computation.5 | async-start | bytes 1966080 | tf_op jit(solution)/shard_map/reduce_scatter | solution.py:275
  103.4 10.4 %collective-permute-start.1 = (bf16[4,288,384]{2,1,0:T(8,128)(2,1)S(1)}, bf16[4,288,384]{2,1,0:T(8,128)(2,1)S(1)}, u32[]{:S(2)}, u32[]{:S(2)}) collective-permute-start(bf16[4,288,384]{2,1,0:T(8,128)(2,1)S(1)} %bitcast.65), channel_id=1, source_target_pairs={{0,4},{4,0},{8,12},{12,8},{16,20},{20,16},{24,28},{28,24},{32,36},... | collective-permute-start | bytes 2654216 | tf_op jit(solution)/shard_map/ppermute | solution.py:217
  110.4 5.5 %collective-permute-start.5 = (bf16[4,288,384]{2,1,0:T(8,128)(2,1)}, bf16[4,288,384]{2,1,0:T(8,128)(2,1)S(1)}, u32[]{:S(2)}, u32[]{:S(2)}) collective-permute-start(bf16[4,288,384]{2,1,0:T(8,128)(2,1)} %collective-permute-done.2.p2), channel_id=1, source_target_pairs={{0,4},{4,0},{8,12},{12,8},{16,20},{20,16},{24,28},{28,24},{32,36},... | collective-permute-start | bytes 2654216 | tf_op jit(solution)/shard_map/ppermute | solution.py:217
  113.8 2.1 %copy-start.4 = (bf16[4,288,384]{2,1,0:T(8,128)(2,1)}, bf16[4,288,384]{2,1,0:T(8,128)(2,1)S(1)}, u32[]{:S(2)}) copy-start(bf16[4,288,384]{2,1,0:T(8,128)(2,1)S(1)} %collective-permute-done.1.p1) | copy-start | bytes 2654212
  115.9 0.9 copy-start.5
  123.6 0.7 copy-start.6
  136.7 20.6 %all-to-all-start.1 = ((f32[128,1,36]{2,1,0:T(1,128)}), f32[128,1,36]{2,1,0:T(1,128)S(1)}, u32[]{:S(2)}, u32[]{:S(2)}) async-start(f32[128,1,36]{2,1,0:T(1,128)} %bitcast.26), calls=%async_computation.3 | async-start | bytes 131072 | tf_op jit(solution)/shard_map/all_to_all | solution.py:325
  148.6 10.8 %copy-start.7 = (f32[2,128]{1,0:T(2,128)S(1)}, f32[2,128]{1,0:T(2,128)}, u32[]{:S(2)}) copy-start(f32[2,128]{1,0:T(2,128)} %get-tuple-element.26) | copy-start | bytes 3076
Sparse Core Ops, SparseCore 0:
  24.3 45.7 all-gather.4
  102.4 26.3 reduce-scatter.2
  131.6 30.7 reduce-scatter.4

commit v5 on v4

--- a/solution.py
+++ b/solution.py
@@ -12,8 +12,7 @@
 QUADS = 4
 VMEM_LIMIT = 56 * 1024 * 1024
 CHUNKS = 2
-RELATIVE = ()
-WEIGH = (1 << 20, 18 * 10**9)
+WEIGH = (1 << 20, 1 << 20, 18 * 10**9)
 
 
 def compare_dot(a, b):
@@ -90,101 +89,116 @@
     return [slice(i * size, (i + 1) * size) for i in range(count)]
 
 
-def load_pieces(copy, pieces, full):
-    rows, blocks = full.shape[0] // QUADS, pieces[0].shape[0]
-    width = full.shape[1] // blocks
-    return [
-        [
-            copy(pieces[i].at[j, 0:rows, :], full.at[at, column])
-            for j, column in enumerate(spans(width, blocks))
-        ]
-        for i, at in enumerate(spans(rows, QUADS))
-    ]
-
-
 def wait(copies):
     for made in copies:
         made.wait()
 
 
-def write_product(copy, relative, place_ref, hidden_t, full, product, product_ref):
-    blocks, _, width = product.shape
-    stores = []
-    for j, column in enumerate(spans(width, blocks)):
-        result = jnp.dot(hidden_t[...], full[:, column], preferred_element_type=jnp.float32)
-        product[j] = result.astype(jnp.bfloat16)
-        place = lax.rem(place_ref[1] + blocks - j, blocks) if relative else j
-        stores.append(copy(product.at[j], product_ref.at[place]))
-    return stores
-
-
-def both_kernel(
-    start, first, relative, place_ref, p0, p1, p2, p3, weight_ref, hidden_t_ref, before_ref,
-    proj_ref, product_ref, full, side, hidden_t, total, product, sems,
-):
-    copy = Copies(sems)
-    blocks, _, width = product.shape
-    rows = total.shape[0] // QUADS
-    sides = [
+def load_rows(copy, pieces, full):
+    rows, blocks = full.shape[0] // len(pieces), pieces[0].shape[0]
+    columns = spans(full.shape[1] // blocks, blocks)
+    return [
+        [copy(piece.at[j, 0:rows, :], full.at[at, column]) for j, column in enumerate(columns)]
+        for piece, at in zip(pieces, spans(rows, len(pieces)))
+    ]
+
+
+def load_weight(copy, weight_ref, start, side):
+    blocks = weight_ref.shape[0]
+    width = side.shape[1] // blocks
+    return [
         copy(weight_ref.at[j, :, start : start + width], side.at[:, column])
         for j, column in enumerate(spans(width, blocks))
     ]
-    loads = load_pieces(copy, (p0, p1, p2, p3), full)
-    if not first:
-        for i, at in enumerate(spans(rows, QUADS)):
-            loads[i].append(copy(before_ref.at[at, :], total.at[at, :]))
-    hidden_t_load = copy(hidden_t_ref, hidden_t)
+
+
+def product_kernel(p0, p1, p2, p3, hidden_t_ref, product_ref, full, hidden_t, product, sems):
+    copy = Copies(sems)
+    blocks, _, width = product.shape
+    rows = full.shape[0] // QUADS
+    columns = spans(width, blocks)
+    first = [copy(hidden_t_ref, hidden_t)]
+    loads = [
+        [
+            copy(piece.at[j, 0:rows, :], full.at[at, column])
+            for piece, at in zip((p0, p1, p2, p3), spans(rows, QUADS))
+        ]
+        for j, column in enumerate(columns)
+    ]
+    wait(first)
+    stores = []
+    for j, column in enumerate(columns):
+        wait(loads[j])
+        result = jnp.dot(hidden_t[...], full[:, column], preferred_element_type=jnp.float32)
+        product[j] = result.astype(jnp.bfloat16)
+        stores.append(copy(product.at[j], product_ref.at[j]))
+    wait(stores)
+
+
+def row_sums(x):
+    lanes = 128
+    folded = sum(x[:, at] for at in spans(lanes, x.shape[1] // lanes))
+    return lax.dot_general(
+        jnp.ones((8, lanes), jnp.float32), folded, (((1,), (1,)), ((), ())),
+        precision=lax.Precision.HIGHEST, preferred_element_type=jnp.float32,
+    )
+
+
+def early_kernel(
+    place_ref, p0, p1, p2, p3, n0, n1, weight_ref, hidden_ref, gate_ref,
+    before_ref, grad_ref, partial_ref,
+    full, side, next_full, next_side, total, hidden, grad, sems,
+):
+    copy = Copies(sems)
+    rows = total.shape[0] // 2
+    width = full.shape[1] // weight_ref.shape[0]
+    sides = load_weight(copy, weight_ref, 0, side)
+    loads = load_rows(copy, (p0, p1, p2, p3), full)
+    sides_next = load_weight(copy, weight_ref, width, next_side)
+    for i, made in enumerate(load_rows(copy, (n0, n1), next_full)):
+        loads[i] += made + [copy(hidden_ref.at[i], hidden.at[i])]
     stores = []
     wait(sides)
-    for i, at in enumerate(spans(rows, QUADS)):
+    for i in (2, 3):
         wait(loads[i])
+        at, to = slice(i * rows, (i + 1) * rows), slice((i - 2) * rows, (i - 1) * rows)
+        total[to, :] = compare_dot(full[at, :], side[...])
+        stores.append(copy(total.at[to, :], before_ref.at[to, :]))
+    wait(sides_next)
+    partial_ref[...] = jnp.zeros(partial_ref.shape, jnp.float32)
+    for i in (0, 1):
+        wait(loads[i])
+        at = slice(i * rows, (i + 1) * rows)
         proj = compare_dot(full[at, :], side[...])
-        total[at, :] = proj if first else total[at, :] + proj
-        stores.append(copy(total.at[at, :], proj_ref.at[at, :]))
-    hidden_t_load.wait()
-    stores += write_product(copy, relative, place_ref, hidden_t, full, product, product_ref)
+        proj = proj + compare_dot(next_full[at, :], next_side[...])
+        owner = jnp.bitwise_xor(place_ref[0], i)
+        partial_ref[owner] = row_sums(hidden[i].astype(jnp.float32) * proj)
+        grad[i] = (gate_ref[i] * proj).astype(jnp.bfloat16)
+        stores.append(copy(grad.at[i], grad_ref.at[owner]))
     wait(stores)
 
 
-def product_kernel(
-    relative, place_ref, p0, p1, p2, p3, hidden_t_ref, product_ref, full, hidden_t, product, sems
-):
-    copy = Copies(sems)
-    hidden_t_load = copy(hidden_t_ref, hidden_t)
-    for loads in load_pieces(copy, (p0, p1, p2, p3), full):
-        wait(loads)
-    hidden_t_load.wait()
-    wait(write_product(copy, relative, place_ref, hidden_t, full, product, product_ref))
-
-
-def last_kernel(
-    start, place_ref, p0, p1, p2, p3, weight_ref, before_ref, hidden_ref, gate_ref,
+def late_kernel(
+    place_ref, p2, p3, weight_ref, before_ref, hidden_ref, gate_ref, early_partial_ref, early_grad,
     grad_ref, partial_ref, full, side, total, hidden, grad, sems,
 ):
     copy = Copies(sems)
-    blocks = p0.shape[0]
-    width = full.shape[1] // blocks
-    rows = total.shape[0] // QUADS
-    sides = [
-        copy(weight_ref.at[j, :, start : start + width], side.at[:, column])
-        for j, column in enumerate(spans(width, blocks))
-    ]
-    loads = load_pieces(copy, (p0, p1, p2, p3), full)
-    for i, at in enumerate(spans(rows, QUADS)):
+    rows = total.shape[0] // 2
+    width = full.shape[1] // weight_ref.shape[0]
+    sides = load_weight(copy, weight_ref, width, side)
+    loads = load_rows(copy, (p2, p3), full)
+    for i, at in enumerate(spans(rows, 2)):
         loads[i].append(copy(before_ref.at[at, :], total.at[at, :]))
-        loads[i].append(copy(hidden_ref.at[i], hidden.at[i]))
-    ones = jnp.ones((8, hidden.shape[2]), jnp.float32)
+        loads[i].append(copy(hidden_ref.at[i + 2], hidden.at[i]))
+    partial_ref[...] = early_partial_ref[...]
     wait(sides)
     stores = []
-    for i, at in enumerate(spans(rows, QUADS)):
+    for i, at in enumerate(spans(rows, 2)):
         wait(loads[i])
         proj = total[at, :] + compare_dot(full[at, :], side[...])
-        owner = jnp.bitwise_xor(place_ref[0], i)
-        partial_ref[owner] = lax.dot_general(
-            ones, hidden[i].astype(jnp.float32) * proj, (((1,), (1,)), ((), ())),
-            precision=lax.Precision.HIGHEST, preferred_element_type=jnp.float32,
-        )
-        grad[i] = (gate_ref[i] * proj).astype(jnp.bfloat16)
+        owner = jnp.bitwise_xor(place_ref[0], i + 2)
+        partial_ref[owner] = row_sums(hidden[i].astype(jnp.float32) * proj)
+        grad[i] = (gate_ref[i + 2] * proj).astype(jnp.bfloat16)
         stores.append(copy(grad.at[i], grad_ref.at[owner]))
     wait(stores)
 
@@ -241,77 +255,64 @@
     hidden_t = (hidden_turned.astype(jnp.float32) * gate.reshape(1, total)).astype(jnp.bfloat16)
     gate_column = gate[:, :, None]
 
-    place = jnp.stack([quad, lax.axis_index("dp")]).astype(jnp.int32)
+    place = quad.astype(jnp.int32).reshape(1)
+    blocks = data_count
     held = pl.BlockSpec(memory_space=pl.ANY)
     vmem = pl.BlockSpec(memory_space=pltpu.VMEM)
     smem = pl.BlockSpec(memory_space=pltpu.SMEM)
-    product_shape = jax.ShapeDtypeStruct((data_count, units, width), jnp.bfloat16)
-    full = pltpu.VMEM((total, data_count * width), jnp.bfloat16)
-    side = pltpu.VMEM((units, data_count * width), jnp.bfloat16)
-    hidden_t_space = pltpu.VMEM((units, total), jnp.bfloat16)
-    total_space = pltpu.VMEM((total, units), jnp.float32)
-    product_space = pltpu.VMEM((data_count, units, width), jnp.bfloat16)
-    quad_space = pltpu.VMEM((QUADS, rows, units), jnp.bfloat16)
-    sems = pltpu.SemaphoreType.DMA((data_count * (QUADS + 2) + 3 * QUADS + 1,))
-
-    def call(kernel, inputs, specs, outputs, out_specs, scratch, weigh, place=place):
+
+    def space(*shape, dtype=jnp.bfloat16):
+        return pltpu.VMEM(shape, dtype)
+
+    def call(kernel, outputs, out_specs, scratch, copies, weigh, specs, inputs, aliases={}):
         return pl.pallas_call(
             kernel,
             out_shape=outputs,
             in_specs=specs,
             out_specs=out_specs,
-            scratch_shapes=scratch,
+            scratch_shapes=scratch + [pltpu.SemaphoreType.DMA((copies,))],
+            input_output_aliases=aliases,
             compiler_params=pltpu.CompilerParams(vmem_limit_bytes=VMEM_LIMIT),
             cost_estimate=pl.CostEstimate(
                 flops=weigh, bytes_accessed=1 << 20, transcendentals=0
             ),
-        )(place, *inputs)
-
-    def turn(x, k):
-        return lax.ppermute(x, "dp", [(d, (d + k) % data_count) for d in range(data_count)])
-
-    def settle(relative, product):
-        if not relative:
-            return lax.psum_scatter(product, "dp", scatter_dimension=0, tiled=False)
-        grad = product[0].astype(jnp.float32)
-        for k in (2, 1, 3):
-            grad = grad + turn(product[k], data_count - k).astype(jnp.float32)
-        return grad.astype(jnp.bfloat16)
-
-    proj, grads = None, []
-    for n in range(CHUNKS):
-        first, last = n == 0, n == CHUNKS - 1
-        relative = n in RELATIVE
-        if first:
-            pieces = firsts
-        else:
-            pieces = (gathered[n], core[n], others[n], swap(after(others[n], proj, gate_column), 1))
-        if last:
-            product = call(
-                functools.partial(product_kernel, relative),
-                pieces + (hidden_t,), [smem] + [held] * 5, product_shape, held,
-                [full, hidden_t_space, product_space, sems], WEIGH[n],
-            )
-            hidden_grad, partial = call(
-                functools.partial(last_kernel, n * width),
-                pieces + (weight, proj, hidden, gate_column),
-                [smem] + [held] * 7 + [vmem],
-                (
-                    jax.ShapeDtypeStruct((QUADS, rows, units), jnp.bfloat16),
-                    jax.ShapeDtypeStruct((QUADS, 8, rows), jnp.float32),
-                ),
-                (held, vmem), [full, side, total_space, quad_space, quad_space, sems], 1 << 20,
-                after(place, product),
-            )
-        else:
-            proj, product = call(
-                functools.partial(both_kernel, n * width, first, relative),
-                pieces + (weight, hidden_t, hidden_t if first else proj),
-                [smem] + [held] * 7,
-                (jax.ShapeDtypeStruct((total, units), jnp.float32), product_shape), (held, held),
-                [full, side, hidden_t_space, total_space, product_space, sems], WEIGH[n],
-            )
-        grads.append(settle(relative, product))
+        )(*inputs)
+
+    def product_of(pieces, weigh):
+        return call(
+            product_kernel, jax.ShapeDtypeStruct((blocks, units, width), jnp.bfloat16), held,
+            [space(total, blocks * width), space(units, total), space(blocks, units, width)],
+            1 + blocks * (QUADS + 1), weigh, [held] * 5, (*pieces, hidden_t),
+        )
+
+    def settle(product):
+        return lax.psum_scatter(product, "dp", scatter_dimension=0, tiled=False)
+
+    grad_shape = jax.ShapeDtypeStruct((QUADS, rows, units), jnp.bfloat16)
+    partial_shape = jax.ShapeDtypeStruct((QUADS, 8, rows), jnp.float32)
+    half = total // 2
+    half_spaces = [
+        space(half, blocks * width), space(units, blocks * width),
+        space(half, units, dtype=jnp.float32), space(2, rows, units), space(2, rows, units),
+    ]
+
+    product = product_of(firsts, WEIGH[0])
+    grads = [settle(product)]
+    before, early_grad, early_partial = call(
+        early_kernel, (jax.ShapeDtypeStruct((half, units), jnp.float32), grad_shape, partial_shape),
+        (held, held, vmem), [space(total, blocks * width), space(units, blocks * width)] + half_spaces,
+        blocks * 8 + 6, WEIGH[1], [smem] + [held] * 8 + [vmem],
+        (after(place, product), *firsts, gathered[1], core[1], weight, hidden, gate_column),
+    )
+    lasts = (others[1], swap(after(others[1], before, gate_column), 1))
+    product = product_of((gathered[1], core[1], *lasts), WEIGH[2])
+    grads.append(settle(product))
+    hidden_grad, partial = call(
+        late_kernel, (grad_shape, partial_shape), (held, vmem), half_spaces, blocks * 3 + 6,
+        1 << 20, [smem] + [held] * 5 + [vmem, vmem, held],
+        (after(place, product), *lasts, weight, before, hidden, gate_column, early_partial, early_grad),
+        {8: 0},
+    )
     down_grad = jnp.concatenate(grads, axis=1)
 
     def canonical(x):

time: 172 us -> 171 us (level)
  waiting for transfers between devices: 22.1 us -> 23.9 us
    reduce_scatter x2, waiting for transfers between devices: 2.52 us -> 7.11 us  [settle(): return lax.psum_scatter(product, 'dp', scatter_dimension=0, tiled=False)]
    ppermute x6, waiting for transfers between devices: 5.49 us -> 2.5 us  [swap(): return lax.ppermute(x, 'ctx', [(c, c ^ bit) for c in range(context_count)])]
    pallas_call x3 -> x4, Pallas kernels: 26.3 us -> 26.8 us  [call(): pl.pallas_call(kernel, out_shape=outputs, in_specs=specs, out_specs=out_s...]
  transfers between devices with their start and end apart: 11 -> 11, of which waited for: 6 -> 5; matrix products, arithmetic and copies ran while one was open for 11% -> 10% of each run, Pallas kernels for 15% -> 16%
where the time goes in v5:
time: 171 us; the launch traced here: 170 us
  starting transfers between devices  48.4 us (28%)
  blocking collectives  33.6 us (20%)
  Pallas kernels  29.1 us (17%)
  waiting for transfers between devices  23.9 us (14%)
  local copies, waits for them, and re-layouts  16 us (9%)
  between operations  14.1 us (8%)
  other arithmetic  4.91 us (3%)
    all_gather x2, blocking collectives, local(): gathered = [lax.all_gather(x, 'tp', axis=0, tiled=False) for x in sent]  33.6 us
    ppermute x6, starting transfers between devices, swap(): return lax.ppermute(x, 'ctx', [(c, c ^ bit) for c in range(context_count)])  27.8 us
    pallas_call x4, Pallas kernels, call(): pl.pallas_call(kernel, out_shape=outputs, in_specs=specs, out_specs=out_s...  26.8 us
    all_to_all x1, starting transfers between devices, local(): lax.all_to_all(outgoing, 'ctx', split_axis=0, concat_axis=0, tiled=True,...  11.9 us
    all_to_all x1, starting transfers between devices, local(): lax.all_to_all(outgoing_sums.reshape(context_count * tensor_count, capaci...  8.69 us
    all_to_all x1, waiting for transfers between devices, local(): lax.all_to_all(outgoing_sums.reshape(context_count * tensor_count, capaci...  7.79 us
    reduce_scatter x2, waiting for transfers between devices, settle(): return lax.psum_scatter(product, 'dp', scatter_dimension=0, tiled=False)  7.11 us
    all_to_all x1, waiting for transfers between devices, local(): lax.all_to_all(outgoing, 'ctx', split_axis=0, concat_axis=0, tiled=True,...  5.82 us
  transfers between devices with their start and end apart: 11, of which 5 were waited for; matrix products, arithmetic and copies ran while one was open for 10% of the time, Pallas kernels for 16%

profile of v5, /device:TPU:1, one launch (start us, length us, event | category | flops | bytes accessed | tf_op | source)
XLA Modules:
  0.0 170.1 jit_solution(4451873092568891796)
XLA Ops:
  7.2 2.3 %shard_map.76 = (bf16[320,768]{1,0:T(8,128)(2,1)}, s32[2,128]{1,0:T(2,128)}, f32[2,128]{1,0:T(2,128)}) custom-call(s32[2,128]{1,0:T(2,128)} %bitcast.72, f32[2,128]{1,0:T(2,128)} %bitcast.73, bf16[128,768]{1,0:T(8,128)(2,1)} %upstream_ref.1), custom_call_target="tpu_custom_call" | custom-call | flops 62914560 | bytes 688128 | tf_op jit(solution)/shard_map/pallas_call | solution.py:63
  9.5 11.9 %all-to-all-start = ((bf16[8,40,768]{2,1,0:T(8,128)(2,1)}), bf16[8,40,768]{2,1,0:T(8,128)(2,1)S(1)}, u32[]{:S(2)}, u32[]{:S(2)}) async-start(bf16[8,40,768]{2,1,0:T(8,128)(2,1)} %bitcast.67), calls=%async_computation | async-start | bytes 983040 | tf_op jit(solution)/shard_map/all_to_all | solution.py:224
  23.1 2.4 %constant_dynamic-slice_fusion = (bf16[1,288,512]{2,0,1:T(2,128)(2,1)S(1)}, bf16[1,288,512]{2,0,1:T(2,128)(2,1)S(1)}, bf16[1,288,512]{2,0,1:T(2,128)(2,1)S(1)}, bf16[1,288,512]{2,0,1:T(2,128)(2,1)S(1)}) fusion(bf16[4,288,512]{2,0,1:T(4,128)(2,1)S(1)} %bitcast.54, s32[]{:T(128)S(6)} %select_n.25, s32[]{:T(128)S(6)} %select_n.24, s32[]{:T(128)S(6)} %select_n.23, ...), kind=kLoop, calls=%fused_computation.20 | loop fusion | bytes 2359312 | tf_op jit(solution)/shard_map/jit(dynamic_index_in_dim)/dynamic_slice | solution.py:237
  25.7 5.8 %all-to-all-done = bf16[8,40,768]{2,1,0:T(8,128)(2,1)S(1)} async-done(((bf16[8,40,768]{2,1,0:T(8,128)(2,1)}), bf16[8,40,768]{2,1,0:T(8,128)(2,1)S(1)}, u32[]{:S(2)}, u32[]{:S(2)}) %all-to-all-start) | async-done | bytes 491552 | tf_op jit(solution)/shard_map/all_to_all | solution.py:224
  31.8 16.7 %all-gather.1 = bf16[1184,384]{1,0:T(8,128)(2,1)S(1)} all-gather(bf16[296,384]{1,0:T(8,128)(2,1)S(1)} %fusion.1), channel_id=3, replica_groups=mesh['dp'=4,'ctx'=32,'tp'=4] {'tp'}, dimensions={0}, use_global_device_ids=true | all-gather | bytes 1136640 | tf_op jit(solution)/shard_map/all_gather | solution.py:248
  48.5 11.8 %collective-permute-start = (bf16[4,296,384]{2,1,0:T(8,128)(2,1)S(1)}, bf16[4,296,384]{2,1,0:T(8,128)(2,1)}, u32[]{:S(2)}, u32[]{:S(2)}) collective-permute-start(bf16[4,296,384]{2,1,0:T(8,128)(2,1)S(1)} %bitcast.55), channel_id=1, source_target_pairs={{0,8},{4,12},{8,0},{12,4},{16,24},{20,28},{24,16},{28,20},{32,40},... | collective-permute-start | bytes 2727944 | tf_op jit(solution)/shard_map/ppermute | solution.py:231
  60.3 17.0 %all-gather = bf16[1152,384]{1,0:T(8,128)(2,1)} all-gather(bf16[288,384]{1,0:T(8,128)(2,1)S(1)} %get-tuple-element.46), channel_id=2, replica_groups=mesh['dp'=4,'ctx'=32,'tp'=4] {'tp'}, dimensions={0}, use_global_device_ids=true | all-gather | bytes 1105920 | tf_op jit(solution)/shard_map/all_gather | solution.py:248
  77.6 6.9 %collective-permute-start.4 = (bf16[4,296,384]{2,1,0:T(8,128)(2,1)}, bf16[4,296,384]{2,1,0:T(8,128)(2,1)}, u32[]{:S(2)}, u32[]{:S(2)}) collective-permute-start(bf16[4,296,384]{2,1,0:T(8,128)(2,1)} %collective-permute-done.p2), channel_id=1, source_target_pairs={{0,4},{4,0},{8,12},{12,8},{16,20},{20,16},{24,28},{28,24},{32,36},... | collective-permute-start | bytes 2727944 | tf_op jit(solution)/shard_map/ppermute | solution.py:231
  84.5 1.9 %collective-permute-start.3 = (bf16[4,296,384]{2,1,0:T(8,128)(2,1)S(1)}, bf16[4,296,384]{2,1,0:T(8,128)(2,1)}, u32[]{:S(2)}, u32[]{:S(2)}) collective-permute-start(bf16[4,296,384]{2,1,0:T(8,128)(2,1)S(1)} %bitcast.56), channel_id=1, source_target_pairs={{0,4},{4,0},{8,12},{12,8},{16,20},{20,16},{24,28},{28,24},{32,36},... | collective-permute-start | bytes 2727944 | tf_op jit(solution)/shard_map/ppermute | solution.py:231
  86.5 0.7 copy.46
  87.2 2.3 %collective-permute-start.2 = (bf16[4,288,384]{2,1,0:T(8,128)(2,1)}, bf16[4,288,384]{2,1,0:T(8,128)(2,1)S(1)}, u32[]{:S(2)}, u32[]{:S(2)}) collective-permute-start(bf16[4,288,384]{2,1,0:T(8,128)(2,1)} %bitcast.62), channel_id=1, source_target_pairs={{0,8},{4,12},{8,0},{12,4},{16,24},{20,28},{24,16},{28,20},{32,40},... | collective-permute-start | bytes 2654216 | tf_op jit(solution)/shard_map/ppermute | solution.py:231
  89.5 2.7 %collective-permute-start.1 = (bf16[4,288,384]{2,1,0:T(8,128)(2,1)}, bf16[4,288,384]{2,1,0:T(8,128)(2,1)}, u32[]{:S(2)}, u32[]{:S(2)}) collective-permute-start(bf16[4,288,384]{2,1,0:T(8,128)(2,1)} %bitcast.63), channel_id=1, source_target_pairs={{0,4},{4,0},{8,12},{12,8},{16,20},{20,16},{24,28},{28,24},{32,36},... | collective-permute-start | bytes 2654216 | tf_op jit(solution)/shard_map/ppermute | solution.py:231
  92.2 0.7 slice_bitcast_fusion.2
  92.9 0.7 slice_bitcast_fusion
  93.6 0.7 slice_bitcast_fusion.4
  94.4 1.3 multiply_convert_fusion.hidden_t_ref
  95.7 5.8 %shard_map.77 = bf16[4,512,384]{2,1,0:T(8,128)(2,1)} custom-call(bf16[4,296,384]{2,1,0:T(8,128)(2,1)} %bitcast.58, bf16[4,296,384]{2,1,0:T(8,128)(2,1)} %collective-permute-done.3.p1, bf16[4,296,384]{2,1,0:T(8,128)(2,1)} %collective-permute-done.p2, bf16[4,296,384]{2,1,0:T(8,128)(2,1)} %collective-permute-done.4.p3, ...), custom_call_target="tpu_custom_call" | custom-call | flops 1048576 | bytes 1048576 | tf_op jit(solution)/shard_map/pallas_call | solution.py:268
  102.2 0.9 maximum_convert_fusion.gate_ref
  103.1 8.7 %shard_map.78 = (f32[576,512]{1,0:T(8,128)}, bf16[4,288,512]{2,1,0:T(8,128)(2,1)}, f32[4,8,288]{2,1,0:T(8,128)}) custom-call(s32[1]{0:T(128)} %bitcast.place_ref, bf16[4,296,384]{2,1,0:T(8,128)(2,1)} %bitcast.59, bf16[4,296,384]{2,1,0:T(8,128)(2,1)} %collective-permute-done.3.p1, bf16[4,296,384]{2,1,0:T(8,128)(2,1)} %collective-permute-done.p2, ...), custom_call_target="tpu_custom_call" | custom-call | flops 1048576 | bytes 1048576 | tf_op jit(solution)/shard_map/pallas_call | solution.py:268
  111.9 2.1 %collective-permute-start.5 = (bf16[4,288,384]{2,1,0:T(8,128)(2,1)S(1)}, bf16[4,288,384]{2,1,0:T(8,128)(2,1)S(1)}, u32[]{:S(2)}, u32[]{:S(2)}) collective-permute-start(bf16[4,288,384]{2,1,0:T(8,128)(2,1)S(1)} %collective-permute-done.2.p2), channel_id=1, source_target_pairs={{0,4},{4,0},{8,12},{12,8},{16,20},{20,16},{24,28},{28,24},{32,36},... | collective-permute-start | bytes 2654216 | tf_op jit(solution)/shard_map/ppermute | solution.py:231
  114.0 2.2 %collective-permute-done.5.p3 = bf16[4,288,384]{2,1,0:T(8,128)(2,1)S(1)} collective-permute-done((bf16[4,288,384]{2,1,0:T(8,128)(2,1)S(1)}, bf16[4,288,384]{2,1,0:T(8,128)(2,1)S(1)}, u32[]{:S(2)}, u32[]{:S(2)}) %collective-permute-start.5) | collective-permute-done | bytes 884768 | tf_op jit(solution)/shard_map/ppermute | solution.py:231
  116.2 0.9 copy-done.4
  117.1 5.8 %shard_map.79 = bf16[4,512,384]{2,1,0:T(8,128)(2,1)} custom-call(bf16[4,288,384]{2,1,0:T(8,128)(2,1)} %bitcast.65, bf16[4,288,384]{2,1,0:T(8,128)(2,1)} %collective-permute-done.1.n1.p1, bf16[4,288,384]{2,1,0:T(8,128)(2,1)} %copy-done.3, bf16[4,288,384]{2,1,0:T(8,128)(2,1)} %copy-done.4, bf16[512,1152]{1,0:T(8,128)(2,1)} %multiply_convert_fusion.hidden_t_ref), custom_call_target="tpu_custom_call" | custom-call | flops 17999998976 | bytes 1048576 | tf_op jit(solution)/shard_map/pallas_call | solution.py:268
  123.7 6.4 %shard_map.80 = (bf16[4,288,512]{2,1,0:T(8,128)(2,1)}, f32[4,8,288]{2,1,0:T(8,128)}) custom-call(s32[1]{0:T(128)} %bitcast.place_ref, bf16[4,288,384]{2,1,0:T(8,128)(2,1)} %copy-done.3, bf16[4,288,384]{2,1,0:T(8,128)(2,1)} %copy-done.4, bf16[4,512,768]{2,1,0:T(8,128)(2,1)} %bitcast.52, ...), custom_call_target="tpu_custom_call", output_to_operand_aliasing={{0}: (8, {})} | custom-call | flops 1048576 | bytes 1048576 | tf_op jit(solution)/shard_map/pallas_call | solution.py:268
  130.1 0.8 slice_reduce_fusion
  131.7 8.7 %all-to-all-start.1 = ((f32[128,1,36]{2,1,0:T(1,128)}), f32[128,1,36]{2,1,0:T(1,128)S(1)}, u32[]{:S(2)}, u32[]{:S(2)}) async-start(f32[128,1,36]{2,1,0:T(1,128)} %bitcast.25), calls=%async_computation.3 | async-start | bytes 131072 | tf_op jit(solution)/shard_map/all_to_all | solution.py:326
  140.4 2.2 %copy.51 = bf16[4,288,512]{2,0,1:T(4,128)(2,1)S(1)} copy(bf16[4,288,512]{2,1,0:T(8,128)(2,1)} %get-tuple-element.29) | data formatting | bytes 2359296 | tf_op jit(solution)/shard_map/pallas_call | solution.py:268
  142.9 1.1 reshape.123
  144.0 7.8 %all-to-all-done.1 = f32[128,1,36]{2,1,0:T(1,128)S(1)} async-done(((f32[128,1,36]{2,1,0:T(1,128)}), f32[128,1,36]{2,1,0:T(1,128)S(1)}, u32[]{:S(2)}, u32[]{:S(2)}) %all-to-all-start.1) | async-done | bytes 18464 | tf_op jit(solution)/shard_map/all_to_all | solution.py:326
  151.9 1.9 %gather_fusion = f32[256]{0:T(256)S(1)} fusion(f32[288]{0:T(512)S(1)} %reshape.125, s32[1024]{0:T(1024)S(1)} %pad_clamp_fusion), kind=kCustom, calls=%fused_computation | custom fusion | bytes 3072 | tf_op jit(solution)/shard_map/jit(_take)/gather | solution.py:331
  154.5 7.1 %reduce-scatter.5.cloned.1.call-done = bf16[1,512,384]{2,1,0:T(8,128)(2,1)} async-done(((bf16[4,512,384]{2,1,0:T(8,128)(2,1)}), bf16[1,512,384]{2,1,0:T(8,128)(2,1)}) %reduce-scatter.5.cloned.1.call-update) | async-done | bytes 393232 | tf_op jit(solution)/shard_map/reduce_scatter | solution.py:289
  161.6 2.1 %pad_maximum_fusion = bf16[512,768]{1,0:T(8,128)(2,1)} fusion(bf16[512,384]{1,0:T(8,128)(2,1)} %bitcast.69, bf16[512,384]{1,0:T(8,128)(2,1)} %bitcast.68), kind=kLoop, calls=%fused_computation.2 | loop fusion | flops 1572864 | bytes 1572864 | tf_op jit(solution)/shard_map/concatenate | solution.py:316
  (54 shorter events, 5.5 us)
Async XLA Ops:
  7.2 15.0 %copy-start.2 = (bf16[1152,512]{1,0:T(8,128)(2,1)S(1)}, bf16[1152,512]{1,0:T(8,128)(2,1)}, u32[]{:S(2)}) copy-start(bf16[1152,512]{1,0:T(8,128)(2,1)} %param.8) | copy-start | bytes 3538948
  9.5 22.1 %all-to-all-start = ((bf16[8,40,768]{2,1,0:T(8,128)(2,1)}), bf16[8,40,768]{2,1,0:T(8,128)(2,1)S(1)}, u32[]{:S(2)}, u32[]{:S(2)}) async-start(bf16[8,40,768]{2,1,0:T(8,128)(2,1)} %bitcast.67), calls=%async_computation | async-start | bytes 983040 | tf_op jit(solution)/shard_map/all_to_all | solution.py:224
  21.3 81.8 %all-gather.5.cloned.1.call-start = ((), (), s32[]{:S(2)}) async-start(), calls=%async_computation.6 | async-start | bytes 3932160 | tf_op jit(solution)/shard_map/all_gather | solution.py:243
  22.1 132.4 %reduce-scatter.3.cloned.1.call-start = ((), (), s32[]{:S(2)}) async-start(), calls=%async_computation.4 | async-start | bytes 1966080 | tf_op jit(solution)/shard_map/reduce_scatter | solution.py:289
  25.7 60.7 %copy-start = (bf16[4,288,512]{2,1,0:T(8,128)(2,1)}, bf16[4,288,512]{2,1,0:T(8,128)(2,1)S(1)}, u32[]{:S(2)}) copy-start(bf16[4,288,512]{2,1,0:T(8,128)(2,1)S(1)} %copy_dynamic-update-slice_fusion.hidden_ref) | copy-start | bytes 3538948
  48.5 41.0 %copy-start.1 = (bf16[1184,384]{1,0:T(8,128)(2,1)}, bf16[1184,384]{1,0:T(8,128)(2,1)S(1)}, u32[]{:S(2)}) copy-start(bf16[1184,384]{1,0:T(8,128)(2,1)S(1)} %all-gather.1) | copy-start | bytes 2727940
  48.5 29.1 %collective-permute-start = (bf16[4,296,384]{2,1,0:T(8,128)(2,1)S(1)}, bf16[4,296,384]{2,1,0:T(8,128)(2,1)}, u32[]{:S(2)}, u32[]{:S(2)}) collective-permute-start(bf16[4,296,384]{2,1,0:T(8,128)(2,1)S(1)} %bitcast.55), channel_id=1, source_target_pairs={{0,8},{4,12},{8,0},{12,4},{16,24},{20,28},{24,16},{28,20},{32,40},... | collective-permute-start | bytes 2727944 | tf_op jit(solution)/shard_map/ppermute | solution.py:231
  77.6 15.3 %collective-permute-start.4 = (bf16[4,296,384]{2,1,0:T(8,128)(2,1)}, bf16[4,296,384]{2,1,0:T(8,128)(2,1)}, u32[]{:S(2)}, u32[]{:S(2)}) collective-permute-start(bf16[4,296,384]{2,1,0:T(8,128)(2,1)} %collective-permute-done.p2), channel_id=1, source_target_pairs={{0,4},{4,0},{8,12},{12,8},{16,20},{20,16},{24,28},{28,24},{32,36},... | collective-permute-start | bytes 2727944 | tf_op jit(solution)/shard_map/ppermute | solution.py:231
  84.5 9.1 %collective-permute-start.3 = (bf16[4,296,384]{2,1,0:T(8,128)(2,1)S(1)}, bf16[4,296,384]{2,1,0:T(8,128)(2,1)}, u32[]{:S(2)}, u32[]{:S(2)}) collective-permute-start(bf16[4,296,384]{2,1,0:T(8,128)(2,1)S(1)} %bitcast.56), channel_id=1, source_target_pairs={{0,4},{4,0},{8,12},{12,8},{16,20},{20,16},{24,28},{28,24},{32,36},... | collective-permute-start | bytes 2727944 | tf_op jit(solution)/shard_map/ppermute | solution.py:231
  87.2 24.7 %collective-permute-start.2 = (bf16[4,288,384]{2,1,0:T(8,128)(2,1)}, bf16[4,288,384]{2,1,0:T(8,128)(2,1)S(1)}, u32[]{:S(2)}, u32[]{:S(2)}) collective-permute-start(bf16[4,288,384]{2,1,0:T(8,128)(2,1)} %bitcast.62), channel_id=1, source_target_pairs={{0,8},{4,12},{8,0},{12,4},{16,24},{20,28},{24,16},{28,20},{32,40},... | collective-permute-start | bytes 2654216 | tf_op jit(solution)/shard_map/ppermute | solution.py:231
  89.5 13.6 %collective-permute-start.1 = (bf16[4,288,384]{2,1,0:T(8,128)(2,1)}, bf16[4,288,384]{2,1,0:T(8,128)(2,1)}, u32[]{:S(2)}, u32[]{:S(2)}) collective-permute-start(bf16[4,288,384]{2,1,0:T(8,128)(2,1)} %bitcast.63), channel_id=1, source_target_pairs={{0,4},{4,0},{8,12},{12,8},{16,20},{20,16},{24,28},{28,24},{32,36},... | collective-permute-start | bytes 2654216 | tf_op jit(solution)/shard_map/ppermute | solution.py:231
  101.5 60.0 %reduce-scatter.5.cloned.1.call-start = ((), (), s32[]{:S(2)}) async-start(), calls=%async_computation.5 | async-start | bytes 1966080 | tf_op jit(solution)/shard_map/reduce_scatter | solution.py:289
  111.9 4.3 %copy-start.3 = (bf16[4,288,384]{2,1,0:T(8,128)(2,1)}, bf16[4,288,384]{2,1,0:T(8,128)(2,1)S(1)}, u32[]{:S(2)}) copy-start(bf16[4,288,384]{2,1,0:T(8,128)(2,1)S(1)} %collective-permute-done.2.p2) | copy-start | bytes 2654212
  111.9 4.3 %collective-permute-start.5 = (bf16[4,288,384]{2,1,0:T(8,128)(2,1)S(1)}, bf16[4,288,384]{2,1,0:T(8,128)(2,1)S(1)}, u32[]{:S(2)}, u32[]{:S(2)}) collective-permute-start(bf16[4,288,384]{2,1,0:T(8,128)(2,1)S(1)} %collective-permute-done.2.p2), channel_id=1, source_target_pairs={{0,4},{4,0},{8,12},{12,8},{16,20},{20,16},{24,28},{28,24},{32,36},... | collective-permute-start | bytes 2654216 | tf_op jit(solution)/shard_map/ppermute | solution.py:231
  116.2 0.9 copy-start.4
  123.0 0.7 copy-start.5
  131.7 20.1 %all-to-all-start.1 = ((f32[128,1,36]{2,1,0:T(1,128)}), f32[128,1,36]{2,1,0:T(1,128)S(1)}, u32[]{:S(2)}, u32[]{:S(2)}) async-start(f32[128,1,36]{2,1,0:T(1,128)} %bitcast.25), calls=%async_computation.3 | async-start | bytes 131072 | tf_op jit(solution)/shard_map/all_to_all | solution.py:326
  142.8 11.0 %copy-start.6 = (f32[2,128]{1,0:T(2,128)S(1)}, f32[2,128]{1,0:T(2,128)}, u32[]{:S(2)}) copy-start(f32[2,128]{1,0:T(2,128)} %get-tuple-element.30) | copy-start | bytes 3076
Sparse Core Ops, SparseCore 0:
  24.3 45.7 all-gather.4
  101.6 26.1 reduce-scatter.2
  130.7 30.8 reduce-scatter.4

commit v6 on v5

--- a/solution.py
+++ b/solution.py
@@ -38,23 +38,17 @@
         (chosen[0] + chosen[1]).astype(jnp.bfloat16), before, preferred_element_type=jnp.float32
     )
     row = lax.broadcasted_iota(jnp.int32, (rows, tokens), 0)
-    column = lax.broadcasted_iota(jnp.int32, (128, tokens), 0)
     place = jnp.zeros((rows, tokens), jnp.float32)
-    gate_block = jnp.zeros((rows, 128), jnp.float32)
     for k in range(TOP):
         slot = jnp.sum(earlier * chosen[k], axis=0, keepdims=True).astype(jnp.int32)
         gate = 1.0 / (1.0 + jnp.exp(logits_ref[1 - k : 2 - k, :] - logits_ref[k : k + 1, :]))
-        base = ids[k] * per_expert
-        place = place + (row == base + slot).astype(jnp.float32)
-        sent = jnp.where(row == base + capacity, gate, 0.0).astype(jnp.bfloat16)
-        gate_block = gate_block + compare_dot(sent, (column == slot).astype(jnp.bfloat16))
+        place = place + jnp.where(row == ids[k] * per_expert + slot, gate, 0.0)
         position_ref[k : k + 1, :] = ids[k] * capacity + slot
         gates_ref[k : k + 1, :] = gate
     packed = jnp.dot(
         place.astype(jnp.bfloat16), upstream_ref[...], preferred_element_type=jnp.float32
     )
-    packed_ref[:, :128] = (packed[:, :128] + gate_block).astype(jnp.bfloat16)
-    packed_ref[:, 128:] = packed[:, 128:].astype(jnp.bfloat16)
+    packed_ref[...] = packed.astype(jnp.bfloat16)
 
 
 def pack(ids, logits, upstream, capacity):
@@ -145,41 +139,40 @@
 
 
 def early_kernel(
-    place_ref, p0, p1, p2, p3, n0, n1, weight_ref, hidden_ref, gate_ref,
+    place_ref, p0, p1, p2, p3, n0, n1, weight_ref, hidden_ref,
     before_ref, grad_ref, partial_ref,
     full, side, next_full, next_side, total, hidden, grad, sems,
 ):
     copy = Copies(sems)
     rows = total.shape[0] // 2
+    half = total.shape[0]
     width = full.shape[1] // weight_ref.shape[0]
     sides = load_weight(copy, weight_ref, 0, side)
-    loads = load_rows(copy, (p0, p1, p2, p3), full)
+    loads = load_rows(copy, (p2, p3, p0, p1), full)
     sides_next = load_weight(copy, weight_ref, width, next_side)
     for i, made in enumerate(load_rows(copy, (n0, n1), next_full)):
-        loads[i] += made + [copy(hidden_ref.at[i], hidden.at[i])]
+        loads[i + 2] += made + [copy(hidden_ref.at[i], hidden.at[i])]
     stores = []
     wait(sides)
-    for i in (2, 3):
+    for i, at in enumerate(spans(rows, 2)):
         wait(loads[i])
-        at, to = slice(i * rows, (i + 1) * rows), slice((i - 2) * rows, (i - 1) * rows)
-        total[to, :] = compare_dot(full[at, :], side[...])
-        stores.append(copy(total.at[to, :], before_ref.at[to, :]))
+        total[at, :] = compare_dot(full[at, :], side[...])
+        stores.append(copy(total.at[at, :], before_ref.at[at, :]))
     wait(sides_next)
     partial_ref[...] = jnp.zeros(partial_ref.shape, jnp.float32)
-    for i in (0, 1):
-        wait(loads[i])
-        at = slice(i * rows, (i + 1) * rows)
-        proj = compare_dot(full[at, :], side[...])
+    for i, at in enumerate(spans(rows, 2)):
+        wait(loads[i + 2])
+        proj = compare_dot(full[half + i * rows : half + (i + 1) * rows, :], side[...])
         proj = proj + compare_dot(next_full[at, :], next_side[...])
         owner = jnp.bitwise_xor(place_ref[0], i)
         partial_ref[owner] = row_sums(hidden[i].astype(jnp.float32) * proj)
-        grad[i] = (gate_ref[i] * proj).astype(jnp.bfloat16)
+        grad[i] = proj.astype(jnp.bfloat16)
         stores.append(copy(grad.at[i], grad_ref.at[owner]))
     wait(stores)
 
 
 def late_kernel(
-    place_ref, p2, p3, weight_ref, before_ref, hidden_ref, gate_ref, early_partial_ref, early_grad,
+    place_ref, p2, p3, weight_ref, before_ref, hidden_ref, early_partial_ref, early_grad,
     grad_ref, partial_ref, full, side, total, hidden, grad, sems,
 ):
     copy = Copies(sems)
@@ -198,9 +191,15 @@
         proj = total[at, :] + compare_dot(full[at, :], side[...])
         owner = jnp.bitwise_xor(place_ref[0], i + 2)
         partial_ref[owner] = row_sums(hidden[i].astype(jnp.float32) * proj)
-        grad[i] = (gate_ref[i + 2] * proj).astype(jnp.bfloat16)
+        grad[i] = proj.astype(jnp.bfloat16)
         stores.append(copy(grad.at[i], grad_ref.at[owner]))
     wait(stores)
+
+
+def join_kernel(a_ref, b_ref, out_ref, sems):
+    copy = Copies(sems)
+    columns = spans(a_ref.shape[1], CHUNKS)
+    wait([copy(ref, out_ref.at[:, column]) for ref, column in zip((a_ref, b_ref), columns)])
 
 
 def after(x, *others):
@@ -225,7 +224,6 @@
         outgoing, "ctx", split_axis=0, concat_axis=0, tiled=True, axis_index_groups=groups
     )
     own_rows = received[:, :capacity].reshape(rows, cols)
-    gate_line = received[:, capacity, :capacity].reshape(1, rows)
 
     def swap(x, bit):
         return lax.ppermute(x, "ctx", [(c, c ^ bit) for c in range(context_count)])
@@ -239,21 +237,16 @@
         ]
     )
 
-    hidden_turned = hidden.reshape(total, units).T
+    hidden_t = hidden.reshape(total, units).T
     weight = lax.all_gather(down_weight, "dp", axis=0, tiled=False)
     width = cols // CHUNKS
     sent = [own_rows[:, column] for column in spans(width, CHUNKS)]
-    sent[0] = jnp.concatenate([sent[0], jnp.pad(gate_line, ((0, 7), (0, width - rows)))])
-    sent[0] = after(sent[0], hidden, hidden_turned)
+    sent[0] = after(sent[0], hidden, hidden_t)
     gathered = [lax.all_gather(x, "tp", axis=0, tiled=False) for x in sent]
     others = [swap(x, 2) for x in gathered]
     core = [swap(after(x, others[0], *gathered), 1) for x in gathered]
     last_others = swap(after(others[0], *gathered), 1)
     firsts = (gathered[0], core[0], others[0], last_others)
-
-    gate = jnp.stack([piece[0, rows, :rows] for piece in firsts]).astype(jnp.float32)
-    hidden_t = (hidden_turned.astype(jnp.float32) * gate.reshape(1, total)).astype(jnp.bfloat16)
-    gate_column = gate[:, :, None]
 
     place = quad.astype(jnp.int32).reshape(1)
     blocks = data_count
@@ -301,19 +294,22 @@
     before, early_grad, early_partial = call(
         early_kernel, (jax.ShapeDtypeStruct((half, units), jnp.float32), grad_shape, partial_shape),
         (held, held, vmem), [space(total, blocks * width), space(units, blocks * width)] + half_spaces,
-        blocks * 8 + 6, WEIGH[1], [smem] + [held] * 8 + [vmem],
-        (after(place, product), *firsts, gathered[1], core[1], weight, hidden, gate_column),
-    )
-    lasts = (others[1], swap(after(others[1], before, gate_column), 1))
+        blocks * 8 + 6, WEIGH[1], [smem] + [held] * 8,
+        (after(place, product), *firsts, gathered[1], core[1], weight, hidden),
+    )
+    lasts = (others[1], swap(after(others[1], before), 1))
     product = product_of((gathered[1], core[1], *lasts), WEIGH[2])
     grads.append(settle(product))
     hidden_grad, partial = call(
         late_kernel, (grad_shape, partial_shape), (held, vmem), half_spaces, blocks * 3 + 6,
-        1 << 20, [smem] + [held] * 5 + [vmem, vmem, held],
-        (after(place, product), *lasts, weight, before, hidden, gate_column, early_partial, early_grad),
-        {8: 0},
-    )
-    down_grad = jnp.concatenate(grads, axis=1)
+        1 << 20, [smem] + [held] * 5 + [vmem, held],
+        (after(place, product), *lasts, weight, before, hidden, early_partial, early_grad),
+        {7: 0},
+    )
+    down_grad = call(
+        join_kernel, jax.ShapeDtypeStruct((units, cols), jnp.bfloat16), held, [], CHUNKS, 1 << 20,
+        [held] * CHUNKS, grads,
+    )
 
     def canonical(x):
         x = x.reshape(QUADS, EXPERTS, capacity, -1).transpose(1, 0, 2, 3)
@@ -328,7 +324,8 @@
         ("ctx", "tp"), split_axis=0, concat_axis=0, tiled=True,
     )
     expert_sums = returned.reshape(EXPERTS, -1, capacity).sum(axis=1)
-    route_grad = jnp.take(expert_sums.reshape(-1), position)
+    gates_sent = gates.astype(jnp.bfloat16).astype(jnp.float32)
+    route_grad = jnp.take(expert_sums.reshape(-1), position) / gates_sent
     logit_grad = gates * (route_grad - jnp.sum(gates * route_grad, axis=0, keepdims=True))
     return (hidden_grad, down_grad, logit_grad.T)
 

time: 171 us -> 192 us (1.12)
  Pallas kernels: 29.1 us -> 52.7 us
  other arithmetic: 4.91 us -> 0.62 us
    pallas_call x4 -> x5, Pallas kernels: 26.8 us -> 50.5 us  [call(): pl.pallas_call(kernel, out_shape=outputs, in_specs=specs, out_specs=out_s...]
    ppermute x6, waiting for transfers between devices: 2.5 us -> 7.67 us  [swap(): return lax.ppermute(x, 'ctx', [(c, c ^ bit) for c in range(context_count)])]
    reduce_scatter x2, waiting for transfers between devices: 7.11 us -> 4.03 us  [settle(): return lax.psum_scatter(product, 'dp', scatter_dimension=0, tiled=False)]
    another operation x9 -> x0, local copies, waits for them, and re-layouts: 2.78 us -> none  [the longest x8 2.7 us: local(): jnp.stack([piece[0, rows, :rows] for piece in firsts]).astype(jnp.float32)]
    convert_element_type x3 -> x0, other arithmetic: 2.2 us -> none  [the longest x1 1.26 us: local(): (hidden_turned.astype(jnp.float32) * gate.reshape(1, total)).astype(jnp.b...]
    concatenate x2 -> x0, other arithmetic: 2.08 us -> none  [the longest x1 2.06 us: local(): down_grad = jnp.concatenate(grads, axis=1)]
  transfers between devices with their start and end apart: 11 -> 11, of which waited for: 5 -> 5; matrix products, arithmetic and copies ran while one was open for 10% -> 7% of each run, Pallas kernels for 16% -> 15%
where the time goes in v6:
time: 192 us; the launch traced here: 191 us
  Pallas kernels  52.7 us (27%)
  starting transfers between devices  48.6 us (25%)
  blocking collectives  33.7 us (18%)
  waiting for transfers between devices  25.3 us (13%)
  local copies, waits for them, and re-layouts  15.7 us (8%)
  between operations  14.1 us (7%)
    pallas_call x5, Pallas kernels, call(): pl.pallas_call(kernel, out_shape=outputs, in_specs=specs, out_specs=out_s...  50.5 us
    all_gather x2, blocking collectives, local(): gathered = [lax.all_gather(x, 'tp', axis=0, tiled=False) for x in sent]  33.7 us
    ppermute x6, starting transfers between devices, swap(): return lax.ppermute(x, 'ctx', [(c, c ^ bit) for c in range(context_count)])  27.8 us
    all_to_all x1, starting transfers between devices, local(): lax.all_to_all(outgoing, 'ctx', split_axis=0, concat_axis=0, tiled=True,...  11.9 us
    all_to_all x1, starting transfers between devices, local(): lax.all_to_all(outgoing_sums.reshape(context_count * tensor_count, capaci...  8.88 us
    all_to_all x1, waiting for transfers between devices, local(): lax.all_to_all(outgoing_sums.reshape(context_count * tensor_count, capaci...  7.79 us
    ppermute x6, waiting for transfers between devices, swap(): return lax.ppermute(x, 'ctx', [(c, c ^ bit) for c in range(context_count)])  7.67 us
    all_to_all x1, waiting for transfers between devices, local(): lax.all_to_all(outgoing, 'ctx', split_axis=0, concat_axis=0, tiled=True,...  5.11 us
  transfers between devices with their start and end apart: 11, of which 5 were waited for; matrix products, arithmetic and copies ran while one was open for 7% of the time, Pallas kernels for 15%

profile of v6, /device:TPU:1, one launch (start us, length us, event | category | flops | bytes accessed | tf_op | source)
XLA Modules:
  0.0 190.8 jit_solution(2332875116669148951)
XLA Ops:
  7.2 0.7 all-gather.5.cloned.1.call-update
  7.9 2.2 %shard_map.76 = (bf16[320,768]{1,0:T(8,128)(2,1)}, s32[2,128]{1,0:T(2,128)}, f32[2,128]{1,0:T(2,128)}) custom-call(s32[2,128]{1,0:T(2,128)} %bitcast.49, f32[2,128]{1,0:T(2,128)} %bitcast.50, bf16[128,768]{1,0:T(8,128)(2,1)} %upstream_ref.1), custom_call_target="tpu_custom_call" | custom-call | flops 62914560 | bytes 688128 | tf_op jit(solution)/shard_map/pallas_call | solution.py:57
  10.1 11.9 %all-to-all-start = ((bf16[8,40,768]{2,1,0:T(8,128)(2,1)}), bf16[8,40,768]{2,1,0:T(8,128)(2,1)S(1)}, u32[]{:S(2)}, u32[]{:S(2)}) async-start(bf16[8,40,768]{2,1,0:T(8,128)(2,1)} %bitcast.44), calls=%async_computation | async-start | bytes 983040 | tf_op jit(solution)/shard_map/all_to_all | solution.py:223
  22.9 2.4 %constant_dynamic-slice_fusion = (bf16[1,288,512]{2,0,1:T(2,128)(2,1)S(1)}, bf16[1,288,512]{2,0,1:T(2,128)(2,1)S(1)}, bf16[1,288,512]{2,0,1:T(2,128)(2,1)S(1)}, bf16[1,288,512]{2,0,1:T(2,128)(2,1)S(1)}) fusion(bf16[4,288,512]{2,0,1:T(4,128)(2,1)S(1)} %bitcast.34, s32[]{:T(128)S(6)} %select_n.25, s32[]{:T(128)S(6)} %select_n.24, s32[]{:T(128)S(6)} %select_n.23, ...), kind=kLoop, calls=%fused_computation.13 | loop fusion | bytes 2359312 | tf_op jit(solution)/shard_map/jit(dynamic_index_in_dim)/dynamic_slice | solution.py:235
  25.6 1.4 copy.26
  27.0 5.1 %all-to-all-done = bf16[8,40,768]{2,1,0:T(8,128)(2,1)S(1)} async-done(((bf16[8,40,768]{2,1,0:T(8,128)(2,1)}), bf16[8,40,768]{2,1,0:T(8,128)(2,1)S(1)}, u32[]{:S(2)}, u32[]{:S(2)}) %all-to-all-start) | async-done | bytes 491552 | tf_op jit(solution)/shard_map/all_to_all | solution.py:223
  32.3 16.6 %all-gather.1 = bf16[1152,384]{1,0:T(8,128)(2,1)S(1)} all-gather(bf16[288,384]{1,0:T(8,128)(2,1)S(1)} %get-tuple-element.19), channel_id=3, replica_groups=mesh['dp'=4,'ctx'=32,'tp'=4] {'tp'}, dimensions={0}, use_global_device_ids=true | all-gather | bytes 1105920 | tf_op jit(solution)/shard_map/all_gather | solution.py:245
  48.9 11.8 %collective-permute-start = (bf16[4,288,384]{2,1,0:T(8,128)(2,1)S(1)}, bf16[4,288,384]{2,1,0:T(8,128)(2,1)S(1)}, u32[]{:S(2)}, u32[]{:S(2)}) collective-permute-start(bf16[4,288,384]{2,1,0:T(8,128)(2,1)S(1)} %bitcast.35), channel_id=1, source_target_pairs={{0,8},{4,12},{8,0},{12,4},{16,24},{20,28},{24,16},{28,20},{32,40},... | collective-permute-start | bytes 2654216 | tf_op jit(solution)/shard_map/ppermute | solution.py:229
  60.7 17.1 %all-gather = bf16[1152,384]{1,0:T(8,128)(2,1)} all-gather(bf16[288,384]{1,0:T(8,128)(2,1)S(1)} %get-tuple-element.40), channel_id=2, replica_groups=mesh['dp'=4,'ctx'=32,'tp'=4] {'tp'}, dimensions={0}, use_global_device_ids=true | all-gather | bytes 1105920 | tf_op jit(solution)/shard_map/all_gather | solution.py:245
  77.8 6.6 %collective-permute-start.4 = (bf16[4,288,384]{2,1,0:T(8,128)(2,1)S(1)}, bf16[4,288,384]{2,1,0:T(8,128)(2,1)S(1)}, u32[]{:S(2)}, u32[]{:S(2)}) collective-permute-start(bf16[4,288,384]{2,1,0:T(8,128)(2,1)S(1)} %collective-permute-done.p2), channel_id=1, source_target_pairs={{0,4},{4,0},{8,12},{12,8},{16,20},{20,16},{24,28},{28,24},{32,36},... | collective-permute-start | bytes 2654216 | tf_op jit(solution)/shard_map/ppermute | solution.py:229
  84.4 1.9 %collective-permute-start.3 = (bf16[4,288,384]{2,1,0:T(8,128)(2,1)S(1)}, bf16[4,288,384]{2,1,0:T(8,128)(2,1)S(1)}, u32[]{:S(2)}, u32[]{:S(2)}) collective-permute-start(bf16[4,288,384]{2,1,0:T(8,128)(2,1)S(1)} %bitcast.36), channel_id=1, source_target_pairs={{0,4},{4,0},{8,12},{12,8},{16,20},{20,16},{24,28},{28,24},{32,36},... | collective-permute-start | bytes 2654216 | tf_op jit(solution)/shard_map/ppermute | solution.py:229
  86.3 2.4 %collective-permute-start.1 = (bf16[4,288,384]{2,1,0:T(8,128)(2,1)}, bf16[4,288,384]{2,1,0:T(8,128)(2,1)}, u32[]{:S(2)}, u32[]{:S(2)}) collective-permute-start(bf16[4,288,384]{2,1,0:T(8,128)(2,1)} %bitcast.4.n0.p0), channel_id=1, source_target_pairs={{0,4},{4,0},{8,12},{12,8},{16,20},{20,16},{24,28},{28,24},{32,36},... | collective-permute-start | bytes 2654216 | tf_op jit(solution)/shard_map/ppermute | solution.py:229
  88.7 2.2 %collective-permute-start.2 = (bf16[4,288,384]{2,1,0:T(8,128)(2,1)}, bf16[4,288,384]{2,1,0:T(8,128)(2,1)}, u32[]{:S(2)}, u32[]{:S(2)}) collective-permute-start(bf16[4,288,384]{2,1,0:T(8,128)(2,1)} %bitcast.4.n0.p0), channel_id=1, source_target_pairs={{0,8},{4,12},{8,0},{12,4},{16,24},{20,28},{24,16},{28,20},{32,40},... | collective-permute-start | bytes 2654216 | tf_op jit(solution)/shard_map/ppermute | solution.py:229
  91.0 0.9 copy-done.3
  91.9 0.9 copy-done.4
  92.8 5.8 %shard_map.77 = bf16[4,512,384]{2,1,0:T(8,128)(2,1)} custom-call(bf16[4,288,384]{2,1,0:T(8,128)(2,1)} %bitcast.37, bf16[4,288,384]{2,1,0:T(8,128)(2,1)} %copy-done.4, bf16[4,288,384]{2,1,0:T(8,128)(2,1)} %copy-done.2, bf16[4,288,384]{2,1,0:T(8,128)(2,1)} %copy-done.3, bf16[512,1152]{1,0:T(8,128)(2,1)} %bitcast.41), custom_call_target="tpu_custom_call" | custom-call | flops 1048576 | bytes 1048576 | tf_op jit(solution)/shard_map/pallas_call | solution.py:261
  98.7 7.9 %shard_map.78 = (f32[576,512]{1,0:T(8,128)}, bf16[4,288,512]{2,1,0:T(8,128)(2,1)}, f32[4,8,288]{2,1,0:T(8,128)}) custom-call(s32[1]{0:T(128)} %bitcast.place_ref, bf16[4,288,384]{2,1,0:T(8,128)(2,1)} %bitcast.38, bf16[4,288,384]{2,1,0:T(8,128)(2,1)} %copy-done.4, bf16[4,288,384]{2,1,0:T(8,128)(2,1)} %copy-done.2, bf16[4,288,384]{2,1,0:T(8,128)(2,1)} %copy-done.3, ...), custom_call_target="tpu_custom_call" | custom-call | flops 1048576 | bytes 1048576 | tf_op jit(solution)/shard_map/pallas_call | solution.py:261
  106.6 5.6 %collective-permute-done.2.p2 = bf16[4,288,384]{2,1,0:T(8,128)(2,1)} collective-permute-done((bf16[4,288,384]{2,1,0:T(8,128)(2,1)}, bf16[4,288,384]{2,1,0:T(8,128)(2,1)}, u32[]{:S(2)}, u32[]{:S(2)}) %collective-permute-start.2) | collective-permute-done | bytes 884768 | tf_op jit(solution)/shard_map/ppermute | solution.py:229
  112.2 2.9 %collective-permute-start.5 = (bf16[4,288,384]{2,1,0:T(8,128)(2,1)}, bf16[4,288,384]{2,1,0:T(8,128)(2,1)S(1)}, u32[]{:S(2)}, u32[]{:S(2)}) collective-permute-start(bf16[4,288,384]{2,1,0:T(8,128)(2,1)} %collective-permute-done.2.p2), channel_id=1, source_target_pairs={{0,4},{4,0},{8,12},{12,8},{16,20},{20,16},{24,28},{28,24},{32,36},... | collective-permute-start | bytes 2654216 | tf_op jit(solution)/shard_map/ppermute | solution.py:229
  115.1 2.1 %collective-permute-done.5.p3 = bf16[4,288,384]{2,1,0:T(8,128)(2,1)S(1)} collective-permute-done((bf16[4,288,384]{2,1,0:T(8,128)(2,1)}, bf16[4,288,384]{2,1,0:T(8,128)(2,1)S(1)}, u32[]{:S(2)}, u32[]{:S(2)}) %collective-permute-start.5) | collective-permute-done | bytes 884768 | tf_op jit(solution)/shard_map/ppermute | solution.py:229
  117.2 1.0 copy-done.6
  118.1 5.9 %shard_map.79 = bf16[4,512,384]{2,1,0:T(8,128)(2,1)} custom-call(bf16[4,288,384]{2,1,0:T(8,128)(2,1)} %bitcast.4.n0.p0, bf16[4,288,384]{2,1,0:T(8,128)(2,1)} %collective-permute-done.1.n1.p1, bf16[4,288,384]{2,1,0:T(8,128)(2,1)} %collective-permute-done.2.p2, bf16[4,288,384]{2,1,0:T(8,128)(2,1)} %copy-done.6, bf16[512,1152]{1,0:T(8,128)(2,1)} %bitcast.42), custom_call_target="tpu_custom_call" | custom-call | flops 17999998976 | bytes 1048576 | tf_op jit(solution)/shard_map/pallas_call | solution.py:261
  124.1 0.6 copy-done.8
  124.7 6.0 %shard_map.80 = (bf16[4,288,512]{2,1,0:T(8,128)(2,1)}, f32[4,8,288]{2,1,0:T(8,128)}) custom-call(s32[1]{0:T(128)} %bitcast.place_ref, bf16[4,288,384]{2,1,0:T(8,128)(2,1)} %collective-permute-done.2.p2, bf16[4,288,384]{2,1,0:T(8,128)(2,1)} %copy-done.6, bf16[4,512,768]{2,1,0:T(8,128)(2,1)} %bitcast.32, ...), custom_call_target="tpu_custom_call", output_to_operand_aliasing={{0}: (7, {})} | custom-call | flops 1048576 | bytes 1048576 | tf_op jit(solution)/shard_map/pallas_call | solution.py:261
  130.7 0.8 slice_reduce_fusion
  132.3 8.9 %all-to-all-start.1 = ((f32[128,1,36]{2,1,0:T(1,128)}), f32[128,1,36]{2,1,0:T(1,128)S(1)}, u32[]{:S(2)}, u32[]{:S(2)}) async-start(f32[128,1,36]{2,1,0:T(1,128)} %bitcast.17), calls=%async_computation.3 | async-start | bytes 131072 | tf_op jit(solution)/shard_map/all_to_all | solution.py:322
  141.2 2.2 %copy.27 = bf16[4,288,512]{2,0,1:T(4,128)(2,1)S(1)} copy(bf16[4,288,512]{2,1,0:T(8,128)(2,1)} %get-tuple-element.29) | data formatting | bytes 2359296 | tf_op jit(solution)/shard_map/pallas_call | solution.py:261
  143.7 1.1 reshape.56
  144.8 7.8 %all-to-all-done.1 = f32[128,1,36]{2,1,0:T(1,128)S(1)} async-done(((f32[128,1,36]{2,1,0:T(1,128)}), f32[128,1,36]{2,1,0:T(1,128)S(1)}, u32[]{:S(2)}, u32[]{:S(2)}) %all-to-all-start.1) | async-done | bytes 18464 | tf_op jit(solution)/shard_map/all_to_all | solution.py:322
  152.7 1.9 %gather_fusion = f32[256]{0:T(256)S(1)} fusion(f32[288]{0:T(512)S(1)} %reshape.58, s32[1024]{0:T(1024)S(1)} %pad_clamp_fusion), kind=kCustom, calls=%fused_computation | custom fusion | bytes 3072 | tf_op jit(solution)/shard_map/jit(_take)/gather | solution.py:328
  155.3 4.0 %reduce-scatter.5.cloned.1.call-done = bf16[1,512,384]{2,1,0:T(8,128)(2,1)} async-done(((bf16[4,512,384]{2,1,0:T(8,128)(2,1)}), bf16[1,512,384]{2,1,0:T(8,128)(2,1)}) %reduce-scatter.5.cloned.1.call-update) | async-done | bytes 393232 | tf_op jit(solution)/shard_map/reduce_scatter | solution.py:282
  159.3 24.9 %shard_map.81 = bf16[512,768]{1,0:T(8,128)(2,1)} custom-call(bf16[512,384]{1,0:T(8,128)(2,1)} %bitcast.45, bf16[512,384]{1,0:T(8,128)(2,1)} %bitcast.46), custom_call_target="tpu_custom_call" | custom-call | flops 1048576 | bytes 1048576 | tf_op jit(solution)/shard_map/pallas_call | solution.py:261
  (43 shorter events, 3.1 us)
Async XLA Ops:
  7.2 14.8 %copy-start.5 = (bf16[1152,512]{1,0:T(8,128)(2,1)S(1)}, bf16[1152,512]{1,0:T(8,128)(2,1)}, u32[]{:S(2)}) copy-start(bf16[1152,512]{1,0:T(8,128)(2,1)} %param.8) | copy-start | bytes 3538948
  7.2 91.5 %all-gather.5.cloned.1.call-start = ((), (), s32[]{:S(2)}) async-start(), calls=%async_computation.6 | async-start | bytes 3932160 | tf_op jit(solution)/shard_map/all_gather | solution.py:241
  10.1 22.1 %all-to-all-start = ((bf16[8,40,768]{2,1,0:T(8,128)(2,1)}), bf16[8,40,768]{2,1,0:T(8,128)(2,1)S(1)}, u32[]{:S(2)}, u32[]{:S(2)}) async-start(bf16[8,40,768]{2,1,0:T(8,128)(2,1)} %bitcast.44), calls=%async_computation | async-start | bytes 983040 | tf_op jit(solution)/shard_map/all_to_all | solution.py:223
  21.9 133.3 %reduce-scatter.3.cloned.1.call-start = ((), (), s32[]{:S(2)}) async-start(), calls=%async_computation.4 | async-start | bytes 1966080 | tf_op jit(solution)/shard_map/reduce_scatter | solution.py:282
  25.6 1.4 copy-start
  48.9 42.1 %copy-start.1 = (bf16[1152,384]{1,0:T(8,128)(2,1)}, bf16[1152,384]{1,0:T(8,128)(2,1)S(1)}, u32[]{:S(2)}) copy-start(bf16[1152,384]{1,0:T(8,128)(2,1)S(1)} %all-gather.1) | copy-start | bytes 2654212
  48.9 28.9 %collective-permute-start = (bf16[4,288,384]{2,1,0:T(8,128)(2,1)S(1)}, bf16[4,288,384]{2,1,0:T(8,128)(2,1)S(1)}, u32[]{:S(2)}, u32[]{:S(2)}) collective-permute-start(bf16[4,288,384]{2,1,0:T(8,128)(2,1)S(1)} %bitcast.35), channel_id=1, source_target_pairs={{0,8},{4,12},{8,0},{12,4},{16,24},{20,28},{24,16},{28,20},{32,40},... | collective-permute-start | bytes 2654216 | tf_op jit(solution)/shard_map/ppermute | solution.py:229
  77.8 13.2 %copy-start.2 = (bf16[4,288,384]{2,1,0:T(8,128)(2,1)}, bf16[4,288,384]{2,1,0:T(8,128)(2,1)S(1)}, u32[]{:S(2)}) copy-start(bf16[4,288,384]{2,1,0:T(8,128)(2,1)S(1)} %collective-permute-done.p2) | copy-start | bytes 2654212
  77.8 13.1 %collective-permute-start.4 = (bf16[4,288,384]{2,1,0:T(8,128)(2,1)S(1)}, bf16[4,288,384]{2,1,0:T(8,128)(2,1)S(1)}, u32[]{:S(2)}, u32[]{:S(2)}) collective-permute-start(bf16[4,288,384]{2,1,0:T(8,128)(2,1)S(1)} %collective-permute-done.p2), channel_id=1, source_target_pairs={{0,4},{4,0},{8,12},{12,8},{16,20},{20,16},{24,28},{28,24},{32,36},... | collective-permute-start | bytes 2654216 | tf_op jit(solution)/shard_map/ppermute | solution.py:229
  84.4 6.6 %collective-permute-start.3 = (bf16[4,288,384]{2,1,0:T(8,128)(2,1)S(1)}, bf16[4,288,384]{2,1,0:T(8,128)(2,1)S(1)}, u32[]{:S(2)}, u32[]{:S(2)}) collective-permute-start(bf16[4,288,384]{2,1,0:T(8,128)(2,1)S(1)} %bitcast.36), channel_id=1, source_target_pairs={{0,4},{4,0},{8,12},{12,8},{16,20},{20,16},{24,28},{28,24},{32,36},... | collective-permute-start | bytes 2654216 | tf_op jit(solution)/shard_map/ppermute | solution.py:229
  86.3 12.4 %collective-permute-start.1 = (bf16[4,288,384]{2,1,0:T(8,128)(2,1)}, bf16[4,288,384]{2,1,0:T(8,128)(2,1)}, u32[]{:S(2)}, u32[]{:S(2)}) collective-permute-start(bf16[4,288,384]{2,1,0:T(8,128)(2,1)} %bitcast.4.n0.p0), channel_id=1, source_target_pairs={{0,4},{4,0},{8,12},{12,8},{16,20},{20,16},{24,28},{28,24},{32,36},... | collective-permute-start | bytes 2654216 | tf_op jit(solution)/shard_map/ppermute | solution.py:229
  88.7 23.5 %collective-permute-start.2 = (bf16[4,288,384]{2,1,0:T(8,128)(2,1)}, bf16[4,288,384]{2,1,0:T(8,128)(2,1)}, u32[]{:S(2)}, u32[]{:S(2)}) collective-permute-start(bf16[4,288,384]{2,1,0:T(8,128)(2,1)} %bitcast.4.n0.p0), channel_id=1, source_target_pairs={{0,8},{4,12},{8,0},{12,4},{16,24},{20,28},{24,16},{28,20},{32,40},... | collective-permute-start | bytes 2654216 | tf_op jit(solution)/shard_map/ppermute | solution.py:229
  91.0 0.9 copy-start.3
  91.9 0.9 copy-start.4
  98.6 60.7 %reduce-scatter.5.cloned.1.call-start = ((), (), s32[]{:S(2)}) async-start(), calls=%async_computation.5 | async-start | bytes 1966080 | tf_op jit(solution)/shard_map/reduce_scatter | solution.py:282
  112.2 4.9 %collective-permute-start.5 = (bf16[4,288,384]{2,1,0:T(8,128)(2,1)}, bf16[4,288,384]{2,1,0:T(8,128)(2,1)S(1)}, u32[]{:S(2)}, u32[]{:S(2)}) collective-permute-start(bf16[4,288,384]{2,1,0:T(8,128)(2,1)} %collective-permute-done.2.p2), channel_id=1, source_target_pairs={{0,4},{4,0},{8,12},{12,8},{16,20},{20,16},{24,28},{28,24},{32,36},... | collective-permute-start | bytes 2654216 | tf_op jit(solution)/shard_map/ppermute | solution.py:229
  117.2 1.0 copy-start.6
  124.0 0.7 copy-start.8
  132.3 20.3 %all-to-all-start.1 = ((f32[128,1,36]{2,1,0:T(1,128)}), f32[128,1,36]{2,1,0:T(1,128)S(1)}, u32[]{:S(2)}, u32[]{:S(2)}) async-start(f32[128,1,36]{2,1,0:T(1,128)} %bitcast.17), calls=%async_computation.3 | async-start | bytes 131072 | tf_op jit(solution)/shard_map/all_to_all | solution.py:322
  143.7 11.0 %copy-start.7 = (f32[2,128]{1,0:T(2,128)S(1)}, f32[2,128]{1,0:T(2,128)}, u32[]{:S(2)}) copy-start(f32[2,128]{1,0:T(2,128)} %get-tuple-element.30) | copy-start | bytes 3076
Sparse Core Ops, SparseCore 0:
  10.1 50.3 all-gather.4
  98.8 26.8 reduce-scatter.2
  128.5 30.7 reduce-scatter.4

commit v7 on v6

--- a/solution.py
+++ b/solution.py
@@ -139,67 +139,65 @@
 
 
 def early_kernel(
-    place_ref, p0, p1, p2, p3, n0, n1, weight_ref, hidden_ref,
+    place_ref, p0, p1, p2, p3, n0, weight_ref, hidden_ref,
     before_ref, grad_ref, partial_ref,
     full, side, next_full, next_side, total, hidden, grad, sems,
 ):
     copy = Copies(sems)
-    rows = total.shape[0] // 2
-    half = total.shape[0]
+    rows = next_full.shape[0]
     width = full.shape[1] // weight_ref.shape[0]
     sides = load_weight(copy, weight_ref, 0, side)
-    loads = load_rows(copy, (p2, p3, p0, p1), full)
+    loads = load_rows(copy, (p0, p1, p2, p3), full)
     sides_next = load_weight(copy, weight_ref, width, next_side)
-    for i, made in enumerate(load_rows(copy, (n0, n1), next_full)):
-        loads[i + 2] += made + [copy(hidden_ref.at[i], hidden.at[i])]
+    loads_next = load_rows(copy, (n0,), next_full)[0] + [copy(hidden_ref.at[0], hidden)]
     stores = []
     wait(sides)
-    for i, at in enumerate(spans(rows, 2)):
+    for i, at in enumerate(spans(rows, QUADS)):
         wait(loads[i])
         total[at, :] = compare_dot(full[at, :], side[...])
-        stores.append(copy(total.at[at, :], before_ref.at[at, :]))
-    wait(sides_next)
+        if i:
+            to = slice((i - 1) * rows, i * rows)
+            stores.append(copy(total.at[at, :], before_ref.at[to, :]))
+    wait(sides_next + loads_next)
+    proj = total[:rows, :] + compare_dot(next_full[...], next_side[...])
+    owner = place_ref[0]
     partial_ref[...] = jnp.zeros(partial_ref.shape, jnp.float32)
-    for i, at in enumerate(spans(rows, 2)):
-        wait(loads[i + 2])
-        proj = compare_dot(full[half + i * rows : half + (i + 1) * rows, :], side[...])
-        proj = proj + compare_dot(next_full[at, :], next_side[...])
-        owner = jnp.bitwise_xor(place_ref[0], i)
+    partial_ref[owner] = row_sums(hidden[...].astype(jnp.float32) * proj)
+    grad[...] = proj.astype(jnp.bfloat16)
+    stores.append(copy(grad, grad_ref.at[owner]))
+    wait(stores)
+
+
+def late_kernel(
+    place_ref, p1, p2, p3, weight_ref, before_ref, hidden_ref, early_partial_ref, early_grad,
+    grad_ref, partial_ref, full, side, total, hidden, grad, sems,
+):
+    copy = Copies(sems)
+    late = QUADS - 1
+    rows = full.shape[0] // late
+    width = full.shape[1] // weight_ref.shape[0]
+    sides = load_weight(copy, weight_ref, width, side)
+    loads = load_rows(copy, (p1, p2, p3), full)
+    for i, at in enumerate(spans(rows, late)):
+        loads[i].append(copy(before_ref.at[at, :], total.at[at, :]))
+        loads[i].append(copy(hidden_ref.at[i + 1], hidden.at[i]))
+    partial_ref[...] = early_partial_ref[...]
+    wait(sides)
+    stores = []
+    for i, at in enumerate(spans(rows, late)):
+        wait(loads[i])
+        proj = total[at, :] + compare_dot(full[at, :], side[...])
+        owner = jnp.bitwise_xor(place_ref[0], i + 1)
         partial_ref[owner] = row_sums(hidden[i].astype(jnp.float32) * proj)
         grad[i] = proj.astype(jnp.bfloat16)
         stores.append(copy(grad.at[i], grad_ref.at[owner]))
     wait(stores)
 
 
-def late_kernel(
-    place_ref, p2, p3, weight_ref, before_ref, hidden_ref, early_partial_ref, early_grad,
-    grad_ref, partial_ref, full, side, total, hidden, grad, sems,
-):
-    copy = Copies(sems)
-    rows = total.shape[0] // 2
-    width = full.shape[1] // weight_ref.shape[0]
-    sides = load_weight(copy, weight_ref, width, side)
-    loads = load_rows(copy, (p2, p3), full)
-    for i, at in enumerate(spans(rows, 2)):
-        loads[i].append(copy(before_ref.at[at, :], total.at[at, :]))
-        loads[i].append(copy(hidden_ref.at[i + 2], hidden.at[i]))
-    partial_ref[...] = early_partial_ref[...]
-    wait(sides)
-    stores = []
-    for i, at in enumerate(spans(rows, 2)):
-        wait(loads[i])
-        proj = total[at, :] + compare_dot(full[at, :], side[...])
-        owner = jnp.bitwise_xor(place_ref[0], i + 2)
-        partial_ref[owner] = row_sums(hidden[i].astype(jnp.float32) * proj)
-        grad[i] = proj.astype(jnp.bfloat16)
-        stores.append(copy(grad.at[i], grad_ref.at[owner]))
-    wait(stores)
-
-
-def join_kernel(a_ref, b_ref, out_ref, sems):
-    copy = Copies(sems)
-    columns = spans(a_ref.shape[1], CHUNKS)
-    wait([copy(ref, out_ref.at[:, column]) for ref, column in zip((a_ref, b_ref), columns)])
+def join_kernel(a_ref, b_ref, out_ref):
+    width = a_ref.shape[1]
+    out_ref[:, :width] = a_ref[...]
+    out_ref[:, width:] = b_ref[...]
 
 
 def after(x, *others):
@@ -250,7 +248,7 @@
 
     place = quad.astype(jnp.int32).reshape(1)
     blocks = data_count
-    held = pl.BlockSpec(memory_space=pl.ANY)
+    held = pl.BlockSpec(memory_space=pltpu.HBM)
     vmem = pl.BlockSpec(memory_space=pltpu.VMEM)
     smem = pl.BlockSpec(memory_space=pltpu.SMEM)
 
@@ -283,33 +281,39 @@
 
     grad_shape = jax.ShapeDtypeStruct((QUADS, rows, units), jnp.bfloat16)
     partial_shape = jax.ShapeDtypeStruct((QUADS, 8, rows), jnp.float32)
-    half = total // 2
-    half_spaces = [
-        space(half, blocks * width), space(units, blocks * width),
-        space(half, units, dtype=jnp.float32), space(2, rows, units), space(2, rows, units),
-    ]
-
+    late = total - rows
     product = product_of(firsts, WEIGH[0])
     grads = [settle(product)]
     before, early_grad, early_partial = call(
-        early_kernel, (jax.ShapeDtypeStruct((half, units), jnp.float32), grad_shape, partial_shape),
-        (held, held, vmem), [space(total, blocks * width), space(units, blocks * width)] + half_spaces,
-        blocks * 8 + 6, WEIGH[1], [smem] + [held] * 8,
-        (after(place, product), *firsts, gathered[1], core[1], weight, hidden),
-    )
-    lasts = (others[1], swap(after(others[1], before), 1))
-    product = product_of((gathered[1], core[1], *lasts), WEIGH[2])
+        early_kernel, (jax.ShapeDtypeStruct((late, units), jnp.float32), grad_shape, partial_shape),
+        (held, held, vmem),
+        [
+            space(total, blocks * width), space(units, blocks * width),
+            space(rows, blocks * width), space(units, blocks * width),
+            space(total, units, dtype=jnp.float32), space(rows, units), space(rows, units),
+        ],
+        blocks * (QUADS + 3) + 1 + QUADS, WEIGH[1], [smem] + [held] * 7,
+        (after(place, product), *firsts, gathered[1], weight, hidden),
+    )
+    lasts = (core[1], others[1], swap(after(others[1], before), 1))
+    product = product_of((gathered[1], *lasts), WEIGH[2])
     grads.append(settle(product))
     hidden_grad, partial = call(
-        late_kernel, (grad_shape, partial_shape), (held, vmem), half_spaces, blocks * 3 + 6,
-        1 << 20, [smem] + [held] * 5 + [vmem, held],
+        late_kernel, (grad_shape, partial_shape), (held, vmem),
+        [
+            space(late, blocks * width), space(units, blocks * width),
+            space(late, units, dtype=jnp.float32),
+            space(QUADS - 1, rows, units), space(QUADS - 1, rows, units),
+        ],
+        blocks * QUADS + 3 * (QUADS - 1), 1 << 20, [smem] + [held] * 6 + [vmem, held],
         (after(place, product), *lasts, weight, before, hidden, early_partial, early_grad),
-        {7: 0},
-    )
-    down_grad = call(
-        join_kernel, jax.ShapeDtypeStruct((units, cols), jnp.bfloat16), held, [], CHUNKS, 1 << 20,
-        [held] * CHUNKS, grads,
-    )
+        {8: 0},
+    )
+    down_grad = pl.pallas_call(
+        join_kernel,
+        out_shape=jax.ShapeDtypeStruct((units, cols), jnp.bfloat16),
+        compiler_params=pltpu.CompilerParams(vmem_limit_bytes=VMEM_LIMIT),
+    )(*grads)
 
     def canonical(x):
         x = x.reshape(QUADS, EXPERTS, capacity, -1).transpose(1, 0, 2, 3)

time: 192 us -> 167 us (0.87)
  Pallas kernels: 52.7 us -> 30 us
  waiting for transfers between devices: 25.3 us -> 22.6 us
    pallas_call x5 -> x4, Pallas kernels: 50.5 us -> 25.8 us  [call(): pl.pallas_call(kernel, out_shape=outputs, in_specs=specs, out_specs=out_s...]
    pallas_call x0 -> x1, Pallas kernels: none -> 2.06 us  [local(): pl.pallas_call(join_kernel, out_shape=jax.ShapeDtypeStruct((units, cols),...]
  transfers between devices with their start and end apart: 11 -> 11, of which waited for: 5 -> 6; matrix products, arithmetic and copies ran while one was open for 7% -> 8% of each run, Pallas kernels for 15% -> 17%
where the time goes in v7:
time: 167 us; the launch traced here: 166 us
  starting transfers between devices  49.4 us (30%)
  blocking collectives  33.7 us (20%)
  Pallas kernels  30 us (18%)
  waiting for transfers between devices  22.6 us (14%)
  local copies, waits for them, and re-layouts  15.5 us (9%)
  between operations  14.1 us (8%)
    all_gather x2, blocking collectives, local(): gathered = [lax.all_gather(x, 'tp', axis=0, tiled=False) for x in sent]  33.7 us
    ppermute x6, starting transfers between devices, swap(): return lax.ppermute(x, 'ctx', [(c, c ^ bit) for c in range(context_count)])  28.6 us
    pallas_call x4, Pallas kernels, call(): pl.pallas_call(kernel, out_shape=outputs, in_specs=specs, out_specs=out_s...  25.8 us
    all_to_all x1, starting transfers between devices, local(): lax.all_to_all(outgoing, 'ctx', split_axis=0, concat_axis=0, tiled=True,...  11.9 us
    all_to_all x1, starting transfers between devices, local(): lax.all_to_all(outgoing_sums.reshape(context_count * tensor_count, capaci...  8.84 us
    all_to_all x1, waiting for transfers between devices, local(): lax.all_to_all(outgoing_sums.reshape(context_count * tensor_count, capaci...  7.79 us
    ppermute x6, waiting for transfers between devices, swap(): return lax.ppermute(x, 'ctx', [(c, c ^ bit) for c in range(context_count)])  5.83 us
    all_to_all x1, waiting for transfers between devices, local(): lax.all_to_all(outgoing, 'ctx', split_axis=0, concat_axis=0, tiled=True,...  5.06 us
  transfers between devices with their start and end apart: 11, of which 6 were waited for; matrix products, arithmetic and copies ran while one was open for 8% of the time, Pallas kernels for 17%

profile of v7, /device:TPU:1, one launch (start us, length us, event | category | flops | bytes accessed | tf_op | source)
XLA Modules:
  0.0 166.0 jit_solution(13445802589921022389)
XLA Ops:
  7.2 0.7 all-gather.5.cloned.1.call-update
  7.9 2.2 %shard_map.76 = (bf16[320,768]{1,0:T(8,128)(2,1)}, s32[2,128]{1,0:T(2,128)}, f32[2,128]{1,0:T(2,128)}) custom-call(s32[2,128]{1,0:T(2,128)} %bitcast.49, f32[2,128]{1,0:T(2,128)} %bitcast.50, bf16[128,768]{1,0:T(8,128)(2,1)} %upstream_ref.1), custom_call_target="tpu_custom_call" | custom-call | flops 62914560 | bytes 688128 | tf_op jit(solution)/shard_map/pallas_call | solution.py:57
  10.1 11.9 %all-to-all-start = ((bf16[8,40,768]{2,1,0:T(8,128)(2,1)}), bf16[8,40,768]{2,1,0:T(8,128)(2,1)S(1)}, u32[]{:S(2)}, u32[]{:S(2)}) async-start(bf16[8,40,768]{2,1,0:T(8,128)(2,1)} %bitcast.44), calls=%async_computation | async-start | bytes 983040 | tf_op jit(solution)/shard_map/all_to_all | solution.py:221
  22.9 2.4 %constant_dynamic-slice_fusion = (bf16[1,288,512]{2,0,1:T(2,128)(2,1)S(1)}, bf16[1,288,512]{2,0,1:T(2,128)(2,1)S(1)}, bf16[1,288,512]{2,0,1:T(2,128)(2,1)S(1)}, bf16[1,288,512]{2,0,1:T(2,128)(2,1)S(1)}) fusion(bf16[4,288,512]{2,0,1:T(4,128)(2,1)S(1)} %bitcast.34, s32[]{:T(128)S(6)} %select_n.25, s32[]{:T(128)S(6)} %select_n.24, s32[]{:T(128)S(6)} %select_n.23, ...), kind=kLoop, calls=%fused_computation.13 | loop fusion | bytes 2359312 | tf_op jit(solution)/shard_map/jit(dynamic_index_in_dim)/dynamic_slice | solution.py:233
  25.6 1.5 copy.26
  27.1 5.1 %all-to-all-done = bf16[8,40,768]{2,1,0:T(8,128)(2,1)S(1)} async-done(((bf16[8,40,768]{2,1,0:T(8,128)(2,1)}), bf16[8,40,768]{2,1,0:T(8,128)(2,1)S(1)}, u32[]{:S(2)}, u32[]{:S(2)}) %all-to-all-start) | async-done | bytes 491552 | tf_op jit(solution)/shard_map/all_to_all | solution.py:221
  32.3 16.6 %all-gather.1 = bf16[1152,384]{1,0:T(8,128)(2,1)S(1)} all-gather(bf16[288,384]{1,0:T(8,128)(2,1)S(1)} %get-tuple-element.19), channel_id=3, replica_groups=mesh['dp'=4,'ctx'=32,'tp'=4] {'tp'}, dimensions={0}, use_global_device_ids=true | all-gather | bytes 1105920 | tf_op jit(solution)/shard_map/all_gather | solution.py:243
  48.9 11.8 %collective-permute-start = (bf16[4,288,384]{2,1,0:T(8,128)(2,1)S(1)}, bf16[4,288,384]{2,1,0:T(8,128)(2,1)S(1)}, u32[]{:S(2)}, u32[]{:S(2)}) collective-permute-start(bf16[4,288,384]{2,1,0:T(8,128)(2,1)S(1)} %bitcast.35), channel_id=1, source_target_pairs={{0,8},{4,12},{8,0},{12,4},{16,24},{20,28},{24,16},{28,20},{32,40},... | collective-permute-start | bytes 2654216 | tf_op jit(solution)/shard_map/ppermute | solution.py:227
  60.7 17.1 %all-gather = bf16[1152,384]{1,0:T(8,128)(2,1)} all-gather(bf16[288,384]{1,0:T(8,128)(2,1)S(1)} %get-tuple-element.40), channel_id=2, replica_groups=mesh['dp'=4,'ctx'=32,'tp'=4] {'tp'}, dimensions={0}, use_global_device_ids=true | all-gather | bytes 1105920 | tf_op jit(solution)/shard_map/all_gather | solution.py:243
  77.8 6.6 %collective-permute-start.4 = (bf16[4,288,384]{2,1,0:T(8,128)(2,1)S(1)}, bf16[4,288,384]{2,1,0:T(8,128)(2,1)S(1)}, u32[]{:S(2)}, u32[]{:S(2)}) collective-permute-start(bf16[4,288,384]{2,1,0:T(8,128)(2,1)S(1)} %collective-permute-done.p2), channel_id=1, source_target_pairs={{0,4},{4,0},{8,12},{12,8},{16,20},{20,16},{24,28},{28,24},{32,36},... | collective-permute-start | bytes 2654216 | tf_op jit(solution)/shard_map/ppermute | solution.py:227
  84.4 1.9 %collective-permute-start.3 = (bf16[4,288,384]{2,1,0:T(8,128)(2,1)S(1)}, bf16[4,288,384]{2,1,0:T(8,128)(2,1)S(1)}, u32[]{:S(2)}, u32[]{:S(2)}) collective-permute-start(bf16[4,288,384]{2,1,0:T(8,128)(2,1)S(1)} %bitcast.36), channel_id=1, source_target_pairs={{0,4},{4,0},{8,12},{12,8},{16,20},{20,16},{24,28},{28,24},{32,36},... | collective-permute-start | bytes 2654216 | tf_op jit(solution)/shard_map/ppermute | solution.py:227
  86.3 2.2 %collective-permute-start.2 = (bf16[4,288,384]{2,1,0:T(8,128)(2,1)}, bf16[4,288,384]{2,1,0:T(8,128)(2,1)}, u32[]{:S(2)}, u32[]{:S(2)}) collective-permute-start(bf16[4,288,384]{2,1,0:T(8,128)(2,1)} %bitcast.4.n0.p0), channel_id=1, source_target_pairs={{0,8},{4,12},{8,0},{12,4},{16,24},{20,28},{24,16},{28,20},{32,40},... | collective-permute-start | bytes 2654216 | tf_op jit(solution)/shard_map/ppermute | solution.py:227
  88.7 0.8 copy-done.3
  89.5 0.9 copy-done.4
  90.4 5.8 %shard_map.77 = bf16[4,512,384]{2,1,0:T(8,128)(2,1)} custom-call(bf16[4,288,384]{2,1,0:T(8,128)(2,1)} %bitcast.37, bf16[4,288,384]{2,1,0:T(8,128)(2,1)} %copy-done.4, bf16[4,288,384]{2,1,0:T(8,128)(2,1)} %copy-done.2, bf16[4,288,384]{2,1,0:T(8,128)(2,1)} %copy-done.3, bf16[512,1152]{1,0:T(8,128)(2,1)} %bitcast.41), custom_call_target="tpu_custom_call" | custom-call | flops 1048576 | bytes 1048576 | tf_op jit(solution)/shard_map/pallas_call | solution.py:259
  96.3 2.7 %collective-permute-start.1 = (bf16[4,288,384]{2,1,0:T(8,128)(2,1)}, bf16[4,288,384]{2,1,0:T(8,128)(2,1)S(1)}, u32[]{:S(2)}, u32[]{:S(2)}) collective-permute-start(bf16[4,288,384]{2,1,0:T(8,128)(2,1)} %bitcast.4.n0.p0), channel_id=1, source_target_pairs={{0,4},{4,0},{8,12},{12,8},{16,20},{20,16},{24,28},{28,24},{32,36},... | collective-permute-start | bytes 2654216 | tf_op jit(solution)/shard_map/ppermute | solution.py:227
  99.0 6.6 %shard_map.78 = (f32[864,512]{1,0:T(8,128)}, bf16[4,288,512]{2,1,0:T(8,128)(2,1)}, f32[4,8,288]{2,1,0:T(8,128)}) custom-call(s32[1]{0:T(128)} %bitcast.place_ref, bf16[4,288,384]{2,1,0:T(8,128)(2,1)} %bitcast.38, bf16[4,288,384]{2,1,0:T(8,128)(2,1)} %copy-done.4, bf16[4,288,384]{2,1,0:T(8,128)(2,1)} %copy-done.2, bf16[4,288,384]{2,1,0:T(8,128)(2,1)} %copy-done.3, ...), custom_call_target="tpu_custom_call" | custom-call | flops 1048576 | bytes 1048576 | tf_op jit(solution)/shard_map/pallas_call | solution.py:259
  105.6 3.6 %collective-permute-done.2.p2 = bf16[4,288,384]{2,1,0:T(8,128)(2,1)} collective-permute-done((bf16[4,288,384]{2,1,0:T(8,128)(2,1)}, bf16[4,288,384]{2,1,0:T(8,128)(2,1)}, u32[]{:S(2)}, u32[]{:S(2)}) %collective-permute-start.2) | collective-permute-done | bytes 884768 | tf_op jit(solution)/shard_map/ppermute | solution.py:227
  109.2 3.4 %collective-permute-start.5 = (bf16[4,288,384]{2,1,0:T(8,128)(2,1)}, bf16[4,288,384]{2,1,0:T(8,128)(2,1)S(1)}, u32[]{:S(2)}, u32[]{:S(2)}) collective-permute-start(bf16[4,288,384]{2,1,0:T(8,128)(2,1)} %collective-permute-done.2.p2), channel_id=1, source_target_pairs={{0,4},{4,0},{8,12},{12,8},{16,20},{20,16},{24,28},{28,24},{32,36},... | collective-permute-start | bytes 2654216 | tf_op jit(solution)/shard_map/ppermute | solution.py:227
  112.7 2.0 %collective-permute-done.5.p3 = bf16[4,288,384]{2,1,0:T(8,128)(2,1)S(1)} collective-permute-done((bf16[4,288,384]{2,1,0:T(8,128)(2,1)}, bf16[4,288,384]{2,1,0:T(8,128)(2,1)S(1)}, u32[]{:S(2)}, u32[]{:S(2)}) %collective-permute-start.5) | collective-permute-done | bytes 884768 | tf_op jit(solution)/shard_map/ppermute | solution.py:227
  114.7 0.9 copy-done.7
  115.7 5.9 %shard_map.79 = bf16[4,512,384]{2,1,0:T(8,128)(2,1)} custom-call(bf16[4,288,384]{2,1,0:T(8,128)(2,1)} %bitcast.4.n0.p0, bf16[4,288,384]{2,1,0:T(8,128)(2,1)} %copy-done.6, bf16[4,288,384]{2,1,0:T(8,128)(2,1)} %collective-permute-done.2.p2, bf16[4,288,384]{2,1,0:T(8,128)(2,1)} %copy-done.7, bf16[512,1152]{1,0:T(8,128)(2,1)} %bitcast.42), custom_call_target="tpu_custom_call" | custom-call | flops 17999998976 | bytes 1048576 | tf_op jit(solution)/shard_map/pallas_call | solution.py:259
  121.6 0.6 copy-done.9
  122.3 7.4 %shard_map.80 = (bf16[4,288,512]{2,1,0:T(8,128)(2,1)}, f32[4,8,288]{2,1,0:T(8,128)}) custom-call(s32[1]{0:T(128)} %bitcast.place_ref, bf16[4,288,384]{2,1,0:T(8,128)(2,1)} %copy-done.6, bf16[4,288,384]{2,1,0:T(8,128)(2,1)} %collective-permute-done.2.p2, bf16[4,288,384]{2,1,0:T(8,128)(2,1)} %copy-done.7, ...), custom_call_target="tpu_custom_call", output_to_operand_aliasing={{0}: (8, {})} | custom-call | flops 1048576 | bytes 1048576 | tf_op jit(solution)/shard_map/pallas_call | solution.py:259
  129.7 0.8 slice_reduce_fusion
  131.3 8.8 %all-to-all-start.1 = ((f32[128,1,36]{2,1,0:T(1,128)}), f32[128,1,36]{2,1,0:T(1,128)S(1)}, u32[]{:S(2)}, u32[]{:S(2)}) async-start(f32[128,1,36]{2,1,0:T(1,128)} %bitcast.17), calls=%async_computation.3 | async-start | bytes 131072 | tf_op jit(solution)/shard_map/all_to_all | solution.py:326
  140.1 2.2 %copy.27 = bf16[4,288,512]{2,0,1:T(4,128)(2,1)S(1)} copy(bf16[4,288,512]{2,1,0:T(8,128)(2,1)} %get-tuple-element.29) | data formatting | bytes 2359296 | tf_op jit(solution)/shard_map/pallas_call | solution.py:259
  142.6 1.1 reshape.56
  143.7 7.8 %all-to-all-done.1 = f32[128,1,36]{2,1,0:T(1,128)S(1)} async-done(((f32[128,1,36]{2,1,0:T(1,128)}), f32[128,1,36]{2,1,0:T(1,128)S(1)}, u32[]{:S(2)}, u32[]{:S(2)}) %all-to-all-start.1) | async-done | bytes 18464 | tf_op jit(solution)/shard_map/all_to_all | solution.py:326
  151.6 1.9 %gather_fusion = f32[256]{0:T(256)S(1)} fusion(f32[288]{0:T(512)S(1)} %reshape.58, s32[1024]{0:T(1024)S(1)} %pad_clamp_fusion), kind=kCustom, calls=%fused_computation | custom fusion | bytes 3072 | tf_op jit(solution)/shard_map/jit(_take)/gather | solution.py:332
  154.2 3.2 %reduce-scatter.5.cloned.1.call-done = bf16[1,512,384]{2,1,0:T(8,128)(2,1)} async-done(((bf16[4,512,384]{2,1,0:T(8,128)(2,1)}), bf16[1,512,384]{2,1,0:T(8,128)(2,1)}) %reduce-scatter.5.cloned.1.call-update) | async-done | bytes 393232 | tf_op jit(solution)/shard_map/reduce_scatter | solution.py:280
  157.4 2.1 %shard_map.81 = bf16[512,768]{1,0:T(8,128)(2,1)} custom-call(bf16[512,384]{1,0:T(8,128)(2,1)} %bitcast.45, bf16[512,384]{1,0:T(8,128)(2,1)} %bitcast.46), custom_call_target="tpu_custom_call" | custom-call | tf_op jit(solution)/shard_map/pallas_call | solution.py:312
  (45 shorter events, 3.2 us)
Async XLA Ops:
  7.2 14.8 %copy-start.5 = (bf16[1152,512]{1,0:T(8,128)(2,1)S(1)}, bf16[1152,512]{1,0:T(8,128)(2,1)}, u32[]{:S(2)}) copy-start(bf16[1152,512]{1,0:T(8,128)(2,1)} %param.8) | copy-start | bytes 3538948
  7.2 91.8 %all-gather.5.cloned.1.call-start = ((), (), s32[]{:S(2)}) async-start(), calls=%async_computation.6 | async-start | bytes 3932160 | tf_op jit(solution)/shard_map/all_gather | solution.py:239
  10.1 22.1 %all-to-all-start = ((bf16[8,40,768]{2,1,0:T(8,128)(2,1)}), bf16[8,40,768]{2,1,0:T(8,128)(2,1)S(1)}, u32[]{:S(2)}, u32[]{:S(2)}) async-start(bf16[8,40,768]{2,1,0:T(8,128)(2,1)} %bitcast.44), calls=%async_computation | async-start | bytes 983040 | tf_op jit(solution)/shard_map/all_to_all | solution.py:221
  21.9 132.2 %reduce-scatter.3.cloned.1.call-start = ((), (), s32[]{:S(2)}) async-start(), calls=%async_computation.4 | async-start | bytes 1966080 | tf_op jit(solution)/shard_map/reduce_scatter | solution.py:280
  25.6 1.5 copy-start
  48.9 39.8 %copy-start.1 = (bf16[1152,384]{1,0:T(8,128)(2,1)}, bf16[1152,384]{1,0:T(8,128)(2,1)S(1)}, u32[]{:S(2)}) copy-start(bf16[1152,384]{1,0:T(8,128)(2,1)S(1)} %all-gather.1) | copy-start | bytes 2654212
  48.9 28.9 %collective-permute-start = (bf16[4,288,384]{2,1,0:T(8,128)(2,1)S(1)}, bf16[4,288,384]{2,1,0:T(8,128)(2,1)S(1)}, u32[]{:S(2)}, u32[]{:S(2)}) collective-permute-start(bf16[4,288,384]{2,1,0:T(8,128)(2,1)S(1)} %bitcast.35), channel_id=1, source_target_pairs={{0,8},{4,12},{8,0},{12,4},{16,24},{20,28},{24,16},{28,20},{32,40},... | collective-permute-start | bytes 2654216 | tf_op jit(solution)/shard_map/ppermute | solution.py:227
  77.8 10.9 %copy-start.2 = (bf16[4,288,384]{2,1,0:T(8,128)(2,1)}, bf16[4,288,384]{2,1,0:T(8,128)(2,1)S(1)}, u32[]{:S(2)}) copy-start(bf16[4,288,384]{2,1,0:T(8,128)(2,1)S(1)} %collective-permute-done.p2) | copy-start | bytes 2654212
  77.8 10.7 %collective-permute-start.4 = (bf16[4,288,384]{2,1,0:T(8,128)(2,1)S(1)}, bf16[4,288,384]{2,1,0:T(8,128)(2,1)S(1)}, u32[]{:S(2)}, u32[]{:S(2)}) collective-permute-start(bf16[4,288,384]{2,1,0:T(8,128)(2,1)S(1)} %collective-permute-done.p2), channel_id=1, source_target_pairs={{0,4},{4,0},{8,12},{12,8},{16,20},{20,16},{24,28},{28,24},{32,36},... | collective-permute-start | bytes 2654216 | tf_op jit(solution)/shard_map/ppermute | solution.py:227
  84.4 4.3 %collective-permute-start.3 = (bf16[4,288,384]{2,1,0:T(8,128)(2,1)S(1)}, bf16[4,288,384]{2,1,0:T(8,128)(2,1)S(1)}, u32[]{:S(2)}, u32[]{:S(2)}) collective-permute-start(bf16[4,288,384]{2,1,0:T(8,128)(2,1)S(1)} %bitcast.36), channel_id=1, source_target_pairs={{0,4},{4,0},{8,12},{12,8},{16,20},{20,16},{24,28},{28,24},{32,36},... | collective-permute-start | bytes 2654216 | tf_op jit(solution)/shard_map/ppermute | solution.py:227
  86.3 22.9 %collective-permute-start.2 = (bf16[4,288,384]{2,1,0:T(8,128)(2,1)}, bf16[4,288,384]{2,1,0:T(8,128)(2,1)}, u32[]{:S(2)}, u32[]{:S(2)}) collective-permute-start(bf16[4,288,384]{2,1,0:T(8,128)(2,1)} %bitcast.4.n0.p0), channel_id=1, source_target_pairs={{0,8},{4,12},{8,0},{12,4},{16,24},{20,28},{24,16},{28,20},{32,40},... | collective-permute-start | bytes 2654216 | tf_op jit(solution)/shard_map/ppermute | solution.py:227
  88.5 0.9 copy-start.3
  89.5 0.9 copy-start.4
  96.2 61.1 %reduce-scatter.5.cloned.1.call-start = ((), (), s32[]{:S(2)}) async-start(), calls=%async_computation.5 | async-start | bytes 1966080 | tf_op jit(solution)/shard_map/reduce_scatter | solution.py:280
  96.3 16.4 %collective-permute-start.1 = (bf16[4,288,384]{2,1,0:T(8,128)(2,1)}, bf16[4,288,384]{2,1,0:T(8,128)(2,1)S(1)}, u32[]{:S(2)}, u32[]{:S(2)}) collective-permute-start(bf16[4,288,384]{2,1,0:T(8,128)(2,1)} %bitcast.4.n0.p0), channel_id=1, source_target_pairs={{0,4},{4,0},{8,12},{12,8},{16,20},{20,16},{24,28},{28,24},{32,36},... | collective-permute-start | bytes 2654216 | tf_op jit(solution)/shard_map/ppermute | solution.py:227
  109.2 5.5 %collective-permute-start.5 = (bf16[4,288,384]{2,1,0:T(8,128)(2,1)}, bf16[4,288,384]{2,1,0:T(8,128)(2,1)S(1)}, u32[]{:S(2)}, u32[]{:S(2)}) collective-permute-start(bf16[4,288,384]{2,1,0:T(8,128)(2,1)} %collective-permute-done.2.p2), channel_id=1, source_target_pairs={{0,4},{4,0},{8,12},{12,8},{16,20},{20,16},{24,28},{28,24},{32,36},... | collective-permute-start | bytes 2654216 | tf_op jit(solution)/shard_map/ppermute | solution.py:227
  112.7 2.1 %copy-start.6 = (bf16[4,288,384]{2,1,0:T(8,128)(2,1)}, bf16[4,288,384]{2,1,0:T(8,128)(2,1)S(1)}, u32[]{:S(2)}) copy-start(bf16[4,288,384]{2,1,0:T(8,128)(2,1)S(1)} %collective-permute-done.1.p1) | copy-start | bytes 2654212
  114.7 0.9 copy-start.7
  121.6 0.7 copy-start.9
  131.3 20.3 %all-to-all-start.1 = ((f32[128,1,36]{2,1,0:T(1,128)}), f32[128,1,36]{2,1,0:T(1,128)S(1)}, u32[]{:S(2)}, u32[]{:S(2)}) async-start(f32[128,1,36]{2,1,0:T(1,128)} %bitcast.17), calls=%async_computation.3 | async-start | bytes 131072 | tf_op jit(solution)/shard_map/all_to_all | solution.py:326
  142.6 11.0 %copy-start.8 = (f32[2,128]{1,0:T(2,128)S(1)}, f32[2,128]{1,0:T(2,128)}, u32[]{:S(2)}) copy-start(f32[2,128]{1,0:T(2,128)} %get-tuple-element.30) | copy-start | bytes 3076
Sparse Core Ops, SparseCore 0:
  10.1 50.3 all-gather.4
  96.4 27.3 reduce-scatter.2
  126.6 30.7 reduce-scatter.4

commit v8 on v7

--- a/solution.py
+++ b/solution.py
@@ -10,7 +10,7 @@
 EXPERTS = 8
 TOP = 2
 QUADS = 4
-VMEM_LIMIT = 56 * 1024 * 1024
+VMEM_LIMIT = 48 * 1024 * 1024
 CHUNKS = 2
 WEIGH = (1 << 20, 1 << 20, 18 * 10**9)
 
@@ -194,10 +194,18 @@
     wait(stores)
 
 
-def join_kernel(a_ref, b_ref, out_ref):
-    width = a_ref.shape[1]
-    out_ref[:, :width] = a_ref[...]
-    out_ref[:, width:] = b_ref[...]
+def join_kernel(a_ref, b_ref, out_ref, whole, sems):
+    copy = Copies(sems)
+    columns, parts = spans(a_ref.shape[1], CHUNKS), spans(a_ref.shape[0] // 2, 2)
+    loads = [
+        [copy(ref.at[at, :], whole.at[at, c]) for ref, c in zip((a_ref, b_ref), columns)]
+        for at in parts
+    ]
+    stores = []
+    for made, at in zip(loads, parts):
+        wait(made)
+        stores.append(copy(whole.at[at, :], out_ref.at[at, :]))
+    wait(stores)
 
 
 def after(x, *others):
@@ -309,11 +317,10 @@
         (after(place, product), *lasts, weight, before, hidden, early_partial, early_grad),
         {8: 0},
     )
-    down_grad = pl.pallas_call(
-        join_kernel,
-        out_shape=jax.ShapeDtypeStruct((units, cols), jnp.bfloat16),
-        compiler_params=pltpu.CompilerParams(vmem_limit_bytes=VMEM_LIMIT),
-    )(*grads)
+    down_grad = call(
+        join_kernel, jax.ShapeDtypeStruct((units, cols), jnp.bfloat16), held, [space(units, cols)],
+        6, 1 << 20, [held] * CHUNKS, grads,
+    )
 
     def canonical(x):
         x = x.reshape(QUADS, EXPERTS, capacity, -1).transpose(1, 0, 2, 3)

time: 167 us -> 169 us (1.012)
  local copies, waits for them, and re-layouts: 15.5 us -> 24.3 us
  Pallas kernels: 30 us -> 23.8 us
  waiting for transfers between devices: 22.6 us -> 20.2 us
  starting transfers between devices: 49.4 us -> 51.2 us
    unnamed x23 -> x39, local copies, waits for them, and re-layouts: 3.39 us -> 14 us
    pallas_call x4 -> x5, Pallas kernels: 25.8 us -> 22.6 us  [call(): pl.pallas_call(kernel, out_shape=outputs, in_specs=specs, out_specs=out_s...]
    ppermute x6, waiting for transfers between devices: 5.83 us -> 3.27 us  [swap(): return lax.ppermute(x, 'ctx', [(c, c ^ bit) for c in range(context_count)])]
    pallas_call x1 -> x0, Pallas kernels: 2.06 us -> none  [local(): pl.pallas_call(join_kernel, out_shape=jax.ShapeDtypeStruct((units, cols),...]
  transfers between devices with their start and end apart: 11 -> 11, of which waited for: 6 -> 5; matrix products, arithmetic and copies ran while one was open for 8% -> 7% of each run, Pallas kernels for 17% -> 14%
where the time goes in v8:
time: 169 us; the launch traced here: 168 us
  starting transfers between devices  51.2 us (30%)
  blocking collectives  33.4 us (20%)
  local copies, waits for them, and re-layouts  24.3 us (14%)
  Pallas kernels  23.8 us (14%)
  waiting for transfers between devices  20.2 us (12%)
  between operations  14.1 us (8%)
    all_gather x2, blocking collectives, local(): gathered = [lax.all_gather(x, 'tp', axis=0, tiled=False) for x in sent]  33.4 us
    ppermute x6, starting transfers between devices, swap(): return lax.ppermute(x, 'ctx', [(c, c ^ bit) for c in range(context_count)])  28.9 us
    pallas_call x5, Pallas kernels, call(): pl.pallas_call(kernel, out_shape=outputs, in_specs=specs, out_specs=out_s...  22.6 us
    unnamed x39, local copies, waits for them, and re-layouts  14 us
    all_to_all x1, starting transfers between devices, local(): lax.all_to_all(outgoing, 'ctx', split_axis=0, concat_axis=0, tiled=True,...  11.9 us
    all_to_all x1, starting transfers between devices, local(): lax.all_to_all(outgoing_sums.reshape(context_count * tensor_count, capaci...  10.4 us
    all_to_all x1, waiting for transfers between devices, local(): lax.all_to_all(outgoing_sums.reshape(context_count * tensor_count, capaci...  8.66 us
    all_to_all x1, waiting for transfers between devices, local(): lax.all_to_all(outgoing, 'ctx', split_axis=0, concat_axis=0, tiled=True,...  5.64 us
  transfers between devices with their start and end apart: 11, of which 5 were waited for; matrix products, arithmetic and copies ran while one was open for 7% of the time, Pallas kernels for 14%

profile of v8, /device:TPU:1, one launch (start us, length us, event | category | flops | bytes accessed | tf_op | source)
XLA Modules:
  0.0 168.4 jit_solution(13925922597800887747)
XLA Ops:
  10.2 1.2 shard_map.76
  11.4 11.9 %all-to-all-start = ((bf16[8,40,768]{2,1,0:T(8,128)(2,1)}), bf16[8,40,768]{2,1,0:T(8,128)(2,1)}, u32[]{:S(2)}, u32[]{:S(2)}) async-start(bf16[8,40,768]{2,1,0:T(8,128)(2,1)} %bitcast.3), calls=%async_computation | async-start | bytes 983040 | tf_op jit(solution)/shard_map/all_to_all | solution.py:229
  24.2 2.4 %constant_dynamic-slice_fusion = (bf16[1,288,512]{2,0,1:T(2,128)(2,1)S(1)}, bf16[1,288,512]{2,0,1:T(2,128)(2,1)S(1)}, bf16[1,288,512]{2,0,1:T(2,128)(2,1)S(1)}, bf16[1,288,512]{2,0,1:T(2,128)(2,1)S(1)}) fusion(bf16[4,288,512]{2,0,1:T(4,128)(2,1)S(1)} %bitcast.44, s32[]{:T(128)S(6)} %select_n.25, s32[]{:T(128)S(6)} %select_n.24, s32[]{:T(128)S(6)} %select_n.23, ...), kind=kLoop, calls=%fused_computation.13 | loop fusion | bytes 2359312 | tf_op jit(solution)/shard_map/jit(dynamic_index_in_dim)/dynamic_slice | solution.py:241
  27.9 5.6 %all-to-all-done = bf16[8,40,768]{2,1,0:T(8,128)(2,1)} async-done(((bf16[8,40,768]{2,1,0:T(8,128)(2,1)}), bf16[8,40,768]{2,1,0:T(8,128)(2,1)}, u32[]{:S(2)}, u32[]{:S(2)}) %all-to-all-start) | async-done | bytes 491552 | tf_op jit(solution)/shard_map/all_to_all | solution.py:229
  33.5 1.1 reshape.51
  34.7 16.2 %all-gather.1 = bf16[1152,384]{1,0:T(8,128)(2,1)S(1)} all-gather(bf16[288,384]{1,0:T(8,128)(2,1)S(1)} %get-tuple-element.19), channel_id=3, replica_groups=mesh['dp'=4,'ctx'=32,'tp'=4] {'tp'}, dimensions={0}, use_global_device_ids=true | all-gather | bytes 1105920 | tf_op jit(solution)/shard_map/all_gather | solution.py:251
  50.9 12.2 %collective-permute-start = (bf16[4,288,384]{2,1,0:T(8,128)(2,1)S(1)}, bf16[4,288,384]{2,1,0:T(8,128)(2,1)S(1)}, u32[]{:S(2)}, u32[]{:S(2)}) collective-permute-start(bf16[4,288,384]{2,1,0:T(8,128)(2,1)S(1)} %bitcast.32), channel_id=1, source_target_pairs={{0,8},{4,12},{8,0},{12,4},{16,24},{20,28},{24,16},{28,20},{32,40},... | collective-permute-start | bytes 2654216 | tf_op jit(solution)/shard_map/ppermute | solution.py:235
  63.1 17.2 %all-gather = bf16[1152,384]{1,0:T(8,128)(2,1)} all-gather(bf16[288,384]{1,0:T(8,128)(2,1)S(1)} %get-tuple-element.40), channel_id=2, replica_groups=mesh['dp'=4,'ctx'=32,'tp'=4] {'tp'}, dimensions={0}, use_global_device_ids=true | all-gather | bytes 1105920 | tf_op jit(solution)/shard_map/all_gather | solution.py:251
  80.3 6.1 %collective-permute-start.4 = (bf16[4,288,384]{2,1,0:T(8,128)(2,1)S(1)}, bf16[4,288,384]{2,1,0:T(8,128)(2,1)S(1)}, u32[]{:S(2)}, u32[]{:S(2)}) collective-permute-start(bf16[4,288,384]{2,1,0:T(8,128)(2,1)S(1)} %collective-permute-done.p2), channel_id=1, source_target_pairs={{0,4},{4,0},{8,12},{12,8},{16,20},{20,16},{24,28},{28,24},{32,36},... | collective-permute-start | bytes 2654216 | tf_op jit(solution)/shard_map/ppermute | solution.py:235
  86.5 1.9 %collective-permute-start.3 = (bf16[4,288,384]{2,1,0:T(8,128)(2,1)S(1)}, bf16[4,288,384]{2,1,0:T(8,128)(2,1)S(1)}, u32[]{:S(2)}, u32[]{:S(2)}) collective-permute-start(bf16[4,288,384]{2,1,0:T(8,128)(2,1)S(1)} %bitcast.33), channel_id=1, source_target_pairs={{0,4},{4,0},{8,12},{12,8},{16,20},{20,16},{24,28},{28,24},{32,36},... | collective-permute-start | bytes 2654216 | tf_op jit(solution)/shard_map/ppermute | solution.py:235
  88.4 2.5 %collective-permute-start.2 = (bf16[4,288,384]{2,1,0:T(8,128)(2,1)}, bf16[4,288,384]{2,1,0:T(8,128)(2,1)}, u32[]{:S(2)}, u32[]{:S(2)}) collective-permute-start(bf16[4,288,384]{2,1,0:T(8,128)(2,1)} %bitcast.4.n0.p0), channel_id=1, source_target_pairs={{0,8},{4,12},{8,0},{12,4},{16,24},{20,28},{24,16},{28,20},{32,40},... | collective-permute-start | bytes 2654216 | tf_op jit(solution)/shard_map/ppermute | solution.py:235
  90.9 5.0 %shard_map.77 = bf16[4,512,384]{2,1,0:T(8,128)(2,1)} custom-call(bf16[4,288,384]{2,1,0:T(8,128)(2,1)S(1)} %bitcast.34, bf16[4,288,384]{2,1,0:T(8,128)(2,1)S(1)} %collective-permute-done.3.p1, bf16[4,288,384]{2,1,0:T(8,128)(2,1)S(1)} %collective-permute-done.p2, bf16[4,288,384]{2,1,0:T(8,128)(2,1)S(1)} %collective-permute-done.4.p3, ...), custom_call_target="tpu_custom_call" | custom-call | flops 1048576 | bytes 1048576 | tf_op jit(solution)/shard_map/pallas_call | solution.py:267
  97.9 2.7 %collective-permute-start.1 = (bf16[4,288,384]{2,1,0:T(8,128)(2,1)}, bf16[4,288,384]{2,1,0:T(8,128)(2,1)}, u32[]{:S(2)}, u32[]{:S(2)}) collective-permute-start(bf16[4,288,384]{2,1,0:T(8,128)(2,1)} %bitcast.4.n0.p0), channel_id=1, source_target_pairs={{0,4},{4,0},{8,12},{12,8},{16,20},{20,16},{24,28},{28,24},{32,36},... | collective-permute-start | bytes 2654216 | tf_op jit(solution)/shard_map/ppermute | solution.py:235
  100.6 1.2 copy-done.3
  101.7 1.2 copy-done.5
  102.9 1.2 copy-done.7
  104.1 5.4 %shard_map.78 = (f32[864,512]{1,0:T(8,128)}, bf16[4,288,512]{2,1,0:T(8,128)(2,1)S(1)}, f32[4,8,288]{2,1,0:T(8,128)S(1)}) custom-call(s32[1]{0:T(128)} %bitcast.place_ref, bf16[4,288,384]{2,1,0:T(8,128)(2,1)S(1)} %bitcast.35, bf16[4,288,384]{2,1,0:T(8,128)(2,1)S(1)} %copy-done.7, bf16[4,288,384]{2,1,0:T(8,128)(2,1)S(1)} %copy-done.3, ...), custom_call_target="tpu_custom_call" | custom-call | flops 1048576 | bytes 1048576 | tf_op jit(solution)/shard_map/pallas_call | solution.py:267
  110.1 1.2 collective-permute-done.2.p2
  111.3 3.4 %collective-permute-start.5 = (bf16[4,288,384]{2,1,0:T(8,128)(2,1)}, bf16[4,288,384]{2,1,0:T(8,128)(2,1)S(1)}, u32[]{:S(2)}, u32[]{:S(2)}) collective-permute-start(bf16[4,288,384]{2,1,0:T(8,128)(2,1)} %collective-permute-done.2.p2), channel_id=1, source_target_pairs={{0,4},{4,0},{8,12},{12,8},{16,20},{20,16},{24,28},{28,24},{32,36},... | collective-permute-start | bytes 2654216 | tf_op jit(solution)/shard_map/ppermute | solution.py:235
  114.8 2.0 %collective-permute-done.5.p3 = bf16[4,288,384]{2,1,0:T(8,128)(2,1)S(1)} collective-permute-done((bf16[4,288,384]{2,1,0:T(8,128)(2,1)}, bf16[4,288,384]{2,1,0:T(8,128)(2,1)S(1)}, u32[]{:S(2)}, u32[]{:S(2)}) %collective-permute-start.5) | collective-permute-done | bytes 884768 | tf_op jit(solution)/shard_map/ppermute | solution.py:235
  116.8 5.8 %shard_map.79 = bf16[4,512,384]{2,1,0:T(8,128)(2,1)} custom-call(bf16[4,288,384]{2,1,0:T(8,128)(2,1)} %bitcast.4.n0.p0, bf16[4,288,384]{2,1,0:T(8,128)(2,1)} %collective-permute-done.1.p1, bf16[4,288,384]{2,1,0:T(8,128)(2,1)} %collective-permute-done.2.p2, bf16[4,288,384]{2,1,0:T(8,128)(2,1)S(1)} %collective-permute-done.5.p3, bf16[512,1152]{1,0:T(8,128)(2,1)S(1)} %bitcast.37), custom_call_target="tpu_custom_call" | custom-call | flops 17999998976 | bytes 1048576 | tf_op jit(solution)/shard_map/pallas_call | solution.py:267
  123.6 1.3 copy-done.1
  124.8 1.2 copy-done.9
  126.0 5.4 %shard_map.80 = (bf16[4,288,512]{2,1,0:T(8,128)(2,1)S(1)}, f32[4,8,288]{2,1,0:T(8,128)S(1)}) custom-call(s32[1]{0:T(128)} %bitcast.place_ref, bf16[4,288,384]{2,1,0:T(8,128)(2,1)} %collective-permute-done.1.p1, bf16[4,288,384]{2,1,0:T(8,128)(2,1)} %collective-permute-done.2.p2, bf16[4,288,384]{2,1,0:T(8,128)(2,1)S(1)} %copy-done.9, ...), custom_call_target="tpu_custom_call", output_to_operand_aliasing={{0}: (8, {})} | custom-call | flops 1048576 | bytes 1048576 | tf_op jit(solution)/shard_map/pallas_call | solution.py:267
  132.2 10.4 %all-to-all-start.1 = ((f32[128,1,36]{2,1,0:T(1,128)}), f32[128,1,36]{2,1,0:T(1,128)}, u32[]{:S(2)}, u32[]{:S(2)}) async-start(f32[128,1,36]{2,1,0:T(1,128)} %bitcast.17), calls=%async_computation.3 | async-start | bytes 131072 | tf_op jit(solution)/shard_map/all_to_all | solution.py:333
  143.7 1.1 reshape.56
  144.9 8.7 %all-to-all-done.1 = f32[128,1,36]{2,1,0:T(1,128)} async-done(((f32[128,1,36]{2,1,0:T(1,128)}), f32[128,1,36]{2,1,0:T(1,128)}, u32[]{:S(2)}, u32[]{:S(2)}) %all-to-all-start.1) | async-done | bytes 18464 | tf_op jit(solution)/shard_map/all_to_all | solution.py:333
  154.5 1.9 %gather_fusion = f32[256]{0:T(256)S(1)} fusion(f32[288]{0:T(512)S(1)} %reshape.58, s32[1024]{0:T(1024)S(1)} %pad_clamp_fusion), kind=kCustom, calls=%fused_computation | custom fusion | bytes 3072 | tf_op jit(solution)/shard_map/jit(_take)/gather | solution.py:339
  157.0 1.8 %reduce-scatter.5.cloned.1.call-done = bf16[1,512,384]{2,1,0:T(8,128)(2,1)} async-done(((bf16[4,512,384]{2,1,0:T(8,128)(2,1)}), bf16[1,512,384]{2,1,0:T(8,128)(2,1)}) %reduce-scatter.5.cloned.1.call-update) | async-done | bytes 393232 | tf_op jit(solution)/shard_map/reduce_scatter | solution.py:288
  158.9 1.0 copy-done.10
  159.9 1.0 copy-done.11
  160.9 1.0 shard_map.81
  (61 shorter events, 12.1 us)
Async XLA Ops:
  7.2 93.4 %all-gather.5.cloned.1.call-start = ((), (), s32[]{:S(2)}) async-start(), calls=%async_computation.6 | async-start | bytes 3932160 | tf_op jit(solution)/shard_map/all_gather | solution.py:247
  7.9 0.9 copy-start.14
  8.8 0.7 copy-start.15
  9.5 0.7 copy-start.16
  10.2 13.1 %copy-start.17 = (bf16[1152,512]{1,0:T(8,128)(2,1)S(1)}, bf16[1152,512]{1,0:T(8,128)(2,1)}, u32[]{:S(2)}) copy-start(bf16[1152,512]{1,0:T(8,128)(2,1)} %param.8) | copy-start | bytes 3538948
  11.4 22.2 %all-to-all-start = ((bf16[8,40,768]{2,1,0:T(8,128)(2,1)}), bf16[8,40,768]{2,1,0:T(8,128)(2,1)}, u32[]{:S(2)}, u32[]{:S(2)}) async-start(bf16[8,40,768]{2,1,0:T(8,128)(2,1)} %bitcast.3), calls=%async_computation | async-start | bytes 983040 | tf_op jit(solution)/shard_map/all_to_all | solution.py:229
  23.2 133.8 %reduce-scatter.3.cloned.1.call-start = ((), (), s32[]{:S(2)}) async-start(), calls=%async_computation.4 | async-start | bytes 1966080 | tf_op jit(solution)/shard_map/reduce_scatter | solution.py:288
  26.9 1.0 copy-start
  50.9 29.4 %collective-permute-start = (bf16[4,288,384]{2,1,0:T(8,128)(2,1)S(1)}, bf16[4,288,384]{2,1,0:T(8,128)(2,1)S(1)}, u32[]{:S(2)}, u32[]{:S(2)}) collective-permute-start(bf16[4,288,384]{2,1,0:T(8,128)(2,1)S(1)} %bitcast.32), channel_id=1, source_target_pairs={{0,8},{4,12},{8,0},{12,4},{16,24},{20,28},{24,16},{28,20},{32,40},... | collective-permute-start | bytes 2654216 | tf_op jit(solution)/shard_map/ppermute | solution.py:235
  80.3 10.6 %collective-permute-start.4 = (bf16[4,288,384]{2,1,0:T(8,128)(2,1)S(1)}, bf16[4,288,384]{2,1,0:T(8,128)(2,1)S(1)}, u32[]{:S(2)}, u32[]{:S(2)}) collective-permute-start(bf16[4,288,384]{2,1,0:T(8,128)(2,1)S(1)} %collective-permute-done.p2), channel_id=1, source_target_pairs={{0,4},{4,0},{8,12},{12,8},{16,20},{20,16},{24,28},{28,24},{32,36},... | collective-permute-start | bytes 2654216 | tf_op jit(solution)/shard_map/ppermute | solution.py:235
  86.5 4.5 %collective-permute-start.3 = (bf16[4,288,384]{2,1,0:T(8,128)(2,1)S(1)}, bf16[4,288,384]{2,1,0:T(8,128)(2,1)S(1)}, u32[]{:S(2)}, u32[]{:S(2)}) collective-permute-start(bf16[4,288,384]{2,1,0:T(8,128)(2,1)S(1)} %bitcast.33), channel_id=1, source_target_pairs={{0,4},{4,0},{8,12},{12,8},{16,20},{20,16},{24,28},{28,24},{32,36},... | collective-permute-start | bytes 2654216 | tf_op jit(solution)/shard_map/ppermute | solution.py:235
  88.4 22.9 %collective-permute-start.2 = (bf16[4,288,384]{2,1,0:T(8,128)(2,1)}, bf16[4,288,384]{2,1,0:T(8,128)(2,1)}, u32[]{:S(2)}, u32[]{:S(2)}) collective-permute-start(bf16[4,288,384]{2,1,0:T(8,128)(2,1)} %bitcast.4.n0.p0), channel_id=1, source_target_pairs={{0,8},{4,12},{8,0},{12,4},{16,24},{20,28},{24,16},{28,20},{32,40},... | collective-permute-start | bytes 2654216 | tf_op jit(solution)/shard_map/ppermute | solution.py:235
  90.9 5.0 %copy-start.6 = (bf16[4,288,384]{2,1,0:T(8,128)(2,1)}, bf16[4,288,384]{2,1,0:T(8,128)(2,1)S(1)}, u32[]{:S(2)}) copy-start(bf16[4,288,384]{2,1,0:T(8,128)(2,1)S(1)} %collective-permute-done.3.p1) | copy-start | bytes 2654212
  95.9 0.9 copy-start.2
  96.9 0.9 copy-start.4
  97.8 61.1 %reduce-scatter.5.cloned.1.call-start = ((), (), s32[]{:S(2)}) async-start(), calls=%async_computation.5 | async-start | bytes 1966080 | tf_op jit(solution)/shard_map/reduce_scatter | solution.py:288
  97.9 16.9 %collective-permute-start.1 = (bf16[4,288,384]{2,1,0:T(8,128)(2,1)}, bf16[4,288,384]{2,1,0:T(8,128)(2,1)}, u32[]{:S(2)}, u32[]{:S(2)}) collective-permute-start(bf16[4,288,384]{2,1,0:T(8,128)(2,1)} %bitcast.4.n0.p0), channel_id=1, source_target_pairs={{0,4},{4,0},{8,12},{12,8},{16,20},{20,16},{24,28},{28,24},{32,36},... | collective-permute-start | bytes 2654216 | tf_op jit(solution)/shard_map/ppermute | solution.py:235
  100.6 1.2 copy-start.3
  101.7 1.2 copy-start.5
  102.9 1.2 copy-start.7
  109.5 0.6 copy-start.12
  111.3 5.5 %collective-permute-start.5 = (bf16[4,288,384]{2,1,0:T(8,128)(2,1)}, bf16[4,288,384]{2,1,0:T(8,128)(2,1)S(1)}, u32[]{:S(2)}, u32[]{:S(2)}) collective-permute-start(bf16[4,288,384]{2,1,0:T(8,128)(2,1)} %collective-permute-done.2.p2), channel_id=1, source_target_pairs={{0,4},{4,0},{8,12},{12,8},{16,20},{20,16},{24,28},{28,24},{32,36},... | collective-permute-start | bytes 2654216 | tf_op jit(solution)/shard_map/ppermute | solution.py:235
  122.6 0.9 copy-start.8
  123.5 1.3 copy-start.1
  123.5 1.3 copy-start.13
  124.8 1.2 copy-start.9
  132.2 21.4 %all-to-all-start.1 = ((f32[128,1,36]{2,1,0:T(1,128)}), f32[128,1,36]{2,1,0:T(1,128)}, u32[]{:S(2)}, u32[]{:S(2)}) async-start(f32[128,1,36]{2,1,0:T(1,128)} %bitcast.17), calls=%async_computation.3 | async-start | bytes 131072 | tf_op jit(solution)/shard_map/all_to_all | solution.py:333
  158.9 1.0 copy-start.10
  159.9 1.0 copy-start.11
Sparse Core Ops, SparseCore 0:
  10.1 50.3 all-gather.4
  97.9 27.2 reduce-scatter.2
  128.1 30.7 reduce-scatter.4

commit v9 on v8

--- a/solution.py
+++ b/solution.py
@@ -10,7 +10,8 @@
 EXPERTS = 8
 TOP = 2
 QUADS = 4
-VMEM_LIMIT = 48 * 1024 * 1024
+VMEM_LIMIT = 56 * 1024 * 1024
+PRODUCT_LIMIT = 48 * 1024 * 1024
 CHUNKS = 2
 WEIGH = (1 << 20, 1 << 20, 18 * 10**9)
 
@@ -263,7 +264,9 @@
     def space(*shape, dtype=jnp.bfloat16):
         return pltpu.VMEM(shape, dtype)
 
-    def call(kernel, outputs, out_specs, scratch, copies, weigh, specs, inputs, aliases={}):
+    def call(
+        kernel, outputs, out_specs, scratch, copies, weigh, specs, inputs, aliases={}, limit=VMEM_LIMIT
+    ):
         return pl.pallas_call(
             kernel,
             out_shape=outputs,
@@ -271,7 +274,7 @@
             out_specs=out_specs,
             scratch_shapes=scratch + [pltpu.SemaphoreType.DMA((copies,))],
             input_output_aliases=aliases,
-            compiler_params=pltpu.CompilerParams(vmem_limit_bytes=VMEM_LIMIT),
+            compiler_params=pltpu.CompilerParams(vmem_limit_bytes=limit),
             cost_estimate=pl.CostEstimate(
                 flops=weigh, bytes_accessed=1 << 20, transcendentals=0
             ),
@@ -282,6 +285,7 @@
             product_kernel, jax.ShapeDtypeStruct((blocks, units, width), jnp.bfloat16), held,
             [space(total, blocks * width), space(units, total), space(blocks, units, width)],
             1 + blocks * (QUADS + 1), weigh, [held] * 5, (*pieces, hidden_t),
+            limit=PRODUCT_LIMIT,
         )
 
     def settle(product):

time: 169 us -> 167 us (0.988)
  local copies, waits for them, and re-layouts: 24.3 us -> 15.4 us
  Pallas kernels: 23.8 us -> 29 us
  waiting for transfers between devices: 20.2 us -> 24.1 us
    unnamed x39 -> x23, local copies, waits for them, and re-layouts: 14 us -> 3 us
    pallas_call x5, Pallas kernels: 22.6 us -> 26.8 us  [call(): pl.pallas_call(kernel, out_shape=outputs, in_specs=specs, out_specs=out_s...]
    ppermute x6, waiting for transfers between devices: 3.27 us -> 6.56 us  [swap(): return lax.ppermute(x, 'ctx', [(c, c ^ bit) for c in range(context_count)])]
  transfers between devices with their start and end apart: 11 -> 11, of which waited for: 5 -> 6; matrix products, arithmetic and copies ran while one was open for 7% -> 8% of each run, Pallas kernels for 14% -> 16%
where the time goes in v9:
time: 167 us; the launch traced here: 166 us
  starting transfers between devices  49.7 us (30%)
  blocking collectives  33.2 us (20%)
  Pallas kernels  29 us (17%)
  waiting for transfers between devices  24.1 us (14%)
  local copies, waits for them, and re-layouts  15.4 us (9%)
  between operations  14.1 us (8%)
    all_gather x2, blocking collectives, local(): gathered = [lax.all_gather(x, 'tp', axis=0, tiled=False) for x in sent]  33.2 us
    ppermute x6, starting transfers between devices, swap(): return lax.ppermute(x, 'ctx', [(c, c ^ bit) for c in range(context_count)])  28.9 us
    pallas_call x5, Pallas kernels, call(): pl.pallas_call(kernel, out_shape=outputs, in_specs=specs, out_specs=out_s...  26.8 us
    all_to_all x1, starting transfers between devices, local(): lax.all_to_all(outgoing, 'ctx', split_axis=0, concat_axis=0, tiled=True,...  11.9 us
    all_to_all x1, starting transfers between devices, local(): lax.all_to_all(outgoing_sums.reshape(context_count * tensor_count, capaci...  8.79 us
    all_to_all x1, waiting for transfers between devices, local(): lax.all_to_all(outgoing_sums.reshape(context_count * tensor_count, capaci...  7.79 us
    ppermute x6, waiting for transfers between devices, swap(): return lax.ppermute(x, 'ctx', [(c, c ^ bit) for c in range(context_count)])  6.56 us
    all_to_all x1, waiting for transfers between devices, local(): lax.all_to_all(outgoing, 'ctx', split_axis=0, concat_axis=0, tiled=True,...  5.64 us
  transfers between devices with their start and end apart: 11, of which 6 were waited for; matrix products, arithmetic and copies ran while one was open for 8% of the time, Pallas kernels for 16%

profile of v9, /device:TPU:1, one launch (start us, length us, event | category | flops | bytes accessed | tf_op | source)
XLA Modules:
  0.0 166.2 jit_solution(9382928529676313838)
XLA Ops:
  7.2 0.7 all-gather.5.cloned.1.call-update
  7.9 2.2 %shard_map.76 = (bf16[320,768]{1,0:T(8,128)(2,1)}, s32[2,128]{1,0:T(2,128)}, f32[2,128]{1,0:T(2,128)}) custom-call(s32[2,128]{1,0:T(2,128)} %bitcast.48, f32[2,128]{1,0:T(2,128)} %bitcast.49, bf16[128,768]{1,0:T(8,128)(2,1)} %upstream_ref.1), custom_call_target="tpu_custom_call" | custom-call | flops 62914560 | bytes 688128 | tf_op jit(solution)/shard_map/pallas_call | solution.py:58
  10.1 11.9 %all-to-all-start = ((bf16[8,40,768]{2,1,0:T(8,128)(2,1)}), bf16[8,40,768]{2,1,0:T(8,128)(2,1)}, u32[]{:S(2)}, u32[]{:S(2)}) async-start(bf16[8,40,768]{2,1,0:T(8,128)(2,1)} %bitcast.43), calls=%async_computation | async-start | bytes 983040 | tf_op jit(solution)/shard_map/all_to_all | solution.py:230
  22.9 2.4 %constant_dynamic-slice_fusion = (bf16[1,288,512]{2,0,1:T(2,128)(2,1)S(1)}, bf16[1,288,512]{2,0,1:T(2,128)(2,1)S(1)}, bf16[1,288,512]{2,0,1:T(2,128)(2,1)S(1)}, bf16[1,288,512]{2,0,1:T(2,128)(2,1)S(1)}) fusion(bf16[4,288,512]{2,0,1:T(4,128)(2,1)S(1)} %bitcast.40, s32[]{:T(128)S(6)} %select_n.25, s32[]{:T(128)S(6)} %select_n.24, s32[]{:T(128)S(6)} %select_n.23, ...), kind=kLoop, calls=%fused_computation.13 | loop fusion | bytes 2359312 | tf_op jit(solution)/shard_map/jit(dynamic_index_in_dim)/dynamic_slice | solution.py:242
  25.6 0.7 copy.26
  26.6 5.6 %all-to-all-done = bf16[8,40,768]{2,1,0:T(8,128)(2,1)} async-done(((bf16[8,40,768]{2,1,0:T(8,128)(2,1)}), bf16[8,40,768]{2,1,0:T(8,128)(2,1)}, u32[]{:S(2)}, u32[]{:S(2)}) %all-to-all-start) | async-done | bytes 491552 | tf_op jit(solution)/shard_map/all_to_all | solution.py:230
  32.2 1.2 reshape.51
  33.4 16.1 %all-gather.1 = bf16[1152,384]{1,0:T(8,128)(2,1)S(1)} all-gather(bf16[288,384]{1,0:T(8,128)(2,1)S(1)} %get-tuple-element.19), channel_id=3, replica_groups=mesh['dp'=4,'ctx'=32,'tp'=4] {'tp'}, dimensions={0}, use_global_device_ids=true | all-gather | bytes 1105920 | tf_op jit(solution)/shard_map/all_gather | solution.py:252
  49.6 12.3 %collective-permute-start = (bf16[4,288,384]{2,1,0:T(8,128)(2,1)S(1)}, bf16[4,288,384]{2,1,0:T(8,128)(2,1)S(1)}, u32[]{:S(2)}, u32[]{:S(2)}) collective-permute-start(bf16[4,288,384]{2,1,0:T(8,128)(2,1)S(1)} %bitcast.31), channel_id=1, source_target_pairs={{0,8},{4,12},{8,0},{12,4},{16,24},{20,28},{24,16},{28,20},{32,40},... | collective-permute-start | bytes 2654216 | tf_op jit(solution)/shard_map/ppermute | solution.py:236
  61.9 17.1 %all-gather = bf16[1152,384]{1,0:T(8,128)(2,1)} all-gather(bf16[288,384]{1,0:T(8,128)(2,1)S(1)} %get-tuple-element.40), channel_id=2, replica_groups=mesh['dp'=4,'ctx'=32,'tp'=4] {'tp'}, dimensions={0}, use_global_device_ids=true | all-gather | bytes 1105920 | tf_op jit(solution)/shard_map/all_gather | solution.py:252
  79.0 6.5 %collective-permute-start.4 = (bf16[4,288,384]{2,1,0:T(8,128)(2,1)S(1)}, bf16[4,288,384]{2,1,0:T(8,128)(2,1)S(1)}, u32[]{:S(2)}, u32[]{:S(2)}) collective-permute-start(bf16[4,288,384]{2,1,0:T(8,128)(2,1)S(1)} %collective-permute-done.p2), channel_id=1, source_target_pairs={{0,4},{4,0},{8,12},{12,8},{16,20},{20,16},{24,28},{28,24},{32,36},... | collective-permute-start | bytes 2654216 | tf_op jit(solution)/shard_map/ppermute | solution.py:236
  85.5 1.9 %collective-permute-start.3 = (bf16[4,288,384]{2,1,0:T(8,128)(2,1)S(1)}, bf16[4,288,384]{2,1,0:T(8,128)(2,1)S(1)}, u32[]{:S(2)}, u32[]{:S(2)}) collective-permute-start(bf16[4,288,384]{2,1,0:T(8,128)(2,1)S(1)} %bitcast.32), channel_id=1, source_target_pairs={{0,4},{4,0},{8,12},{12,8},{16,20},{20,16},{24,28},{28,24},{32,36},... | collective-permute-start | bytes 2654216 | tf_op jit(solution)/shard_map/ppermute | solution.py:236
  87.5 2.2 %collective-permute-start.2 = (bf16[4,288,384]{2,1,0:T(8,128)(2,1)}, bf16[4,288,384]{2,1,0:T(8,128)(2,1)}, u32[]{:S(2)}, u32[]{:S(2)}) collective-permute-start(bf16[4,288,384]{2,1,0:T(8,128)(2,1)} %bitcast.4.n0.p0), channel_id=1, source_target_pairs={{0,8},{4,12},{8,0},{12,4},{16,24},{20,28},{24,16},{28,20},{32,40},... | collective-permute-start | bytes 2654216 | tf_op jit(solution)/shard_map/ppermute | solution.py:236
  89.8 5.0 %shard_map.77 = bf16[4,512,384]{2,1,0:T(8,128)(2,1)} custom-call(bf16[4,288,384]{2,1,0:T(8,128)(2,1)S(1)} %bitcast.33, bf16[4,288,384]{2,1,0:T(8,128)(2,1)S(1)} %collective-permute-done.3.p1, bf16[4,288,384]{2,1,0:T(8,128)(2,1)S(1)} %collective-permute-done.p2, bf16[4,288,384]{2,1,0:T(8,128)(2,1)S(1)} %collective-permute-done.4.p3, ...), custom_call_target="tpu_custom_call" | custom-call | flops 1048576 | bytes 1048576 | tf_op jit(solution)/shard_map/pallas_call | solution.py:270
  94.8 0.9 copy-done.2
  95.8 1.0 copy-done.3
  96.8 2.5 %collective-permute-start.1 = (bf16[4,288,384]{2,1,0:T(8,128)(2,1)}, bf16[4,288,384]{2,1,0:T(8,128)(2,1)S(1)}, u32[]{:S(2)}, u32[]{:S(2)}) collective-permute-start(bf16[4,288,384]{2,1,0:T(8,128)(2,1)} %bitcast.4.n0.p0), channel_id=1, source_target_pairs={{0,4},{4,0},{8,12},{12,8},{16,20},{20,16},{24,28},{28,24},{32,36},... | collective-permute-start | bytes 2654216 | tf_op jit(solution)/shard_map/ppermute | solution.py:236
  99.4 6.6 %shard_map.78 = (f32[864,512]{1,0:T(8,128)}, bf16[4,288,512]{2,1,0:T(8,128)(2,1)}, f32[4,8,288]{2,1,0:T(8,128)}) custom-call(s32[1]{0:T(128)} %bitcast.place_ref, bf16[4,288,384]{2,1,0:T(8,128)(2,1)} %bitcast.34, bf16[4,288,384]{2,1,0:T(8,128)(2,1)} %copy-done.3, bf16[4,288,384]{2,1,0:T(8,128)(2,1)} %copy-done.1, bf16[4,288,384]{2,1,0:T(8,128)(2,1)} %copy-done.2, ...), custom_call_target="tpu_custom_call" | custom-call | flops 1048576 | bytes 1048576 | tf_op jit(solution)/shard_map/pallas_call | solution.py:270
  106.0 4.4 %collective-permute-done.2.p2 = bf16[4,288,384]{2,1,0:T(8,128)(2,1)} collective-permute-done((bf16[4,288,384]{2,1,0:T(8,128)(2,1)}, bf16[4,288,384]{2,1,0:T(8,128)(2,1)}, u32[]{:S(2)}, u32[]{:S(2)}) %collective-permute-start.2) | collective-permute-done | bytes 884768 | tf_op jit(solution)/shard_map/ppermute | solution.py:236
  110.4 3.4 %collective-permute-start.5 = (bf16[4,288,384]{2,1,0:T(8,128)(2,1)}, bf16[4,288,384]{2,1,0:T(8,128)(2,1)S(1)}, u32[]{:S(2)}, u32[]{:S(2)}) collective-permute-start(bf16[4,288,384]{2,1,0:T(8,128)(2,1)} %collective-permute-done.2.p2), channel_id=1, source_target_pairs={{0,4},{4,0},{8,12},{12,8},{16,20},{20,16},{24,28},{28,24},{32,36},... | collective-permute-start | bytes 2654216 | tf_op jit(solution)/shard_map/ppermute | solution.py:236
  113.8 2.0 %collective-permute-done.5.p3 = bf16[4,288,384]{2,1,0:T(8,128)(2,1)S(1)} collective-permute-done((bf16[4,288,384]{2,1,0:T(8,128)(2,1)}, bf16[4,288,384]{2,1,0:T(8,128)(2,1)S(1)}, u32[]{:S(2)}, u32[]{:S(2)}) %collective-permute-start.5) | collective-permute-done | bytes 884768 | tf_op jit(solution)/shard_map/ppermute | solution.py:236
  115.9 5.8 %shard_map.79 = bf16[4,512,384]{2,1,0:T(8,128)(2,1)} custom-call(bf16[4,288,384]{2,1,0:T(8,128)(2,1)} %bitcast.4.n0.p0, bf16[4,288,384]{2,1,0:T(8,128)(2,1)S(1)} %collective-permute-done.1.p1, bf16[4,288,384]{2,1,0:T(8,128)(2,1)} %collective-permute-done.2.p2, bf16[4,288,384]{2,1,0:T(8,128)(2,1)S(1)} %collective-permute-done.5.p3, bf16[512,1152]{1,0:T(8,128)(2,1)S(1)} %bitcast.36), custom_call_target="tpu_custom_call" | custom-call | flops 17999998976 | bytes 1048576 | tf_op jit(solution)/shard_map/pallas_call | solution.py:270
  121.7 0.6 copy-done.9
  122.3 7.5 %shard_map.80 = (bf16[4,288,512]{2,1,0:T(8,128)(2,1)}, f32[4,8,288]{2,1,0:T(8,128)}) custom-call(s32[1]{0:T(128)} %bitcast.place_ref, bf16[4,288,384]{2,1,0:T(8,128)(2,1)} %copy-done.4, bf16[4,288,384]{2,1,0:T(8,128)(2,1)} %collective-permute-done.2.p2, bf16[4,288,384]{2,1,0:T(8,128)(2,1)} %copy-done.5, ...), custom_call_target="tpu_custom_call", output_to_operand_aliasing={{0}: (8, {})} | custom-call | flops 1048576 | bytes 1048576 | tf_op jit(solution)/shard_map/pallas_call | solution.py:270
  129.8 0.8 slice_reduce_fusion
  131.4 8.8 %all-to-all-start.1 = ((f32[128,1,36]{2,1,0:T(1,128)}), f32[128,1,36]{2,1,0:T(1,128)S(1)}, u32[]{:S(2)}, u32[]{:S(2)}) async-start(f32[128,1,36]{2,1,0:T(1,128)} %bitcast.17), calls=%async_computation.3 | async-start | bytes 131072 | tf_op jit(solution)/shard_map/all_to_all | solution.py:337
  140.2 2.2 %copy.27 = bf16[4,288,512]{2,0,1:T(4,128)(2,1)S(1)} copy(bf16[4,288,512]{2,1,0:T(8,128)(2,1)} %get-tuple-element.29) | data formatting | bytes 2359296 | tf_op jit(solution)/shard_map/pallas_call | solution.py:270
  142.6 1.1 reshape.56
  143.8 7.8 %all-to-all-done.1 = f32[128,1,36]{2,1,0:T(1,128)S(1)} async-done(((f32[128,1,36]{2,1,0:T(1,128)}), f32[128,1,36]{2,1,0:T(1,128)S(1)}, u32[]{:S(2)}, u32[]{:S(2)}) %all-to-all-start.1) | async-done | bytes 18464 | tf_op jit(solution)/shard_map/all_to_all | solution.py:337
  151.7 1.9 %gather_fusion = f32[256]{0:T(256)S(1)} fusion(f32[288]{0:T(512)S(1)} %reshape.58, s32[1024]{0:T(1024)S(1)} %pad_clamp_fusion), kind=kCustom, calls=%fused_computation | custom fusion | bytes 3072 | tf_op jit(solution)/shard_map/jit(_take)/gather | solution.py:343
  154.2 3.4 %reduce-scatter.5.cloned.1.call-done = bf16[1,512,384]{2,1,0:T(8,128)(2,1)} async-done(((bf16[4,512,384]{2,1,0:T(8,128)(2,1)}), bf16[1,512,384]{2,1,0:T(8,128)(2,1)}) %reduce-scatter.5.cloned.1.call-update) | async-done | bytes 393232 | tf_op jit(solution)/shard_map/reduce_scatter | solution.py:292
  157.6 2.0 %shard_map.81 = bf16[512,768]{1,0:T(8,128)(2,1)} custom-call(bf16[512,384]{1,0:T(8,128)(2,1)} %bitcast.44, bf16[512,384]{1,0:T(8,128)(2,1)} %bitcast.45), custom_call_target="tpu_custom_call" | custom-call | flops 1048576 | bytes 1048576 | tf_op jit(solution)/shard_map/pallas_call | solution.py:270
  (45 shorter events, 3.4 us)
Async XLA Ops:
  7.2 14.8 %copy-start.7 = (bf16[1152,512]{1,0:T(8,128)(2,1)S(1)}, bf16[1152,512]{1,0:T(8,128)(2,1)}, u32[]{:S(2)}) copy-start(bf16[1152,512]{1,0:T(8,128)(2,1)} %param.8) | copy-start | bytes 3538948
  7.2 92.2 %all-gather.5.cloned.1.call-start = ((), (), s32[]{:S(2)}) async-start(), calls=%async_computation.6 | async-start | bytes 3932160 | tf_op jit(solution)/shard_map/all_gather | solution.py:248
  10.1 22.2 %all-to-all-start = ((bf16[8,40,768]{2,1,0:T(8,128)(2,1)}), bf16[8,40,768]{2,1,0:T(8,128)(2,1)}, u32[]{:S(2)}, u32[]{:S(2)}) async-start(bf16[8,40,768]{2,1,0:T(8,128)(2,1)} %bitcast.43), calls=%async_computation | async-start | bytes 983040 | tf_op jit(solution)/shard_map/all_to_all | solution.py:230
  21.9 132.3 %reduce-scatter.3.cloned.1.call-start = ((), (), s32[]{:S(2)}) async-start(), calls=%async_computation.4 | async-start | bytes 1966080 | tf_op jit(solution)/shard_map/reduce_scatter | solution.py:292
  25.6 1.0 copy-start.6
  49.6 45.2 %copy-start = (bf16[1152,384]{1,0:T(8,128)(2,1)}, bf16[1152,384]{1,0:T(8,128)(2,1)S(1)}, u32[]{:S(2)}) copy-start(bf16[1152,384]{1,0:T(8,128)(2,1)S(1)} %all-gather.1) | copy-start | bytes 2654212
  49.6 29.4 %collective-permute-start = (bf16[4,288,384]{2,1,0:T(8,128)(2,1)S(1)}, bf16[4,288,384]{2,1,0:T(8,128)(2,1)S(1)}, u32[]{:S(2)}, u32[]{:S(2)}) collective-permute-start(bf16[4,288,384]{2,1,0:T(8,128)(2,1)S(1)} %bitcast.31), channel_id=1, source_target_pairs={{0,8},{4,12},{8,0},{12,4},{16,24},{20,28},{24,16},{28,20},{32,40},... | collective-permute-start | bytes 2654216 | tf_op jit(solution)/shard_map/ppermute | solution.py:236
  79.0 15.8 %copy-start.1 = (bf16[4,288,384]{2,1,0:T(8,128)(2,1)}, bf16[4,288,384]{2,1,0:T(8,128)(2,1)S(1)}, u32[]{:S(2)}) copy-start(bf16[4,288,384]{2,1,0:T(8,128)(2,1)S(1)} %collective-permute-done.p2) | copy-start | bytes 2654212
  79.0 10.7 %collective-permute-start.4 = (bf16[4,288,384]{2,1,0:T(8,128)(2,1)S(1)}, bf16[4,288,384]{2,1,0:T(8,128)(2,1)S(1)}, u32[]{:S(2)}, u32[]{:S(2)}) collective-permute-start(bf16[4,288,384]{2,1,0:T(8,128)(2,1)S(1)} %collective-permute-done.p2), channel_id=1, source_target_pairs={{0,4},{4,0},{8,12},{12,8},{16,20},{20,16},{24,28},{28,24},{32,36},... | collective-permute-start | bytes 2654216 | tf_op jit(solution)/shard_map/ppermute | solution.py:236
  85.5 4.3 %collective-permute-start.3 = (bf16[4,288,384]{2,1,0:T(8,128)(2,1)S(1)}, bf16[4,288,384]{2,1,0:T(8,128)(2,1)S(1)}, u32[]{:S(2)}, u32[]{:S(2)}) collective-permute-start(bf16[4,288,384]{2,1,0:T(8,128)(2,1)S(1)} %bitcast.32), channel_id=1, source_target_pairs={{0,4},{4,0},{8,12},{12,8},{16,20},{20,16},{24,28},{28,24},{32,36},... | collective-permute-start | bytes 2654216 | tf_op jit(solution)/shard_map/ppermute | solution.py:236
  87.5 22.9 %collective-permute-start.2 = (bf16[4,288,384]{2,1,0:T(8,128)(2,1)}, bf16[4,288,384]{2,1,0:T(8,128)(2,1)}, u32[]{:S(2)}, u32[]{:S(2)}) collective-permute-start(bf16[4,288,384]{2,1,0:T(8,128)(2,1)} %bitcast.4.n0.p0), channel_id=1, source_target_pairs={{0,8},{4,12},{8,0},{12,4},{16,24},{20,28},{24,16},{28,20},{32,40},... | collective-permute-start | bytes 2654216 | tf_op jit(solution)/shard_map/ppermute | solution.py:236
  94.8 1.0 copy-start.2
  95.8 1.0 copy-start.3
  96.8 60.9 %reduce-scatter.5.cloned.1.call-start = ((), (), s32[]{:S(2)}) async-start(), calls=%async_computation.5 | async-start | bytes 1966080 | tf_op jit(solution)/shard_map/reduce_scatter | solution.py:292
  96.8 17.0 %collective-permute-start.1 = (bf16[4,288,384]{2,1,0:T(8,128)(2,1)}, bf16[4,288,384]{2,1,0:T(8,128)(2,1)S(1)}, u32[]{:S(2)}, u32[]{:S(2)}) collective-permute-start(bf16[4,288,384]{2,1,0:T(8,128)(2,1)} %bitcast.4.n0.p0), channel_id=1, source_target_pairs={{0,4},{4,0},{8,12},{12,8},{16,20},{20,16},{24,28},{28,24},{32,36},... | collective-permute-start | bytes 2654216 | tf_op jit(solution)/shard_map/ppermute | solution.py:236
  110.4 5.5 %collective-permute-start.5 = (bf16[4,288,384]{2,1,0:T(8,128)(2,1)}, bf16[4,288,384]{2,1,0:T(8,128)(2,1)S(1)}, u32[]{:S(2)}, u32[]{:S(2)}) collective-permute-start(bf16[4,288,384]{2,1,0:T(8,128)(2,1)} %collective-permute-done.2.p2), channel_id=1, source_target_pairs={{0,4},{4,0},{8,12},{12,8},{16,20},{20,16},{24,28},{28,24},{32,36},... | collective-permute-start | bytes 2654216 | tf_op jit(solution)/shard_map/ppermute | solution.py:236
  113.8 7.8 %copy-start.4 = (bf16[4,288,384]{2,1,0:T(8,128)(2,1)}, bf16[4,288,384]{2,1,0:T(8,128)(2,1)S(1)}, u32[]{:S(2)}) copy-start(bf16[4,288,384]{2,1,0:T(8,128)(2,1)S(1)} %collective-permute-done.1.p1) | copy-start | bytes 2654212
  115.9 5.8 %copy-start.5 = (bf16[4,288,384]{2,1,0:T(8,128)(2,1)}, bf16[4,288,384]{2,1,0:T(8,128)(2,1)S(1)}, u32[]{:S(2)}) copy-start(bf16[4,288,384]{2,1,0:T(8,128)(2,1)S(1)} %collective-permute-done.5.p3) | copy-start | bytes 2654212
  121.7 0.7 copy-start.9
  131.4 20.2 %all-to-all-start.1 = ((f32[128,1,36]{2,1,0:T(1,128)}), f32[128,1,36]{2,1,0:T(1,128)S(1)}, u32[]{:S(2)}, u32[]{:S(2)}) async-start(f32[128,1,36]{2,1,0:T(1,128)} %bitcast.17), calls=%async_computation.3 | async-start | bytes 131072 | tf_op jit(solution)/shard_map/all_to_all | solution.py:337
  142.6 11.0 %copy-start.8 = (f32[2,128]{1,0:T(2,128)S(1)}, f32[2,128]{1,0:T(2,128)}, u32[]{:S(2)}) copy-start(f32[2,128]{1,0:T(2,128)} %get-tuple-element.30) | copy-start | bytes 3076
Sparse Core Ops, SparseCore 0:
  10.1 50.3 all-gather.4
  96.9 26.9 reduce-scatter.2
  126.8 30.7 reduce-scatter.4
